TPU v7x, 32 devices: a whole 2x2x4 slice. The times are simulated.
32 devices in a mesh: groups: 2 (over y), tm: 4 (over z), space: 4 (over x, core).
Axes of the slice: x: 2, y: 2, z: 4, core: 2. Of those that a mesh axis runs over, the one named last changes fastest.
Arguments:
- guess: float32 [8, 320, 2048], P('tm', None, ('groups', 'space')), parts along dimension 2, may hold values from -6 to 6
- source_cos: bfloat16 [320, 2048], P(None, ('groups', 'space')), parts along dimension 1, may hold values from -6 to 6
- source_sin: bfloat16 [320, 2048], P(None, ('groups', 'space')), parts along dimension 1, may hold values from -6 to 6
- damping: float32 [320, 2048], P(None, ('groups', 'space')), parts along dimension 1, may hold values from 0.5 to 4
- volume: bfloat16 [320, 320], replicated, may hold values from -0.3125 to 0.3125
- lifts: bfloat16 [6, 320, 80], replicated, may hold values from -0.25 to 0.25
- neighbor: int32 [6, 2048], P(None, ('groups', 'space')), parts along dimension 1, may hold values from 0 to 1023, as said below
- tags: int32 [6, 2048], P(None, ('groups', 'space')), parts along dimension 1, may hold values from 0 to 3, as said below
- codes: int32 [6, 2048], P(None, ('groups', 'space')), parts along dimension 1, may hold values from 0 to 7
Outputs:
- solution: float32 [8, 320, 2048], P('tm', None, ('groups', 'space')), parts along dimension 2
- after_residual: bfloat16 [8, 320, 2048], P('tm', None, ('groups', 'space')), parts along dimension 2
There are 2 independent parts, one for each index of `groups`. A program takes and returns all parts, laid end to end along the dimension named above; an argument that names none is the same for every part. Nothing has to cross between parts.
Inputs may be any that keep to these rules, and one draw needn't show every extreme that they name: `neighbor`: elements are numbered layer by layer along the trench, 64 to a layer, 16 layers. Where tags is 0, faces 0 and 1 join an element to one of the previous and of the next layer, faces 2 to 5 to one of its own layer; where tags is not 0, the entry is the element itself. `tags`: face 0 of every element of the first layer is 2 and face 1 of every element of the last layer is 3.
All inputs are finite; a program needn't handle non-finite values.
Results may differ from a plain program's by a relative error of at most 0.001.
Values sent between devices are 32-bit elements; how exact they have to be, the bound alone decides.
No kernel may reach another device: no remote copies, remote signals or barrier semaphores. Data moves between devices by JAX's collectives and lax.ppermute only.
A program may use at most 192 MiB of HBM per device.

v0:
```python
import math

import jax
import jax.numpy as jnp
from jax import lax
from jax.sharding import PartitionSpec as P

NF = 5
NP = 4
XSEC = 64


HIGHEST = lax.Precision.HIGHEST


def shifted(block, axis, distance):
    devices = range(lax.axis_size(axis))
    route = [((i - distance) % len(devices), i) for i in devices]
    return lax.ppermute(block, axis, route)


def padded_2(value, sides, width):
    for axis, dim in sides:
        devices, length = (lax.axis_size(axis), value.shape[dim])
        up = [(i, (i + 1) % devices) for i in range(devices - 1)]
        down = [(j, i) for i, j in up]
        last = lax.slice_in_dim(value, length - width, length, axis=dim)
        initial = lax.slice_in_dim(value, 0, width, axis=dim)
        before = lax.ppermute(last, axis, up)
        after = lax.ppermute(initial, axis, down)
        value = jnp.concatenate([before, value, after], axis=dim)
    return value


def face_traces(field_state):
    slices = field_state.shape[0]
    columns = field_state.shape[2]
    cube_view = field_state.reshape(slices, NF, NP, NP, NP, columns)
    edge = NP - 1
    return jnp.stack(
        [
            cube_view[:, :, 0],
            cube_view[:, :, edge],
            cube_view[:, :, :, 0],
            cube_view[:, :, :, edge],
            cube_view[:, :, :, :, 0],
            cube_view[:, :, :, :, edge],
        ],
        axis=0,
    )


def orient(trace_block, codes_row):
    turned = jnp.swapaxes(trace_block, 2, 3)
    trace_block = jnp.where(codes_row % 2 == 1, turned, trace_block)
    trace_block = jnp.where(codes_row // 2 % 2 == 1, jnp.flip(trace_block, 2), trace_block)
    trace_block = jnp.where(codes_row // 4 % 2 == 1, jnp.flip(trace_block, 3), trace_block)
    return trace_block


def seen_traces(own_traces, lookup, targets, tags, codes):
    pieces = []
    for face in range(6):
        across = jnp.take(lookup[face ^ 1], targets[face], axis=-1)
        across = orient(across, codes[face])
        mine = own_traces[face]
        normal_sign = jnp.where(jnp.arange(NF) == 1 + face // 2, -1.0, 1.0).astype(jnp.float32)
        wall = mine * normal_sign[None, :, None, None, None]
        kind = tags[face]
        chosen = jnp.where(
            kind == 0,
            across,
            jnp.where(kind == 1, wall, jnp.where(kind == 2, jnp.zeros_like(mine), mine)),
        )
        pieces.append(chosen)
    return jnp.stack(pieces, axis=0)


def apply_operator(field_state, own_traces, lookup, targets, tags, codes, volume, lifts):
    slices = field_state.shape[0]
    columns = field_state.shape[2]
    seen = seen_traces(own_traces, lookup, targets, tags, codes).reshape(
        6, slices, NF * NP * NP, columns
    )
    inner = jnp.einsum("mk,ske->sme", volume.astype(jnp.float32), field_state, precision=HIGHEST)
    return inner + jnp.einsum("fmk,fske->sme", lifts.astype(jnp.float32), seen, precision=HIGHEST)


def frequency_solve(residual_block, damping_block):
    total_slices = residual_block.shape[0]
    flat = residual_block.reshape(total_slices, -1)
    index = jnp.arange(total_slices, dtype=jnp.int32)
    angle = (
        2.0
        * math.pi
        * (index[:, None] * index[None, :] % total_slices).astype(jnp.float32)
        / total_slices
    )
    cos_table = jnp.cos(angle)
    sin_table = jnp.sin(angle)
    real_part = jnp.dot(cos_table, flat, precision=HIGHEST).reshape(residual_block.shape)
    imag_part = (-jnp.dot(sin_table, flat, precision=HIGHEST)).reshape(residual_block.shape)
    phase = 2.0 * math.pi * index.astype(jnp.float32) / total_slices
    shape_out = (total_slices,) + (1,) * (residual_block.ndim - 1)
    near = (1.0 - jnp.cos(phase)).reshape(shape_out) + damping_block[None]
    far = jnp.sin(phase).reshape(shape_out)
    modulus = near * near + far * far
    fix_real = (real_part * near + imag_part * far) / modulus
    fix_imag = (imag_part * near - real_part * far) / modulus
    back = jnp.dot(cos_table, fix_real.reshape(total_slices, -1), precision=HIGHEST) - jnp.dot(
        sin_table, fix_imag.reshape(total_slices, -1), precision=HIGHEST
    )
    return (back / total_slices).reshape(residual_block.shape)


def local_residual(field_state, forcing, volume, lifts, targets, tags, codes):
    previous_end = shifted(field_state[-1:], "tm", 1)
    previous = jnp.concatenate([previous_end, field_state[:-1]], axis=0)
    own_traces = face_traces(field_state)
    padded = padded_2(field_state, (("space", 2),), XSEC)
    left_rim = face_traces(padded[..., :XSEC])
    right_rim = face_traces(padded[..., -XSEC:])
    lookup = jnp.concatenate([left_rim, own_traces, right_rim], axis=-1)
    image = apply_operator(field_state, own_traces, lookup, targets, tags, codes, volume, lifts)
    return forcing - field_state + previous + image


def local(guess, source_cos, source_sin, damping, volume, lifts, neighbor, tags, codes):
    local_slices = guess.shape[0]
    columns = guess.shape[2]
    time_devices = lax.axis_size("tm")
    total_slices = local_slices * time_devices
    first_slice = lax.axis_index("tm") * local_slices
    slice_index = (first_slice + jnp.arange(local_slices, dtype=jnp.int32)).astype(jnp.float32)
    phases = 2.0 * math.pi * slice_index / total_slices
    forcing = (
        jnp.cos(phases)[:, None, None] * source_cos.astype(jnp.float32)[None]
        + jnp.sin(phases)[:, None, None] * source_sin.astype(jnp.float32)[None]
    )
    offset = lax.axis_index("space") * columns - XSEC
    targets = jnp.clip(neighbor - offset, 0, columns + 2 * XSEC - 1)
    first = local_residual(guess, forcing, volume, lifts, targets, tags, codes)
    spectral = lax.all_to_all(first, "tm", split_axis=1, concat_axis=0, tiled=True)
    share = spectral.shape[1]
    damp_piece = lax.dynamic_slice_in_dim(damping, lax.axis_index("tm") * share, share, 0)
    fixed = frequency_solve(spectral, damp_piece)
    correction = lax.all_to_all(fixed, "tm", split_axis=0, concat_axis=1, tiled=True)
    solution = guess + correction
    after_residual = local_residual(solution, forcing, volume, lifts, targets, tags, codes).astype(
        jnp.bfloat16
    )
    return (solution, after_residual)


def solution(mesh):
    in_specs = (
        P("tm", None, ("groups", "space")),
        P(None, ("groups", "space")),
        P(None, ("groups", "space")),
        P(None, ("groups", "space")),
        P(),
        P(),
        P(None, ("groups", "space")),
        P(None, ("groups", "space")),
        P(None, ("groups", "space")),
    )
    out_specs = (P("tm", None, ("groups", "space")), P("tm", None, ("groups", "space")))
    return jax.shard_map(local, mesh=mesh, in_specs=in_specs, out_specs=out_specs, check_vma=False)
```

profile of v0, /device:TPU:1, one launch (start us, length us, event | category | flops | bytes accessed | tf_op | source)
XLA Modules:
  0.0 735.8 jit_solution(13791018159809136979)
XLA Ops:
  69.9 8.4 %gather_fusion.4 = f32[256,2,5,4,4]{2,4,3,1,0:T(4,128)} fusion(f32[2,5,4,4,384]{1,3,4,2,0:T(4,128)} %bitcast.389, s32[1024]{0:T(1024)S(1)} %get-tuple-element.110), kind=kCustom, calls=%fused_computation.4.clone | custom fusion | bytes 328704 | tf_op jit(solution)/shard_map/jit(_take)/gather | solution.py:64
  89.3 11.8 %rev.83 = f32[2,5,4,4,256]{1,3,2,0,4:T(4,128)} reverse(f32[2,5,4,4,256]{1,3,2,0,4:T(4,128)} %reverse_select_fusion.7), dimensions={3} | reverse | bytes 327680 | tf_op jit(solution)/shard_map/jit(_flip)/rev | solution.py:57
  105.6 8.4 %gather_fusion.5 = f32[256,2,5,4,4]{2,4,3,1,0:T(4,128)} fusion(f32[2,5,4,4,384]{1,3,4,2,0:T(4,128)} %bitcast.380, s32[1024]{0:T(1024)S(1)} %get-tuple-element.109), kind=kCustom, calls=%fused_computation.5.clone | custom fusion | bytes 328704 | tf_op jit(solution)/shard_map/jit(_take)/gather | solution.py:64
  124.7 11.8 %rev.85 = f32[2,5,4,4,256]{1,3,2,0,4:T(4,128)} reverse(f32[2,5,4,4,256]{1,3,2,0,4:T(4,128)} %reverse_select_fusion.6), dimensions={3} | reverse | bytes 327680 | tf_op jit(solution)/shard_map/jit(_flip)/rev | solution.py:57
  136.6 15.3 %fusion.14 = (f32[2,5,4,4,256]{1,3,2,0,4:T(4,128)}, f32[2,5,4,4,256]{1,3,2,0,4:T(4,128)}) fusion(f32[2,5,4,4,1,256]{1,3,2,0,5,4:T(4,128)} %copy.312, f32[2,5,4,4,256]{1,3,2,0,4:T(4,128)} %rev.85, f32[5]{0:T(128)S(1)} %copy-done.103, pred[256]{0:T(512)(128)(4,1)S(1)} %copy-done.67, pred[256]{0:T(512)(128)(4,1)S(1)} %copy-done.65, ...), kind=kLoop, calls=%fused_computation.60 | loop fusion | flops 491520 | bytes 1313300 | tf_op jit(solution)/shard_map/jit(_where)/select_n | solution.py:70
  160.1 8.3 %gather_fusion.2 = f32[256,2,5,4,4]{2,4,3,1,0:T(4,128)} fusion(f32[2,5,4,4,384]{1,3,4,2,0:T(4,128)} %bitcast.390, s32[1024]{0:T(1024)S(1)} %get-tuple-element.112), kind=kCustom, calls=%fused_computation.2.clone | custom fusion | bytes 328704 | tf_op jit(solution)/shard_map/jit(_take)/gather | solution.py:64
  179.2 11.8 %rev.79 = f32[2,5,4,4,256]{1,3,2,0,4:T(4,128)} reverse(f32[2,5,4,4,256]{1,3,2,0,4:T(4,128)} %reverse_select_fusion.9), dimensions={3} | reverse | bytes 327680 | tf_op jit(solution)/shard_map/jit(_flip)/rev | solution.py:57
  195.6 8.4 %gather_fusion.3 = f32[256,2,5,4,4]{2,4,3,1,0:T(4,128)} fusion(f32[2,5,4,4,384]{1,3,4,2,0:T(4,128)} %bitcast.381, s32[1024]{0:T(1024)S(1)} %get-tuple-element.111), kind=kCustom, calls=%fused_computation.3.clone | custom fusion | bytes 328704 | tf_op jit(solution)/shard_map/jit(_take)/gather | solution.py:64
  214.6 11.8 %rev.81 = f32[2,5,4,4,256]{1,3,2,0,4:T(4,128)} reverse(f32[2,5,4,4,256]{1,3,2,0,4:T(4,128)} %reverse_select_fusion.8), dimensions={3} | reverse | bytes 327680 | tf_op jit(solution)/shard_map/jit(_flip)/rev | solution.py:57
  226.5 15.5 %fusion.18 = (f32[2,5,4,4,256]{1,3,2,0,4:T(4,128)}, f32[2,5,4,4,256]{1,3,2,0,4:T(4,128)}) fusion(f32[2,5,4,1,4,256]{1,4,2,0,5,3:T(4,128)} %copy.310, f32[2,5,4,4,256]{1,3,2,0,4:T(4,128)} %rev.81, f32[5]{0:T(128)S(1)} %copy-done.97, pred[256]{0:T(512)(128)(4,1)S(1)} %copy-done.53, pred[256]{0:T(512)(128)(4,1)S(1)} %copy-done.51, ...), kind=kLoop, calls=%fused_computation.70 | loop fusion | flops 491520 | bytes 1313300 | tf_op jit(solution)/shard_map/jit(_where)/select_n | solution.py:70
  250.5 8.4 %gather_fusion.1 = f32[256,2,5,4,4]{2,4,3,1,0:T(4,128)} fusion(f32[2,5,4,4,384]{1,3,4,2,0:T(4,128)} %bitcast.391, s32[1024]{0:T(1024)S(1)} %get-tuple-element.113), kind=kCustom, calls=%fused_computation.1.clone | custom fusion | bytes 328704 | tf_op jit(solution)/shard_map/jit(_take)/gather | solution.py:64
  269.6 11.9 %rev.77 = f32[2,5,4,4,256]{1,3,2,0,4:T(4,128)} reverse(f32[2,5,4,4,256]{1,3,2,0,4:T(4,128)} %reverse_select_fusion.10), dimensions={3} | reverse | bytes 327680 | tf_op jit(solution)/shard_map/jit(_flip)/rev | solution.py:57
  286.0 8.4 %gather_fusion = f32[256,2,5,4,4]{2,4,3,1,0:T(4,128)} fusion(f32[2,5,4,4,384]{1,3,4,2,0:T(4,128)} %bitcast.382, s32[1024]{0:T(1024)S(1)} %get-tuple-element.114), kind=kCustom, calls=%fused_computation.clone | custom fusion | bytes 328704 | tf_op jit(solution)/shard_map/jit(_take)/gather | solution.py:64
  304.3 12.3 %rev.75 = f32[2,5,4,4,256]{1,3,2,0,4:T(4,128)} reverse(f32[2,5,4,4,256]{1,3,2,0,4:T(4,128)} %reverse_select_fusion.11), dimensions={3} | reverse | bytes 327680 | tf_op jit(solution)/shard_map/jit(_flip)/rev | solution.py:57
  316.7 15.4 %fusion.22 = (f32[2,5,4,4,256]{1,3,2,0,4:T(4,128)}, f32[2,5,4,4,256]{1,3,2,0,4:T(4,128)}) fusion(f32[2,5,1,4,4,256]{1,4,3,0,5,2:T(4,128)} %copy.308, f32[2,5,4,4,256]{1,3,2,0,4:T(4,128)} %rev.77, f32[5]{0:T(128)S(1)} %copy-done.105, pred[256]{0:T(512)(128)(4,1)S(1)} %copy-done.41, pred[256]{0:T(512)(128)(4,1)S(1)} %copy-done.39, ...), kind=kLoop, calls=%fused_computation.80 | loop fusion | flops 491520 | bytes 1313300 | tf_op jit(solution)/shard_map/jit(_where)/select_n | solution.py:70
  356.0 15.7 %all-to-all-done = f32[2,320,256]{2,0,1:T(2,128)S(1)} async-done(((f32[2,320,256]{2,0,1:T(2,128)}), f32[2,320,256]{2,0,1:T(2,128)S(1)}, u32[]{:S(2)}, u32[]{:S(2)}) %all-to-all-start) | async-done | bytes 655392 | tf_op jit(solution)/shard_map/all_to_all | solution.py:143
  375.8 19.6 %all_to_all.33 = f32[8,80,256]{2,1,0:T(8,128)S(1)} all-to-all(f32[8,80,256]{2,1,0:T(8,128)S(1)} %copy.261), channel_id=1, replica_groups=mesh['groups'=2,'tm'=4,'space'=4] {'tm'}, dimensions={0} | all-to-all | bytes 1310720 | tf_op jit(solution)/shard_map/all_to_all | solution.py:147
  447.8 8.4 %gather_fusion.10 = f32[256,2,5,4,4]{2,4,3,1,0:T(4,128)} fusion(f32[2,5,4,4,384]{1,3,4,2,0:T(4,128)} %bitcast.383, s32[1024]{0:T(1024)S(1)} %get-tuple-element.110), kind=kCustom, calls=%fused_computation.10.clone | custom fusion | bytes 328704 | tf_op jit(solution)/shard_map/jit(_take)/gather | solution.py:64
  466.9 11.8 %rev.95 = f32[2,5,4,4,256]{1,3,2,0,4:T(4,128)} reverse(f32[2,5,4,4,256]{1,3,2,0,4:T(4,128)} %reverse_select_fusion.1), dimensions={3} | reverse | bytes 327680 | tf_op jit(solution)/shard_map/jit(_flip)/rev | solution.py:57
  483.3 8.4 %gather_fusion.11 = f32[256,2,5,4,4]{2,4,3,1,0:T(4,128)} fusion(f32[2,5,4,4,384]{1,3,4,2,0:T(4,128)} %bitcast.384, s32[1024]{0:T(1024)S(1)} %get-tuple-element.109), kind=kCustom, calls=%fused_computation.11.clone | custom fusion | bytes 328704 | tf_op jit(solution)/shard_map/jit(_take)/gather | solution.py:64
  502.5 11.9 %rev.97 = f32[2,5,4,4,256]{1,3,2,0,4:T(4,128)} reverse(f32[2,5,4,4,256]{1,3,2,0,4:T(4,128)} %reverse_select_fusion), dimensions={3} | reverse | bytes 327680 | tf_op jit(solution)/shard_map/jit(_flip)/rev | solution.py:57
  514.5 15.7 %fusion.2 = (f32[2,5,4,4,256]{1,3,2,0,4:T(4,128)}, f32[2,5,4,4,256]{1,3,2,0,4:T(4,128)}) fusion(f32[2,5,4,4,1,256]{1,3,2,0,5,4:T(4,128)} %copy.330, f32[2,5,4,4,256]{1,3,2,0,4:T(4,128)} %rev.97, f32[5]{0:T(128)S(1)} %copy-done.104, pred[256]{0:T(512)(128)(4,1)S(1)} %copy-done.68, pred[256]{0:T(512)(128)(4,1)S(1)} %copy-done.66, ...), kind=kLoop, calls=%fused_computation.30 | loop fusion | flops 491520 | bytes 1313300 | tf_op jit(solution)/shard_map/jit(_where)/select_n | solution.py:70
  538.5 8.3 %gather_fusion.8 = f32[256,2,5,4,4]{2,4,3,1,0:T(4,128)} fusion(f32[2,5,4,4,384]{1,3,4,2,0:T(4,128)} %bitcast.385, s32[1024]{0:T(1024)S(1)} %get-tuple-element.112), kind=kCustom, calls=%fused_computation.8.clone | custom fusion | bytes 328704 | tf_op jit(solution)/shard_map/jit(_take)/gather | solution.py:64
  557.5 11.9 %rev.91 = f32[2,5,4,4,256]{1,3,2,0,4:T(4,128)} reverse(f32[2,5,4,4,256]{1,3,2,0,4:T(4,128)} %reverse_select_fusion.3), dimensions={3} | reverse | bytes 327680 | tf_op jit(solution)/shard_map/jit(_flip)/rev | solution.py:57
  574.2 8.4 %gather_fusion.9 = f32[256,2,5,4,4]{2,4,3,1,0:T(4,128)} fusion(f32[2,5,4,4,384]{1,3,4,2,0:T(4,128)} %bitcast.386, s32[1024]{0:T(1024)S(1)} %get-tuple-element.111), kind=kCustom, calls=%fused_computation.9.clone | custom fusion | bytes 328704 | tf_op jit(solution)/shard_map/jit(_take)/gather | solution.py:64
  593.3 11.9 %rev.93 = f32[2,5,4,4,256]{1,3,2,0,4:T(4,128)} reverse(f32[2,5,4,4,256]{1,3,2,0,4:T(4,128)} %reverse_select_fusion.2), dimensions={3} | reverse | bytes 327680 | tf_op jit(solution)/shard_map/jit(_flip)/rev | solution.py:57
  605.2 15.1 %fusion.6 = (f32[2,5,4,4,256]{1,3,2,0,4:T(4,128)}, f32[2,5,4,4,256]{1,3,2,0,4:T(4,128)}) fusion(f32[2,5,4,1,4,256]{1,4,2,0,5,3:T(4,128)} %copy.328, f32[2,5,4,4,256]{1,3,2,0,4:T(4,128)} %rev.93, f32[5]{0:T(128)S(1)} %copy-done.98, pred[256]{0:T(512)(128)(4,1)S(1)} %copy-done.54, pred[256]{0:T(512)(128)(4,1)S(1)} %copy-done.52, ...), kind=kLoop, calls=%fused_computation.40 | loop fusion | flops 491520 | bytes 1313300 | tf_op jit(solution)/shard_map/jit(_where)/select_n | solution.py:70
  629.2 8.4 %gather_fusion.6 = f32[256,2,5,4,4]{2,4,3,1,0:T(4,128)} fusion(f32[2,5,4,4,384]{1,3,4,2,0:T(4,128)} %bitcast.387, s32[1024]{0:T(1024)S(1)} %get-tuple-element.114), kind=kCustom, calls=%fused_computation.6.clone | custom fusion | bytes 328704 | tf_op jit(solution)/shard_map/jit(_take)/gather | solution.py:64
  648.4 11.8 %rev.87 = f32[2,5,4,4,256]{1,3,2,0,4:T(4,128)} reverse(f32[2,5,4,4,256]{1,3,2,0,4:T(4,128)} %reverse_select_fusion.5), dimensions={3} | reverse | bytes 327680 | tf_op jit(solution)/shard_map/jit(_flip)/rev | solution.py:57
  664.8 8.4 %gather_fusion.7 = f32[256,2,5,4,4]{2,4,3,1,0:T(4,128)} fusion(f32[2,5,4,4,384]{1,3,4,2,0:T(4,128)} %bitcast.388, s32[1024]{0:T(1024)S(1)} %get-tuple-element.113), kind=kCustom, calls=%fused_computation.7.clone | custom fusion | bytes 328704 | tf_op jit(solution)/shard_map/jit(_take)/gather | solution.py:64
  683.9 11.9 %rev.89 = f32[2,5,4,4,256]{1,3,2,0,4:T(4,128)} reverse(f32[2,5,4,4,256]{1,3,2,0,4:T(4,128)} %reverse_select_fusion.4), dimensions={3} | reverse | bytes 327680 | tf_op jit(solution)/shard_map/jit(_flip)/rev | solution.py:57
  695.8 15.8 %fusion.10 = (f32[2,5,4,4,256]{1,3,2,0,4:T(4,128)}, f32[2,5,4,4,256]{1,3,2,0,4:T(4,128)}) fusion(f32[2,5,1,4,4,256]{1,4,3,0,5,2:T(4,128)} %copy.326, f32[2,5,4,4,256]{1,3,2,0,4:T(4,128)} %rev.89, f32[5]{0:T(128)S(1)} %copy-done.106, pred[256]{0:T(512)(128)(4,1)S(1)} %copy-done.42, pred[256]{0:T(512)(128)(4,1)S(1)} %copy-done.40, ...), kind=kLoop, calls=%fused_computation.50 | loop fusion | flops 491520 | bytes 1313300 | tf_op jit(solution)/shard_map/jit(_where)/select_n | solution.py:70
  (428 shorter events, 361.5 us)
Async XLA Ops:
  0.6 346.5 %copy-start = (bf16[6,320,80]{1,2,0:T(8,128)(2,1)S(1)}, bf16[6,320,80]{1,2,0:T(8,128)(2,1)}, u32[]{:S(2)}) copy-start(bf16[6,320,80]{1,2,0:T(8,128)(2,1)} %param.16) | copy-start | bytes 921604
  2.7 60.8 %collective-permute-start.1 = (f32[2,320,64]{2,1,0:T(8,128)}, f32[2,320,64]{2,1,0:T(8,128)S(1)}, u32[]{:S(2)}, u32[]{:S(2)}) collective-permute-start(f32[2,320,64]{2,1,0:T(8,128)} %get-tuple-element.45), channel_id=1, source_target_pairs={{0,1},{1,2},{2,3},{4,5},{5,6},{6,7},{8,9},{9,10},{10,11},{12,13},{... | collective-permute-start | bytes 491528 | tf_op jit(solution)/shard_map/ppermute | solution.py:29
  7.2 56.5 %collective-permute-start.2 = (f32[2,320,64]{2,1,0:T(8,128)S(1)}, f32[2,320,64]{2,1,0:T(8,128)S(1)}, u32[]{:S(2)}, u32[]{:S(2)}) collective-permute-start(f32[2,320,64]{2,1,0:T(8,128)S(1)} %get-tuple-element.46), channel_id=1, source_target_pairs={{1,0},{2,1},{3,2},{5,4},{6,5},{7,6},{9,8},{10,9},{11,10},{13,12},{... | collective-permute-start | bytes 491528 | tf_op jit(solution)/shard_map/ppermute | solution.py:30
  11.0 336.9 %collective-permute-start = (f32[1,320,256]{2,1,0:T(8,128)}, f32[1,320,256]{2,1,0:T(8,128)}, u32[]{:S(2)}, u32[]{:S(2)}) collective-permute-start(f32[1,320,256]{2,1,0:T(8,128)} %get-tuple-element.53), channel_id=1, source_target_pairs={{12,0},{0,4},{4,8},{8,12},{13,1},{1,5},{5,9},{9,13},{14,2},{2,6},{... | collective-permute-start | bytes 983048 | tf_op jit(solution)/shard_map/ppermute | solution.py:19
  304.2 12.4 %copy-start.35 = (pred[256]{0:T(512)(128)(4,1)S(1)}, pred[256]{0:T(512)(128)(4,1)}, u32[]{:S(2)}) copy-start(pred[256]{0:T(512)(128)(4,1)} %get-tuple-element.4) | copy-start | bytes 772
  304.2 12.4 %copy-start.37 = (pred[256]{0:T(512)(128)(4,1)S(1)}, pred[256]{0:T(512)(128)(4,1)}, u32[]{:S(2)}) copy-start(pred[256]{0:T(512)(128)(4,1)} %get-tuple-element.5) | copy-start | bytes 772
  304.2 12.4 %copy-start.39 = (pred[256]{0:T(512)(128)(4,1)S(1)}, pred[256]{0:T(512)(128)(4,1)}, u32[]{:S(2)}) copy-start(pred[256]{0:T(512)(128)(4,1)} %get-tuple-element.6) | copy-start | bytes 772
  304.2 12.4 %copy-start.41 = (pred[256]{0:T(512)(128)(4,1)S(1)}, pred[256]{0:T(512)(128)(4,1)}, u32[]{:S(2)}) copy-start(pred[256]{0:T(512)(128)(4,1)} %get-tuple-element.7) | copy-start | bytes 772
  304.2 12.4 %copy-start.43 = (pred[256]{0:T(512)(128)(4,1)S(1)}, pred[256]{0:T(512)(128)(4,1)}, u32[]{:S(2)}) copy-start(pred[256]{0:T(512)(128)(4,1)} %get-tuple-element.18) | copy-start | bytes 772
  304.3 12.4 %copy-start.45 = (pred[256]{0:T(512)(128)(4,1)S(1)}, pred[256]{0:T(512)(128)(4,1)}, u32[]{:S(2)}) copy-start(pred[256]{0:T(512)(128)(4,1)} %get-tuple-element.19) | copy-start | bytes 772
  304.3 12.4 %copy-start.71 = (pred[256]{0:T(512)(128)(4,1)S(1)}, pred[256]{0:T(512)(128)(4,1)}, u32[]{:S(2)}) copy-start(pred[256]{0:T(512)(128)(4,1)} %get-tuple-element.87) | copy-start | bytes 772
  304.3 12.4 %copy-start.73 = (pred[256]{0:T(512)(128)(4,1)S(1)}, pred[256]{0:T(512)(128)(4,1)}, u32[]{:S(2)}) copy-start(pred[256]{0:T(512)(128)(4,1)} %get-tuple-element.90) | copy-start | bytes 772
  304.3 12.4 %copy-start.105 = (f32[5]{0:T(128)S(1)}, f32[5]{0:T(128)}, u32[]{:S(2)}) copy-start(f32[5]{0:T(128)} %compare_select_fusion.32) | copy-start | bytes 64
  351.4 20.3 %all-to-all-start = ((f32[2,320,256]{2,0,1:T(2,128)}), f32[2,320,256]{2,0,1:T(2,128)S(1)}, u32[]{:S(2)}, u32[]{:S(2)}) async-start(f32[2,320,256]{2,0,1:T(2,128)} %copy.259), calls=%async_computation | async-start | bytes 1310720 | tf_op jit(solution)/shard_map/all_to_all | solution.py:143
  395.6 337.5 %copy-start.25 = (f32[2,320,256]{2,1,0:T(8,128)}, f32[2,320,256]{2,1,0:T(8,128)S(1)}, u32[]{:S(2)}) copy-start(f32[2,320,256]{2,1,0:T(8,128)S(1)} %bitcast_add_fusion) | copy-start | bytes 1966084
  400.3 36.5 %collective-permute-start.4 = (f32[2,320,64]{2,1,0:T(8,128)}, f32[2,320,64]{2,1,0:T(8,128)}, u32[]{:S(2)}, u32[]{:S(2)}) collective-permute-start(f32[2,320,64]{2,1,0:T(8,128)} %get-tuple-element.39), channel_id=1, source_target_pairs={{0,1},{1,2},{2,3},{4,5},{5,6},{6,7},{8,9},{9,10},{10,11},{12,13},{... | collective-permute-start | bytes 491528 | tf_op jit(solution)/shard_map/ppermute | solution.py:29
  412.5 26.4 %collective-permute-start.5 = (f32[2,320,64]{2,1,0:T(8,128)}, f32[2,320,64]{2,1,0:T(8,128)S(1)}, u32[]{:S(2)}, u32[]{:S(2)}) collective-permute-start(f32[2,320,64]{2,1,0:T(8,128)} %get-tuple-element.40), channel_id=1, source_target_pairs={{1,0},{2,1},{3,2},{5,4},{6,5},{7,6},{9,8},{10,9},{11,10},{13,12},{... | collective-permute-start | bytes 491528 | tf_op jit(solution)/shard_map/ppermute | solution.py:30
  429.4 303.6 %collective-permute-start.3 = (f32[1,320,256]{2,1,0:T(8,128)}, f32[1,320,256]{2,1,0:T(8,128)}, u32[]{:S(2)}, u32[]{:S(2)}) collective-permute-start(f32[1,320,256]{2,1,0:T(8,128)} %get-tuple-element.43), channel_id=1, source_target_pairs={{12,0},{0,4},{4,8},{8,12},{13,1},{1,5},{5,9},{9,13},{14,2},{2,6},{... | collective-permute-start | bytes 983048 | tf_op jit(solution)/shard_map/ppermute | solution.py:19
  593.2 11.9 %copy-start.56 = (pred[256]{0:T(512)(128)(4,1)S(1)}, pred[256]{0:T(512)(128)(4,1)}, u32[]{:S(2)}) copy-start(pred[256]{0:T(512)(128)(4,1)} %get-tuple-element.16) | copy-start | bytes 772
  593.2 11.9 %copy-start.58 = (pred[256]{0:T(512)(128)(4,1)S(1)}, pred[256]{0:T(512)(128)(4,1)}, u32[]{:S(2)}) copy-start(pred[256]{0:T(512)(128)(4,1)} %get-tuple-element.17) | copy-start | bytes 772
  593.2 11.9 %copy-start.78 = (pred[256]{0:T(512)(128)(4,1)S(1)}, pred[256]{0:T(512)(128)(4,1)}, u32[]{:S(2)}) copy-start(pred[256]{0:T(512)(128)(4,1)} %get-tuple-element.84) | copy-start | bytes 772
  593.3 11.9 %copy-start.82 = (pred[256]{0:T(512)(128)(4,1)S(1)}, pred[256]{0:T(512)(128)(4,1)}, u32[]{:S(2)}) copy-start(pred[256]{0:T(512)(128)(4,1)} %get-tuple-element.81) | copy-start | bytes 772
  593.3 11.9 %copy-start.98 = (f32[5]{0:T(128)S(1)}, f32[5]{0:T(128)}, u32[]{:S(2)}) copy-start(f32[5]{0:T(128)} %compare_select_fusion.31) | copy-start | bytes 64
  683.8 11.9 %copy-start.36 = (pred[256]{0:T(512)(128)(4,1)S(1)}, pred[256]{0:T(512)(128)(4,1)}, u32[]{:S(2)}) copy-start(pred[256]{0:T(512)(128)(4,1)} %get-tuple-element.4) | copy-start | bytes 772
  683.8 11.9 %copy-start.38 = (pred[256]{0:T(512)(128)(4,1)S(1)}, pred[256]{0:T(512)(128)(4,1)}, u32[]{:S(2)}) copy-start(pred[256]{0:T(512)(128)(4,1)} %get-tuple-element.5) | copy-start | bytes 772
  683.8 11.9 %copy-start.40 = (pred[256]{0:T(512)(128)(4,1)S(1)}, pred[256]{0:T(512)(128)(4,1)}, u32[]{:S(2)}) copy-start(pred[256]{0:T(512)(128)(4,1)} %get-tuple-element.6) | copy-start | bytes 772
  683.8 11.9 %copy-start.42 = (pred[256]{0:T(512)(128)(4,1)S(1)}, pred[256]{0:T(512)(128)(4,1)}, u32[]{:S(2)}) copy-start(pred[256]{0:T(512)(128)(4,1)} %get-tuple-element.7) | copy-start | bytes 772
  683.8 12.0 %copy-start.44 = (pred[256]{0:T(512)(128)(4,1)S(1)}, pred[256]{0:T(512)(128)(4,1)}, u32[]{:S(2)}) copy-start(pred[256]{0:T(512)(128)(4,1)} %get-tuple-element.18) | copy-start | bytes 772
  683.8 12.0 %copy-start.46 = (pred[256]{0:T(512)(128)(4,1)S(1)}, pred[256]{0:T(512)(128)(4,1)}, u32[]{:S(2)}) copy-start(pred[256]{0:T(512)(128)(4,1)} %get-tuple-element.19) | copy-start | bytes 772
  683.8 12.0 %copy-start.72 = (pred[256]{0:T(512)(128)(4,1)S(1)}, pred[256]{0:T(512)(128)(4,1)}, u32[]{:S(2)}) copy-start(pred[256]{0:T(512)(128)(4,1)} %get-tuple-element.87) | copy-start | bytes 772
  683.9 12.0 %copy-start.74 = (pred[256]{0:T(512)(128)(4,1)S(1)}, pred[256]{0:T(512)(128)(4,1)}, u32[]{:S(2)}) copy-start(pred[256]{0:T(512)(128)(4,1)} %get-tuple-element.90) | copy-start | bytes 772
  683.9 12.0 %copy-start.106 = (f32[5]{0:T(128)S(1)}, f32[5]{0:T(128)}, u32[]{:S(2)}) copy-start(f32[5]{0:T(128)} %compare_select_fusion.32) | copy-start | bytes 64
  (82 other events, 589.8 us)
where the time goes:
time: 751 us; the launch traced here: 736 us
  local copies, waits for them, and re-layouts  469 us (62%)
  other arithmetic  203 us (27%)
  blocking collectives  19.6 us (3%)
  starting transfers between devices  16.3 us (2%)
  waiting for transfers between devices  15.7 us (2%)
  matrix products  9.6 us (1%)
    rev x12, local copies, waits for them, and re-layouts, orient(): jnp.flip(trace_block, 3)  143 us
    unnamed x280, local copies, waits for them, and re-layouts  134 us
    gather x12, local copies, waits for them, and re-layouts, seen_traces(): across = jnp.take(lookup[face ^ 1], targets[face], axis=-1)  101 us
    select_n x6, other arithmetic, seen_traces(): jnp.where(kind == 0, across, jnp.where(kind == 1, wall, jnp.where(kind ==...  92.8 us
    select_n x12, local copies, waits for them, and re-layouts, seen_traces(): jnp.where(kind == 0, across, jnp.where(kind == 1, wall, jnp.where(kind ==...  43.6 us
    transpose x11, other arithmetic, orient(): turned = jnp.swapaxes(trace_block, 2, 3)  36.1 us
    select_n x12, other arithmetic, orient(): jnp.where(codes_row // 2 % 2 == 1, jnp.flip(trace_block, 2), trace_block)  32.7 us
    another operation x13, local copies, waits for them, and re-layouts, face_traces(): jnp.stack([cube_view[:, :, 0], cube_view[:, :, edge], cube_view[:, :, :,...  29.9 us
  transfers between devices with their start and end apart: 7, of which 1 were waited for; matrix products, arithmetic and copies ran while one was open for 87% of the time, Pallas kernels for 0%

commit v1 on v0

v1 whole, which is shorter than its diff:
```python
import functools
import math

import jax
import jax.numpy as jnp
import numpy as np
from jax import lax
from jax.experimental import pallas as pl
from jax.experimental.pallas import tpu as pltpu
from jax.sharding import PartitionSpec as P

NF = 5
NP = 4
FACE = NF * NP * NP
LANES = 128
HALF = 64


def split(value):
    high = value.astype(jnp.bfloat16)
    low = (value - high.astype(jnp.float32)).astype(jnp.bfloat16)
    return high, low


def end_trace(cube, face):
    rows = cube[:, 0:16] if face == 0 else cube[:, 48:64]
    return rows.reshape(FACE, LANES)


def side_trace(cube, face):
    tiles = cube.reshape(NF, 2, 2, 16, LANES)
    part = tiles[:, :, :, 0:8] if face == 2 else tiles[:, :, :, 8:16]
    even = part[:, :, 0].reshape(FACE // 8, 8, LANES)
    odd = part[:, :, 1].reshape(FACE // 8, 8, LANES)
    lower = lax.broadcasted_iota(jnp.int32, (FACE // 8, 8, LANES), 1) < 4
    if face == 2:
        odd = pltpu.roll(odd, 4, axis=1)
    else:
        even = pltpu.roll(even, 4, axis=1)
    return jnp.where(lower, even, odd).reshape(FACE, LANES)


def lane_index(row):
    return jnp.broadcast_to(row, (FACE, LANES))


def orientation(code):
    swap = (code & 1) == 1
    turn_i = (code & 2) == 2
    turn_j = (code & 4) == 4
    result = []
    for tile in range(2):
        row = lax.broadcasted_iota(jnp.int32, (8, LANES), 0) + 8 * tile
        i, j = row >> 2, row & 3
        i = jnp.where(turn_i, 3 - i, i)
        j = jnp.where(turn_j, 3 - j, j)
        source = jnp.where(swap, j * 4 + i, i * 4 + j)
        result.append((source >= 8, source & 7))
    return result


def oriented(value, plan):
    pieces = []
    for field in range(NF):
        first = value[field * 16 : field * 16 + 8]
        second = value[field * 16 + 8 : field * 16 + 16]
        for upper, sub in plan:
            pick = functools.partial(jnp.take_along_axis, axis=0, mode="promise_in_bounds")
            pieces.append(jnp.where(upper, pick(second, sub), pick(first, sub)))
    return jnp.concatenate(pieces, axis=0)


def gather_lanes(value, row):
    return jnp.take_along_axis(value, lane_index(row), axis=1, mode="promise_in_bounds")


def operator(state, blocks, stack, weights, volume_ref, lifts_ref, neighbor_ref, tags_ref, codes_ref):
    slices, rows, columns = state.shape
    count = columns // LANES
    wide = slices * columns
    weights[:, 0:rows] = volume_ref[...]
    for face in range(6):
        weights[:, rows + FACE * face : rows + FACE * (face + 1)] = lifts_ref[face]
    lane = lax.broadcasted_iota(jnp.int32, (FACE, LANES), 1)
    for item in range(slices):
        for block in range(count):
            n = item * count + block
            value = state[item, :, block * LANES : (block + 1) * LANES]
            blocks[n] = value
            high, low = split(value)
            stack[0:rows, n * LANES : (n + 1) * LANES] = high
            stack[0:rows, wide + n * LANES : wide + (n + 1) * LANES] = low
    for item in range(slices):
        cubes = []
        turned = []
        for block in range(count):
            cube = blocks[item * count + block].reshape(NF, NP**3, LANES)
            cubes.append(cube)
            turned.append(
                [pltpu.roll(end_trace(cube, face), HALF, axis=1) for face in range(2)]
            )
        zero = jnp.zeros((FACE, LANES), jnp.float32)
        for block in range(count):
            n = item * count + block
            cube = cubes[block]
            before = turned[block - 1][1] if block > 0 else zero
            after = turned[block + 1][0] if block + 1 < count else zero
            ends = [end_trace(cube, 0), end_trace(cube, 1)]
            sides = [side_trace(cube, 2), side_trace(cube, 3)]
            tops = [
                blocks[n, pl.ds(0, FACE, stride=4), :],
                blocks[n, pl.ds(3, FACE, stride=4), :],
            ]
            mine = ends + sides + tops
            across = [
                jnp.where(lane < HALF, before, turned[block][1]),
                jnp.where(lane < HALF, turned[block][0], after),
                sides[1],
                sides[0],
                tops[1],
                tops[0],
            ]
            for face in range(6):
                span = slice(block * LANES, (block + 1) * LANES)
                target = neighbor_ref[face : face + 1, span]
                kind = tags_ref[face : face + 1, span]
                code = codes_ref[face : face + 1, span]
                if face < 2:
                    target = target + HALF
                plan = orientation(code)
                taken = oriented(gather_lanes(across[face], target & (LANES - 1)), plan)
                keep = jnp.where((kind == 1) | (kind == 3), 1.0, 0.0)
                flip = jnp.where(kind == 1, -1.0, keep)
                axis = 1 + face // 2
                inner = []
                for field in range(NF):
                    own = mine[face][field * 16 : (field + 1) * 16]
                    inner.append(own * (flip if field == axis else keep))
                seen = jnp.where(kind == 0, taken, jnp.concatenate(inner, axis=0))
                high, low = split(seen)
                place = rows + FACE * face
                stack[place : place + FACE, n * LANES : (n + 1) * LANES] = high
                stack[place : place + FACE, wide + n * LANES : wide + (n + 1) * LANES] = low
    image = jnp.dot(weights[...], stack[:, 0:wide], preferred_element_type=jnp.float32)
    return image + jnp.dot(weights[...], stack[:, wide:], preferred_element_type=jnp.float32)


def rim(left, right, lifts_ref, neighbor_ref, tags_ref, codes_ref, count):
    slices = left.shape[0]
    lane = lax.broadcasted_iota(jnp.int32, (1, LANES), 1)
    result = []
    for face, halo in ((0, left), (1, right)):
        block = 0 if face == 0 else count - 1
        span = slice(block * LANES, (block + 1) * LANES)
        target = (neighbor_ref[face : face + 1, span] + HALF) & (LANES - 1)
        inside = lane < HALF if face == 0 else lane >= HALF
        use = (tags_ref[face : face + 1, span] == 0) & inside
        plan = orientation(codes_ref[face : face + 1, span])
        pieces = []
        for item in range(slices):
            shifted = pltpu.roll(halo[item], HALF, axis=1)
            seen = jnp.where(use, oriented(gather_lanes(shifted, target), plan), 0.0)
            pieces.append(split(seen))
        both = jnp.concatenate([p[0] for p in pieces] + [p[1] for p in pieces], axis=1)
        product = jnp.dot(lifts_ref[face], both, preferred_element_type=jnp.float32)
        wide = slices * LANES
        result.append(product[:, :wide] + product[:, wide:])
    return result


def send_kernel(state_ref, left_ref, right_ref):
    slices, rows, columns = state_ref.shape
    for item in range(slices):
        for field in range(NF):
            at = field * 64
            to = slice(field * 16, field * 16 + 16)
            left_ref[item, to, :] = state_ref[item, at : at + 16, 0:LANES]
            right_ref[item, to, :] = state_ref[item, at + 48 : at + 64, columns - LANES :]


def forcing_of(waves_ref, item, slices, cos_ref, sin_ref):
    at = lax.axis_index("tm") * slices + item
    return waves_ref[0, at] * cos_ref[...].astype(jnp.float32) + waves_ref[1, at] * sin_ref[
        ...
    ].astype(jnp.float32)


def first_kernel(
    waves_ref, state_ref, cos_ref, sin_ref, damping_ref, volume_ref, lifts_ref, neighbor_ref,
    tags_ref, codes_ref, out_ref, blocks, stack, weights,
):
    slices, _, columns = state_ref.shape
    image = operator(
        state_ref, blocks, stack, weights, volume_ref, lifts_ref, neighbor_ref, tags_ref, codes_ref
    )
    for item in range(slices):
        forcing = forcing_of(waves_ref, item, slices, cos_ref, sin_ref)
        out_ref[item] = (
            image[:, item * columns : (item + 1) * columns]
            + forcing
            + damping_ref[...] * state_ref[item]
        )


def carry_kernel(
    part_ref, left_ref, right_ref, damping_ref, lifts_ref, neighbor_ref, tags_ref, codes_ref,
    out_ref, carry_ref,
):
    slices, _, columns = part_ref.shape
    count = columns // LANES
    low, high = rim(left_ref, right_ref, lifts_ref, neighbor_ref, tags_ref, codes_ref, count)
    for block in range(count):
        span = slice(block * LANES, (block + 1) * LANES)
        rate = 1.0 / (1.0 + damping_ref[:, span])
        carry = None
        for item in range(slices):
            value = part_ref[item, :, span]
            piece = slice(item * LANES, (item + 1) * LANES)
            if block == 0:
                value = value + low[:, piece]
            if block == count - 1:
                value = value + high[:, piece]
            out_ref[item, :, span] = value
            carry = rate * value if carry is None else rate * (carry + value)
        carry_ref[:, span] = carry


def solve_kernel(pieces, *refs):
    piece_refs = refs[:pieces]
    right_ref, damping_ref, state_ref, before_ref, low_ref, high_ref = refs[pieces:]
    slices, rows, columns = right_ref.shape
    if pieces == 1:
        before_ref[...] = piece_refs[0][...]
    else:
        share = rows // pieces
        me = lax.axis_index("tm")
        for step in range(pieces):
            owner = lax.rem(me + pieces - step, pieces)
            before_ref[pl.ds(pl.multiple_of(owner * share, 8), share), :] = piece_refs[step][...]
    rate = 1.0 / (1.0 + damping_ref[...])
    value = before_ref[...]
    for item in range(slices):
        value = rate * (value + right_ref[item])
        state_ref[item] = value
    send_kernel(state_ref, low_ref, high_ref)


def second_kernel(
    waves_ref, state_ref, before_ref, cos_ref, sin_ref, volume_ref, lifts_ref, neighbor_ref,
    tags_ref, codes_ref, out_ref, blocks, stack, weights,
):
    slices, _, columns = state_ref.shape
    image = operator(
        state_ref, blocks, stack, weights, volume_ref, lifts_ref, neighbor_ref, tags_ref, codes_ref
    )
    for item in range(slices):
        forcing = forcing_of(waves_ref, item, slices, cos_ref, sin_ref)
        previous = before_ref[...] if item == 0 else state_ref[item - 1]
        out_ref[item] = (
            image[:, item * columns : (item + 1) * columns]
            + forcing
            + (previous - state_ref[item])
        )


def finish_kernel(
    part_ref, left_ref, right_ref, lifts_ref, neighbor_ref, tags_ref, codes_ref, out_ref
):
    slices, _, columns = part_ref.shape
    count = columns // LANES
    low, high = rim(left_ref, right_ref, lifts_ref, neighbor_ref, tags_ref, codes_ref, count)
    for block in range(count):
        span = slice(block * LANES, (block + 1) * LANES)
        for item in range(slices):
            value = part_ref[item, :, span]
            piece = slice(item * LANES, (item + 1) * LANES)
            if block == 0:
                value = value + low[:, piece]
            if block == count - 1:
                value = value + high[:, piece]
            out_ref[item, :, span] = value.astype(out_ref.dtype)


def call(kernel, name, outs, args, scratch=(), scalars=0, flops=0):
    vmem = pl.BlockSpec(memory_space=pltpu.VMEM)
    smem = pl.BlockSpec(memory_space=pltpu.SMEM)
    size = sum(math.prod(a.shape) * a.dtype.itemsize for a in list(args) + list(outs))
    return pl.pallas_call(
        kernel,
        name=name,
        out_shape=outs,
        in_specs=[smem] * scalars + [vmem] * (len(args) - scalars),
        out_specs=[vmem] * len(outs),
        scratch_shapes=list(scratch),
        compiler_params=pltpu.CompilerParams(vmem_limit_bytes=40 * 2**20),
        cost_estimate=pl.CostEstimate(flops=flops, bytes_accessed=size, transcendentals=0),
    )(*args)


def halos(low, high):
    count = lax.axis_size("space")
    left = lax.ppermute(high, "space", [(i, i + 1) for i in range(count - 1)])
    right = lax.ppermute(low, "space", [(i + 1, i) for i in range(count - 1)])
    return left, right


def turned(value, distance):
    count = lax.axis_size("tm")
    return lax.ppermute(value, "tm", [(i, (i + distance) % count) for i in range(count)])


def periodic(carries, factor):
    count = len(carries)
    total = carries[0]
    for k in range(1, count):
        total = carries[k] + factor * total
    power = factor
    for _ in range(count - 1):
        power = power * factor
    entering = [total / (1.0 - power)]
    for k in range(count - 1):
        entering.append(carries[k] + factor * entering[-1])
    return entering


def around(carry, damping, slices):
    count = lax.axis_size("tm")
    rows = carry.shape[0]
    share = rows // count
    me = lax.axis_index("tm")
    rate = 1.0 / (1.0 + lax.dynamic_slice_in_dim(damping, me * share, share, 0))
    factor = rate
    for _ in range(slices - 1):
        factor = factor * rate
    if count > 8 or share % 8:
        parts = lax.all_to_all(carry, "tm", split_axis=0, concat_axis=0, tiled=True)
        parts = parts.reshape(count, share, -1)
        back = jnp.concatenate(periodic([parts[k] for k in range(count)], factor), axis=0)
        return [lax.all_to_all(back, "tm", split_axis=0, concat_axis=0, tiled=True)]
    parts = carry.reshape(count, share, -1)
    sent = [
        lax.dynamic_index_in_dim(parts, lax.rem(me + d, count), 0, keepdims=False)
        for d in range(count)
    ]
    got = [sent[0]] + [turned(sent[d], d) for d in range(1, count)]
    entering = periodic([got[(count - k) % count] for k in range(count)], factor)
    return [entering[0]] + [turned(entering[d], d) for d in range(1, count)]


def local(guess, source_cos, source_sin, damping, volume, lifts, neighbor, tags, codes):
    slices, rows, columns = guess.shape
    total = slices * lax.axis_size("tm")
    angles = 2.0 * np.pi * np.arange(total) / total
    waves = jnp.asarray(np.stack([np.cos(angles), np.sin(angles)]).astype(np.float32))
    f32 = jnp.float32
    whole = jax.ShapeDtypeStruct((slices, rows, columns), f32)
    plane = jax.ShapeDtypeStruct((rows, columns), f32)
    rimmed = jax.ShapeDtypeStruct((slices, FACE, LANES), f32)
    tables = (lifts, neighbor, tags, codes)
    depth = rows + 6 * FACE
    scratch = (
        pltpu.VMEM((slices * columns // LANES, rows, LANES), f32),
        pltpu.VMEM((depth, 2 * slices * columns), jnp.bfloat16),
        pltpu.VMEM((rows, depth), jnp.bfloat16),
    )
    work = 4 * rows * depth * slices * columns

    low, high = call(send_kernel, "ends", [rimmed] * 2, [guess])
    left, right = halos(low, high)
    (part,) = call(
        first_kernel, "first", [whole],
        [waves, guess, source_cos, source_sin, damping, volume, *tables],
        scratch, scalars=1, flops=work,
    )
    known, carry = call(
        carry_kernel, "carry", [whole, plane], [part, left, right, damping, *tables]
    )
    pieces = around(carry, damping, slices)
    state, before, low, high = call(
        functools.partial(solve_kernel, len(pieces)), "solve",
        [whole, plane, rimmed, rimmed], [*pieces, known, damping],
    )
    left, right = halos(low, high)
    (part,) = call(
        second_kernel, "second", [whole],
        [waves, state, before, source_cos, source_sin, volume, *tables],
        scratch, scalars=1, flops=work,
    )
    (after,) = call(
        finish_kernel, "finish", [jax.ShapeDtypeStruct(whole.shape, jnp.bfloat16)],
        [part, left, right, *tables],
    )
    return state, after


def solution(mesh):
    column = P(None, ("groups", "space"))
    state = P("tm", None, ("groups", "space"))
    in_specs = (state, column, column, column, P(), P(), column, column, column)
    return jax.shard_map(
        local, mesh=mesh, in_specs=in_specs, out_specs=(state, state), check_vma=False
    )
```

time: 751 us -> 45 us (0.06); the launches traced: 736 us -> 44.7 us
  local copies, waits for them, and re-layouts: 469 us -> 3.58 us
  other arithmetic: 203 us -> 0.07 us
  blocking collectives: 19.6 us -> 0 us
  matrix products: 9.6 us -> 0 us
    select_n x40 -> x0, other arithmetic: 160 us -> none  [the longest x6 92.8 us: seen_traces(): jnp.where(kind == 0, across, jnp.where(kind == 1, wall, jnp.where(kind ==...]
    rev x12 -> x0, local copies, waits for them, and re-layouts: 143 us -> none  [orient(): jnp.flip(trace_block, 3)]
    unnamed x280 -> x23, local copies, waits for them, and re-layouts: 134 us -> 3.55 us
    gather x12 -> x0, local copies, waits for them, and re-layouts: 101 us -> none  [seen_traces(): across = jnp.take(lookup[face ^ 1], targets[face], axis=-1)]
    select_n x12 -> x0, local copies, waits for them, and re-layouts: 43.6 us -> none  [seen_traces(): jnp.where(kind == 0, across, jnp.where(kind == 1, wall, jnp.where(kind ==...]
    transpose x11 -> x0, other arithmetic: 36.1 us -> none  [orient(): turned = jnp.swapaxes(trace_block, 2, 3)]
    another operation x27 -> x0, local copies, waits for them, and re-layouts: 34.3 us -> none  [the longest x13 29.9 us: face_traces(): jnp.stack([cube_view[:, :, 0], cube_view[:, :, edge], cube_view[:, :, :,...]
    all_to_all x1 -> x0, blocking collectives: 19.6 us -> none  [local(): lax.all_to_all(fixed, 'tm', split_axis=0, concat_axis=1, tiled=True)]
  transfers between devices with their start and end apart: 7 -> 10, of which waited for: 1 -> 6; matrix products, arithmetic and copies ran while one was open for 87% -> 3% of each run, Pallas kernels for 0% -> 10%
where the time goes in v1:
time: 45 us; the launch traced here: 44.7 us
  starting transfers between devices  18.5 us (41%)
  waiting for transfers between devices  14.1 us (31%)
  Pallas kernels  7.47 us (17%)
  local copies, waits for them, and re-layouts  3.58 us (8%)
  between operations  0.91 us (2%)
    ppermute x6, waiting for transfers between devices, turned(): lax.ppermute(value, 'tm', [(i, (i + distance) % count) for i in range(cou...  13.8 us
    ppermute x2, starting transfers between devices, halos(): left = lax.ppermute(high, 'space', [(i, i + 1) for i in range(count - 1)])  8.07 us
    pallas_call x6, Pallas kernels, call(): pl.pallas_call(kernel, name=name, out_shape=outs, in_specs=[smem] * scala...  7.47 us
    ppermute x6, starting transfers between devices, turned(): lax.ppermute(value, 'tm', [(i, (i + distance) % count) for i in range(cou...  6.58 us
    ppermute x2, starting transfers between devices, halos(): right = lax.ppermute(low, 'space', [(i + 1, i) for i in range(count - 1)])  3.84 us
    unnamed x23, local copies, waits for them, and re-layouts  3.55 us
  transfers between devices with their start and end apart: 10, of which 6 were waited for; matrix products, arithmetic and copies ran while one was open for 3% of the time, Pallas kernels for 10%

profile of v1, /device:TPU:1, one launch (start us, length us, event | category | flops | bytes accessed | tf_op | source)
XLA Modules:
  0.0 44.7 jit_solution(10405467421930479271)
XLA Ops:
  0.6 1.1 %copy-done.1 = f32[2,320,256]{2,1,0:T(8,128)S(1)} copy-done((f32[2,320,256]{2,1,0:T(8,128)S(1)}, f32[2,320,256]{2,1,0:T(8,128)}, u32[]{:S(2)}) %copy-start.1) | copy-done | bytes 655384
  1.7 4.6 %collective-permute-start = (f32[2,80,128]{2,1,0:T(8,128)S(1)}, f32[2,80,128]{2,1,0:T(8,128)S(1)}, u32[]{:S(2)}, u32[]{:S(2)}) collective-permute-start(f32[2,80,128]{2,1,0:T(8,128)S(1)} %get-tuple-element.10), channel_id=1, source_target_pairs={{0,1},{1,2},{2,3},{4,5},{5,6},{6,7},{8,9},{9,10},{10,11},{12,13},{... | collective-permute-start | bytes 245768 | tf_op jit(solution)/shard_map/ppermute | solution.py:302
  6.4 1.9 %collective-permute-start.1 = (f32[2,80,128]{2,1,0:T(8,128)S(1)}, f32[2,80,128]{2,1,0:T(8,128)S(1)}, u32[]{:S(2)}, u32[]{:S(2)}) collective-permute-start(f32[2,80,128]{2,1,0:T(8,128)S(1)} %get-tuple-element.11), channel_id=1, source_target_pairs={{1,0},{2,1},{3,2},{5,4},{6,5},{7,6},{9,8},{10,9},{11,10},{13,12},{... | collective-permute-start | bytes 245768 | tf_op jit(solution)/shard_map/ppermute | solution.py:303
  8.3 0.0 copy-start.7
  8.3 0.0 copy-start.8
  8.3 0.0 copy-start.10
  8.4 0.0 copy-start.5
  8.4 0.0 copy-start
  8.4 0.0 copy-start.3
  8.4 0.0 copy-start.4
  8.4 1.3 %copy.12.lifts_ref = bf16[6,320,80]{2,1,0:T(8,128)(2,1)S(1)} copy(bf16[6,320,80]{1,2,0:T(8,128)(2,1)} %param.15) | data formatting | bytes 614400 | tf_op args[5]
  9.9 2.3 %first.1.part_ref = f32[2,320,256]{2,1,0:T(8,128)S(1)} custom-call(f32[2,8]{1,0:T(2,128)S(1)} %copy-done.10, f32[2,320,256]{2,1,0:T(8,128)S(1)} %copy-done.2, bf16[320,256]{1,0:T(8,128)(2,1)S(1)} %copy-done.4, bf16[320,256]{1,0:T(8,128)(2,1)S(1)} %copy-done.5, f32[320,256]{1,0:T(8,128)S(1)} %copy-done, bf16[320,320]{1,0:T(8,128)(2,1)S(1)} %copy-done.3, ...), custom_call_target="tpu_custom_call" | custom-call | flops 524288000 | bytes 2496576 | tf_op jit(solution)/shard_map/first/pallas_call | solution.py:288
  12.2 0.5 %carry.1 = (f32[2,320,256]{2,1,0:T(8,128)S(1)}, f32[320,256]{1,0:T(8,128)S(1)}) custom-call(f32[2,320,256]{2,1,0:T(8,128)S(1)} %first.1.part_ref, f32[2,80,128]{2,1,0:T(8,128)S(1)} %collective-permute-done.left_ref, f32[2,80,128]{2,1,0:T(8,128)S(1)} %collective-permute-done.1.right_ref, f32[320,256]{1,0:T(8,128)S(1)} %copy-done, ...), custom_call_target="tpu_custom_call" | custom-call | bytes 2455552 | tf_op jit(solution)/shard_map/carry/pallas_call | solution.py:288
  12.8 1.4 %collective-permute-start.2 = (f32[80,256]{1,0:T(8,128)S(1)}, f32[80,256]{1,0:T(8,128)S(1)}, u32[]{:S(2)}, u32[]{:S(2)}) collective-permute-start(f32[80,256]{1,0:T(8,128)S(1)} %get-tuple-element.22), channel_id=1, source_target_pairs={{0,4},{4,8},{8,12},{12,0},{1,5},{5,9},{9,13},{13,1},{2,6},{6,10},{... | collective-permute-start | bytes 245768 | tf_op jit(solution)/shard_map/ppermute | solution.py:309
  14.1 2.1 %collective-permute-start.4 = (f32[80,256]{1,0:T(8,128)S(1)}, f32[80,256]{1,0:T(8,128)S(1)}, u32[]{:S(2)}, u32[]{:S(2)}) collective-permute-start(f32[80,256]{1,0:T(8,128)S(1)} %get-tuple-element.23), channel_id=1, source_target_pairs={{0,12},{4,0},{8,4},{12,8},{1,13},{5,1},{9,5},{13,9},{2,14},{6,2},{... | collective-permute-start | bytes 245768 | tf_op jit(solution)/shard_map/ppermute | solution.py:309
  16.2 0.4 collective-permute-start.3
  16.6 1.9 %collective-permute-done.2 = f32[80,256]{1,0:T(8,128)S(1)} collective-permute-done((f32[80,256]{1,0:T(8,128)S(1)}, f32[80,256]{1,0:T(8,128)S(1)}, u32[]{:S(2)}, u32[]{:S(2)}) %collective-permute-start.2) | collective-permute-done | bytes 81952 | tf_op jit(solution)/shard_map/ppermute | solution.py:309
  18.6 1.0 %collective-permute-done.4 = f32[80,256]{1,0:T(8,128)S(1)} collective-permute-done((f32[80,256]{1,0:T(8,128)S(1)}, f32[80,256]{1,0:T(8,128)S(1)}, u32[]{:S(2)}, u32[]{:S(2)}) %collective-permute-start.4) | collective-permute-done | bytes 81952 | tf_op jit(solution)/shard_map/ppermute | solution.py:309
  19.6 3.0 %collective-permute-done.3 = f32[80,256]{1,0:T(8,128)S(1)} collective-permute-done((f32[80,256]{1,0:T(8,128)S(1)}, f32[80,256]{1,0:T(8,128)S(1)}, u32[]{:S(2)}, u32[]{:S(2)}) %collective-permute-start.3) | collective-permute-done | bytes 81952 | tf_op jit(solution)/shard_map/ppermute | solution.py:309
  22.6 0.1 multiply_add_fusion
  22.6 2.4 %collective-permute-start.7 = (f32[80,256]{1,0:T(8,128)S(1)}, f32[80,256]{1,0:T(8,128)S(1)}, u32[]{:S(2)}, u32[]{:S(2)}) collective-permute-start(f32[80,256]{1,0:T(8,128)S(1)} %get-tuple-element.18), channel_id=1, source_target_pairs={{0,12},{4,0},{8,4},{12,8},{1,13},{5,1},{9,5},{13,9},{2,14},{6,2},{... | collective-permute-start | bytes 245768 | tf_op jit(solution)/shard_map/ppermute | solution.py:309
  25.0 0.4 collective-permute-start.5
  25.4 1.3 %collective-permute-done.7.refs_3_ = f32[80,256]{1,0:T(8,128)S(1)} collective-permute-done((f32[80,256]{1,0:T(8,128)S(1)}, f32[80,256]{1,0:T(8,128)S(1)}, u32[]{:S(2)}, u32[]{:S(2)}) %collective-permute-start.7) | collective-permute-done | bytes 81952 | tf_op jit(solution)/shard_map/ppermute | solution.py:309
  26.7 6.5 %collective-permute-done.6.refs_2_ = f32[80,256]{1,0:T(8,128)S(1)} collective-permute-done((f32[80,256]{1,0:T(8,128)S(1)}, f32[80,256]{1,0:T(8,128)S(1)}, u32[]{:S(2)}, u32[]{:S(2)}) %collective-permute-start.6) | collective-permute-done | bytes 81952 | tf_op jit(solution)/shard_map/ppermute | solution.py:309
  33.2 1.0 %solve.1 = (f32[2,320,256]{2,1,0:T(8,128)}, f32[320,256]{1,0:T(8,128)S(1)}, f32[2,80,128]{2,1,0:T(8,128)S(1)}, f32[2,80,128]{2,1,0:T(8,128)S(1)}) custom-call(f32[80,256]{1,0:T(8,128)S(1)} %get-tuple-element.21.refs_0_, f32[80,256]{1,0:T(8,128)S(1)} %collective-permute-done.5.refs_1_, f32[80,256]{1,0:T(8,128)S(1)} %collective-permute-done.6.refs_2_, ...), custom_call_target="tpu_custom_call" | custom-call | bytes 2457600 | tf_op jit(solution)/shard_map/solve/pallas_call | solution.py:288
  34.2 3.4 %collective-permute-start.8 = (f32[2,80,128]{2,1,0:T(8,128)S(1)}, f32[2,80,128]{2,1,0:T(8,128)S(1)}, u32[]{:S(2)}, u32[]{:S(2)}) collective-permute-start(f32[2,80,128]{2,1,0:T(8,128)S(1)} %get-tuple-element.16), channel_id=1, source_target_pairs={{0,1},{1,2},{2,3},{4,5},{5,6},{6,7},{8,9},{9,10},{10,11},{12,13},{... | collective-permute-start | bytes 245768 | tf_op jit(solution)/shard_map/ppermute | solution.py:302
  37.6 1.9 %collective-permute-start.9 = (f32[2,80,128]{2,1,0:T(8,128)S(1)}, f32[2,80,128]{2,1,0:T(8,128)S(1)}, u32[]{:S(2)}, u32[]{:S(2)}) collective-permute-start(f32[2,80,128]{2,1,0:T(8,128)S(1)} %get-tuple-element.17), channel_id=1, source_target_pairs={{1,0},{2,1},{3,2},{5,4},{6,5},{7,6},{9,8},{10,9},{11,10},{13,12},{... | collective-permute-start | bytes 245768 | tf_op jit(solution)/shard_map/ppermute | solution.py:303
  39.6 0.0 copy-start.6
  39.6 1.1 %copy-done.6 = f32[2,320,256]{2,1,0:T(8,128)S(1)} copy-done((f32[2,320,256]{2,1,0:T(8,128)S(1)}, f32[2,320,256]{2,1,0:T(8,128)}, u32[]{:S(2)}) %copy-start.6) | copy-done | bytes 655384
  40.7 2.4 %second.1.part_ref = f32[2,320,256]{2,1,0:T(8,128)S(1)} custom-call(f32[2,8]{1,0:T(2,128)S(1)} %copy-done.10, f32[2,320,256]{2,1,0:T(8,128)S(1)} %copy-done.6, f32[320,256]{1,0:T(8,128)S(1)} %get-tuple-element.15.before_ref, bf16[320,256]{1,0:T(8,128)(2,1)S(1)} %copy-done.4, bf16[320,256]{1,0:T(8,128)(2,1)S(1)} %copy-done.5, bf16[320,320]{1,0:T(8,128)(2,1)S(1)} %copy-done.3, ...), custom_call_target="tpu_custom_call" | custom-call | flops 524288000 | bytes 2496576 | tf_op jit(solution)/shard_map/second/pallas_call | solution.py:288
  43.0 0.4 collective-permute-done.9.right_ref
  43.4 1.3 %finish.1 = bf16[2,320,256]{2,1,0:T(8,128)(2,1)} custom-call(f32[2,320,256]{2,1,0:T(8,128)S(1)} %second.1.part_ref, f32[2,80,128]{2,1,0:T(8,128)S(1)} %collective-permute-done.8.left_ref, f32[2,80,128]{2,1,0:T(8,128)S(1)} %collective-permute-done.9.right_ref, bf16[6,320,80]{2,1,0:T(8,128)(2,1)S(1)} %copy.12.lifts_ref, s32[6,256]{1,0:T(8,128)S(1)} %copy-done.7, ...), custom_call_target="tpu_custom_call" | custom-call | bytes 1472512 | tf_op jit(solution)/shard_map/finish/pallas_call | solution.py:288
  (19 shorter events, 0.1 us)
Async XLA Ops:
  0.6 1.1 %copy-start.1 = (f32[2,320,256]{2,1,0:T(8,128)S(1)}, f32[2,320,256]{2,1,0:T(8,128)}, u32[]{:S(2)}) copy-start(f32[2,320,256]{2,1,0:T(8,128)} %state_ref.3) | copy-start | bytes 1966084
  1.7 8.1 %copy-start.2 = (f32[2,320,256]{2,1,0:T(8,128)S(1)}, f32[2,320,256]{2,1,0:T(8,128)}, u32[]{:S(2)}) copy-start(f32[2,320,256]{2,1,0:T(8,128)} %state_ref.3) | copy-start | bytes 1966084
  1.7 8.1 %copy-start.9 = (s32[6,256]{1,0:T(8,128)S(1)}, s32[6,256]{1,0:T(8,128)}, u32[]{:S(2)}) copy-start(s32[6,256]{1,0:T(8,128)} %codes_ref.7) | copy-start | bytes 18436
  1.7 10.5 %collective-permute-start = (f32[2,80,128]{2,1,0:T(8,128)S(1)}, f32[2,80,128]{2,1,0:T(8,128)S(1)}, u32[]{:S(2)}, u32[]{:S(2)}) collective-permute-start(f32[2,80,128]{2,1,0:T(8,128)S(1)} %get-tuple-element.10), channel_id=1, source_target_pairs={{0,1},{1,2},{2,3},{4,5},{5,6},{6,7},{8,9},{9,10},{10,11},{12,13},{... | collective-permute-start | bytes 245768 | tf_op jit(solution)/shard_map/ppermute | solution.py:302
  6.4 5.8 %collective-permute-start.1 = (f32[2,80,128]{2,1,0:T(8,128)S(1)}, f32[2,80,128]{2,1,0:T(8,128)S(1)}, u32[]{:S(2)}, u32[]{:S(2)}) collective-permute-start(f32[2,80,128]{2,1,0:T(8,128)S(1)} %get-tuple-element.11), channel_id=1, source_target_pairs={{1,0},{2,1},{3,2},{5,4},{6,5},{7,6},{9,8},{10,9},{11,10},{13,12},{... | collective-permute-start | bytes 245768 | tf_op jit(solution)/shard_map/ppermute | solution.py:303
  8.3 1.5 %copy-start.7 = (s32[6,256]{1,0:T(8,128)S(1)}, s32[6,256]{1,0:T(8,128)}, u32[]{:S(2)}) copy-start(s32[6,256]{1,0:T(8,128)} %neighbor_ref.7) | copy-start | bytes 18436
  8.3 1.5 %copy-start.8 = (s32[6,256]{1,0:T(8,128)S(1)}, s32[6,256]{1,0:T(8,128)}, u32[]{:S(2)}) copy-start(s32[6,256]{1,0:T(8,128)} %tags_ref.7) | copy-start | bytes 18436
  8.3 1.5 %copy-start.10 = (f32[2,8]{1,0:T(2,128)S(1)}, f32[2,8]{1,0:T(2,128)}, u32[]{:S(2)}) copy-start(f32[2,8]{1,0:T(2,128)} %constant.41.clone.waves_ref) | copy-start | bytes 196
  8.4 1.5 %copy-start.5 = (bf16[320,256]{1,0:T(8,128)(2,1)S(1)}, bf16[320,256]{1,0:T(8,128)(2,1)}, u32[]{:S(2)}) copy-start(bf16[320,256]{1,0:T(8,128)(2,1)} %sin_ref.3) | copy-start | bytes 491524
  8.4 1.4 %copy-start = (f32[320,256]{1,0:T(8,128)S(1)}, f32[320,256]{1,0:T(8,128)}, u32[]{:S(2)}) copy-start(f32[320,256]{1,0:T(8,128)} %refs_5_.1) | copy-start | bytes 983044
  8.4 1.4 %copy-start.3 = (bf16[320,320]{1,0:T(8,128)(2,1)S(1)}, bf16[320,320]{1,0:T(8,128)(2,1)}, u32[]{:S(2)}) copy-start(bf16[320,320]{1,0:T(8,128)(2,1)} %volume_ref.3) | copy-start | bytes 614404
  8.4 1.4 %copy-start.4 = (bf16[320,256]{1,0:T(8,128)(2,1)S(1)}, bf16[320,256]{1,0:T(8,128)(2,1)}, u32[]{:S(2)}) copy-start(bf16[320,256]{1,0:T(8,128)(2,1)} %cos_ref.3) | copy-start | bytes 491524
  12.8 5.8 %collective-permute-start.2 = (f32[80,256]{1,0:T(8,128)S(1)}, f32[80,256]{1,0:T(8,128)S(1)}, u32[]{:S(2)}, u32[]{:S(2)}) collective-permute-start(f32[80,256]{1,0:T(8,128)S(1)} %get-tuple-element.22), channel_id=1, source_target_pairs={{0,4},{4,8},{8,12},{12,0},{1,5},{5,9},{9,13},{13,1},{2,6},{6,10},{... | collective-permute-start | bytes 245768 | tf_op jit(solution)/shard_map/ppermute | solution.py:309
  14.1 5.4 %collective-permute-start.4 = (f32[80,256]{1,0:T(8,128)S(1)}, f32[80,256]{1,0:T(8,128)S(1)}, u32[]{:S(2)}, u32[]{:S(2)}) collective-permute-start(f32[80,256]{1,0:T(8,128)S(1)} %get-tuple-element.23), channel_id=1, source_target_pairs={{0,12},{4,0},{8,4},{12,8},{1,13},{5,1},{9,5},{13,9},{2,14},{6,2},{... | collective-permute-start | bytes 245768 | tf_op jit(solution)/shard_map/ppermute | solution.py:309
  16.2 6.3 %collective-permute-start.3 = (f32[80,256]{1,0:T(8,128)S(1)}, f32[80,256]{1,0:T(8,128)S(1)}, u32[]{:S(2)}, u32[]{:S(2)}) collective-permute-start(f32[80,256]{1,0:T(8,128)S(1)} %get-tuple-element.24), channel_id=1, source_target_pairs={{0,8},{4,12},{8,0},{12,4},{1,9},{5,13},{9,1},{13,5},{2,10},{6,14},... | collective-permute-start | bytes 245768 | tf_op jit(solution)/shard_map/ppermute | solution.py:309
  22.6 4.1 %collective-permute-start.7 = (f32[80,256]{1,0:T(8,128)S(1)}, f32[80,256]{1,0:T(8,128)S(1)}, u32[]{:S(2)}, u32[]{:S(2)}) collective-permute-start(f32[80,256]{1,0:T(8,128)S(1)} %get-tuple-element.18), channel_id=1, source_target_pairs={{0,12},{4,0},{8,4},{12,8},{1,13},{5,1},{9,5},{13,9},{2,14},{6,2},{... | collective-permute-start | bytes 245768 | tf_op jit(solution)/shard_map/ppermute | solution.py:309
  25.0 8.2 %collective-permute-start.6 = (f32[80,256]{1,0:T(8,128)S(1)}, f32[80,256]{1,0:T(8,128)S(1)}, u32[]{:S(2)}, u32[]{:S(2)}) collective-permute-start(f32[80,256]{1,0:T(8,128)S(1)} %get-tuple-element.19), channel_id=1, source_target_pairs={{0,8},{4,12},{8,0},{12,4},{1,9},{5,13},{9,1},{13,5},{2,10},{6,14},... | collective-permute-start | bytes 245768 | tf_op jit(solution)/shard_map/ppermute | solution.py:309
  25.0 8.2 %collective-permute-start.5 = (f32[80,256]{1,0:T(8,128)S(1)}, f32[80,256]{1,0:T(8,128)S(1)}, u32[]{:S(2)}, u32[]{:S(2)}) collective-permute-start(f32[80,256]{1,0:T(8,128)S(1)} %get-tuple-element.20), channel_id=1, source_target_pairs={{0,4},{4,8},{8,12},{12,0},{1,5},{5,9},{9,13},{13,1},{2,6},{6,10},{... | collective-permute-start | bytes 245768 | tf_op jit(solution)/shard_map/ppermute | solution.py:309
  34.2 8.8 %collective-permute-start.8 = (f32[2,80,128]{2,1,0:T(8,128)S(1)}, f32[2,80,128]{2,1,0:T(8,128)S(1)}, u32[]{:S(2)}, u32[]{:S(2)}) collective-permute-start(f32[2,80,128]{2,1,0:T(8,128)S(1)} %get-tuple-element.16), channel_id=1, source_target_pairs={{0,1},{1,2},{2,3},{4,5},{5,6},{6,7},{8,9},{9,10},{10,11},{12,13},{... | collective-permute-start | bytes 245768 | tf_op jit(solution)/shard_map/ppermute | solution.py:302
  37.6 5.8 %collective-permute-start.9 = (f32[2,80,128]{2,1,0:T(8,128)S(1)}, f32[2,80,128]{2,1,0:T(8,128)S(1)}, u32[]{:S(2)}, u32[]{:S(2)}) collective-permute-start(f32[2,80,128]{2,1,0:T(8,128)S(1)} %get-tuple-element.17), channel_id=1, source_target_pairs={{1,0},{2,1},{3,2},{5,4},{6,5},{7,6},{9,8},{10,9},{11,10},{13,12},{... | collective-permute-start | bytes 245768 | tf_op jit(solution)/shard_map/ppermute | solution.py:303
  39.6 1.1 %copy-start.6 = (f32[2,320,256]{2,1,0:T(8,128)S(1)}, f32[2,320,256]{2,1,0:T(8,128)}, u32[]{:S(2)}) copy-start(f32[2,320,256]{2,1,0:T(8,128)} %get-tuple-element.8.state_ref) | copy-start | bytes 1966084

commit v2 on v1

--- a/solution.py
+++ b/solution.py
@@ -74,13 +74,11 @@
     return jnp.take_along_axis(value, lane_index(row), axis=1, mode="promise_in_bounds")
 
 
-def operator(state, blocks, stack, weights, volume_ref, lifts_ref, neighbor_ref, tags_ref, codes_ref):
+def operator(state, blocks, stack, weights_ref, neighbor_ref, tags_ref, codes_ref):
     slices, rows, columns = state.shape
     count = columns // LANES
     wide = slices * columns
-    weights[:, 0:rows] = volume_ref[...]
-    for face in range(6):
-        weights[:, rows + FACE * face : rows + FACE * (face + 1)] = lifts_ref[face]
+    base = 6 * FACE
     lane = lax.broadcasted_iota(jnp.int32, (FACE, LANES), 1)
     for item in range(slices):
         for block in range(count):
@@ -88,8 +86,8 @@
             value = state[item, :, block * LANES : (block + 1) * LANES]
             blocks[n] = value
             high, low = split(value)
-            stack[0:rows, n * LANES : (n + 1) * LANES] = high
-            stack[0:rows, wide + n * LANES : wide + (n + 1) * LANES] = low
+            stack[base:, n * LANES : (n + 1) * LANES] = high
+            stack[base:, wide + n * LANES : wide + (n + 1) * LANES] = low
     for item in range(slices):
         cubes = []
         turned = []
@@ -138,44 +136,75 @@
                     inner.append(own * (flip if field == axis else keep))
                 seen = jnp.where(kind == 0, taken, jnp.concatenate(inner, axis=0))
                 high, low = split(seen)
-                place = rows + FACE * face
+                place = FACE * face
                 stack[place : place + FACE, n * LANES : (n + 1) * LANES] = high
                 stack[place : place + FACE, wide + n * LANES : wide + (n + 1) * LANES] = low
-    image = jnp.dot(weights[...], stack[:, 0:wide], preferred_element_type=jnp.float32)
-    return image + jnp.dot(weights[...], stack[:, wide:], preferred_element_type=jnp.float32)
-
-
-def rim(left, right, lifts_ref, neighbor_ref, tags_ref, codes_ref, count):
-    slices = left.shape[0]
+    image = jnp.dot(weights_ref[...], stack[:, 0:wide], preferred_element_type=jnp.float32)
+    return image + jnp.dot(
+        weights_ref[...], stack[:, wide:], preferred_element_type=jnp.float32
+    )
+
+
+def even_place():
+    return (lax.axis_index("space") & 1) == 0
+
+
+def rim(near, far, slices, rim_weights_ref, neighbor_ref, tags_ref, codes_ref, count):
     lane = lax.broadcasted_iota(jnp.int32, (1, LANES), 1)
+    even = even_place()
     result = []
-    for face, halo in ((0, left), (1, right)):
+    for face in range(2):
         block = 0 if face == 0 else count - 1
         span = slice(block * LANES, (block + 1) * LANES)
-        target = (neighbor_ref[face : face + 1, span] + HALF) & (LANES - 1)
+        target = neighbor_ref[face : face + 1, span] & (HALF - 1)
         inside = lane < HALF if face == 0 else lane >= HALF
         use = (tags_ref[face : face + 1, span] == 0) & inside
         plan = orientation(codes_ref[face : face + 1, span])
         pieces = []
         for item in range(slices):
-            shifted = pltpu.roll(halo[item], HALF, axis=1)
-            seen = jnp.where(use, oriented(gather_lanes(shifted, target), plan), 0.0)
-            pieces.append(split(seen))
+            a, b = (far, near) if face == 0 else (near, far)
+            halo = jnp.where(even, a[item // 2], b[item // 2])
+            taken = gather_lanes(halo, target + HALF * (item % 2))
+            pieces.append(split(jnp.where(use, oriented(taken, plan), 0.0)))
         both = jnp.concatenate([p[0] for p in pieces] + [p[1] for p in pieces], axis=1)
-        product = jnp.dot(lifts_ref[face], both, preferred_element_type=jnp.float32)
+        product = jnp.dot(rim_weights_ref[face], both, preferred_element_type=jnp.float32)
         wide = slices * LANES
         result.append(product[:, :wide] + product[:, wide:])
     return result
 
 
-def send_kernel(state_ref, left_ref, right_ref):
-    slices, rows, columns = state_ref.shape
-    for item in range(slices):
-        for field in range(NF):
-            at = field * 64
-            to = slice(field * 16, field * 16 + 16)
-            left_ref[item, to, :] = state_ref[item, at : at + 16, 0:LANES]
-            right_ref[item, to, :] = state_ref[item, at + 48 : at + 64, columns - LANES :]
+def send(low, high, near_ref, far_ref):
+    slices = len(low)
+    lane = lax.broadcasted_iota(jnp.int32, (FACE, LANES), 1)
+    even = even_place()
+    for item in range(0, slices, 2):
+        other = min(item + 1, slices - 1)
+        first = jnp.where(lane < HALF, low[item], pltpu.roll(low[other], HALF, axis=1))
+        last = jnp.where(lane < HALF, pltpu.roll(high[item], HALF, axis=1), high[other])
+        near_ref[item // 2] = jnp.where(even, last, first)
+        far_ref[item // 2] = jnp.where(even, first, last)
+
+
+def ends_kernel(state_ref, near_ref, far_ref, low, high, semaphore):
+    slices, _, _, columns = state_ref.shape
+    copies = [
+        pltpu.make_async_copy(
+            state_ref.at[:, :, pl.ds(0, 16), pl.ds(0, LANES)], low, semaphore.at[0]
+        ),
+        pltpu.make_async_copy(
+            state_ref.at[:, :, pl.ds(48, 16), pl.ds(columns - LANES, LANES)], high, semaphore.at[1]
+        ),
+    ]
+    for copy in copies:
+        copy.start()
+    for copy in copies:
+        copy.wait()
+    send(
+        [low[item].reshape(FACE, LANES) for item in range(slices)],
+        [high[item].reshape(FACE, LANES) for item in range(slices)],
+        near_ref,
+        far_ref,
+    )
 
 
 def forcing_of(waves_ref, item, slices, cos_ref, sin_ref):
@@ -187,11 +216,18 @@
 
 def first_kernel(
     waves_ref, state_ref, cos_ref, sin_ref, damping_ref, volume_ref, lifts_ref, neighbor_ref,
-    tags_ref, codes_ref, out_ref, blocks, stack, weights,
+    tags_ref, codes_ref, out_ref, weights_ref, rim_weights_ref, rate_ref, blocks, stack,
 ):
     slices, _, columns = state_ref.shape
+    for face in range(6):
+        lift = lifts_ref[face].T
+        weights_ref[:, FACE * face : FACE * (face + 1)] = lift
+        if face < 2:
+            rim_weights_ref[face] = lift
+    weights_ref[:, 6 * FACE :] = volume_ref[...]
+    rate_ref[...] = 1.0 / (1.0 + damping_ref[...])
     image = operator(
-        state_ref, blocks, stack, weights, volume_ref, lifts_ref, neighbor_ref, tags_ref, codes_ref
+        state_ref, blocks, stack, weights_ref, neighbor_ref, tags_ref, codes_ref
     )
     for item in range(slices):
         forcing = forcing_of(waves_ref, item, slices, cos_ref, sin_ref)
@@ -203,15 +239,17 @@
 
 
 def carry_kernel(
-    part_ref, left_ref, right_ref, damping_ref, lifts_ref, neighbor_ref, tags_ref, codes_ref,
+    part_ref, near_ref, far_ref, rate_ref, rim_weights_ref, neighbor_ref, tags_ref, codes_ref,
     out_ref, carry_ref,
 ):
     slices, _, columns = part_ref.shape
     count = columns // LANES
-    low, high = rim(left_ref, right_ref, lifts_ref, neighbor_ref, tags_ref, codes_ref, count)
+    low, high = rim(
+        near_ref, far_ref, slices, rim_weights_ref, neighbor_ref, tags_ref, codes_ref, count
+    )
     for block in range(count):
         span = slice(block * LANES, (block + 1) * LANES)
-        rate = 1.0 / (1.0 + damping_ref[:, span])
+        rate = rate_ref[:, span]
         carry = None
         for item in range(slices):
             value = part_ref[item, :, span]
@@ -227,7 +265,7 @@
 
 def solve_kernel(pieces, *refs):
     piece_refs = refs[:pieces]
-    right_ref, damping_ref, state_ref, before_ref, low_ref, high_ref = refs[pieces:]
+    right_ref, rate_ref, state_ref, before_ref, near_ref, far_ref = refs[pieces:]
     slices, rows, columns = right_ref.shape
     if pieces == 1:
         before_ref[...] = piece_refs[0][...]
@@ -237,21 +275,28 @@
         for step in range(pieces):
             owner = lax.rem(me + pieces - step, pieces)
             before_ref[pl.ds(pl.multiple_of(owner * share, 8), share), :] = piece_refs[step][...]
-    rate = 1.0 / (1.0 + damping_ref[...])
+    rate = rate_ref[...]
     value = before_ref[...]
+    low = []
+    high = []
     for item in range(slices):
         value = rate * (value + right_ref[item])
         state_ref[item] = value
-    send_kernel(state_ref, low_ref, high_ref)
+        cube = value.reshape(NF, NP**3, columns)
+        low.append(cube[:, 0:16, 0:LANES].reshape(FACE, LANES))
+        high.append(cube[:, 48:64, columns - LANES :].reshape(FACE, LANES))
+    send(low, high, near_ref, far_ref)
 
 
 def second_kernel(
-    waves_ref, state_ref, before_ref, cos_ref, sin_ref, volume_ref, lifts_ref, neighbor_ref,
-    tags_ref, codes_ref, out_ref, blocks, stack, weights,
+    waves_ref, state_ref, before_ref, cos_ref, sin_ref, weights_ref, neighbor_ref, tags_ref,
+    codes_ref, out_ref, result_ref, blocks, stack, semaphore,
 ):
     slices, _, columns = state_ref.shape
+    copy = pltpu.make_async_copy(state_ref, result_ref, semaphore)
+    copy.start()
     image = operator(
-        state_ref, blocks, stack, weights, volume_ref, lifts_ref, neighbor_ref, tags_ref, codes_ref
+        state_ref, blocks, stack, weights_ref, neighbor_ref, tags_ref, codes_ref
     )
     for item in range(slices):
         forcing = forcing_of(waves_ref, item, slices, cos_ref, sin_ref)
@@ -261,14 +306,17 @@
             + forcing
             + (previous - state_ref[item])
         )
+    copy.wait()
 
 
 def finish_kernel(
-    part_ref, left_ref, right_ref, lifts_ref, neighbor_ref, tags_ref, codes_ref, out_ref
+    part_ref, near_ref, far_ref, rim_weights_ref, neighbor_ref, tags_ref, codes_ref, out_ref
 ):
     slices, _, columns = part_ref.shape
     count = columns // LANES
-    low, high = rim(left_ref, right_ref, lifts_ref, neighbor_ref, tags_ref, codes_ref, count)
+    low, high = rim(
+        near_ref, far_ref, slices, rim_weights_ref, neighbor_ref, tags_ref, codes_ref, count
+    )
     for block in range(count):
         span = slice(block * LANES, (block + 1) * LANES)
         for item in range(slices):
@@ -281,27 +329,32 @@
             out_ref[item, :, span] = value.astype(out_ref.dtype)
 
 
-def call(kernel, name, outs, args, scratch=(), scalars=0, flops=0):
-    vmem = pl.BlockSpec(memory_space=pltpu.VMEM)
-    smem = pl.BlockSpec(memory_space=pltpu.SMEM)
+VMEM = pl.BlockSpec(memory_space=pltpu.VMEM)
+SMEM = pl.BlockSpec(memory_space=pltpu.SMEM)
+HBM = pl.BlockSpec(memory_space=pltpu.HBM)
+
+
+def call(kernel, name, outs, args, scratch=(), flops=0, in_specs=None, out_specs=None):
     size = sum(math.prod(a.shape) * a.dtype.itemsize for a in list(args) + list(outs))
     return pl.pallas_call(
         kernel,
         name=name,
         out_shape=outs,
-        in_specs=[smem] * scalars + [vmem] * (len(args) - scalars),
-        out_specs=[vmem] * len(outs),
+        in_specs=in_specs or [VMEM] * len(args),
+        out_specs=out_specs or [VMEM] * len(outs),
         scratch_shapes=list(scratch),
         compiler_params=pltpu.CompilerParams(vmem_limit_bytes=40 * 2**20),
         cost_estimate=pl.CostEstimate(flops=flops, bytes_accessed=size, transcendentals=0),
     )(*args)
 
 
-def halos(low, high):
+def exchange(near, far):
     count = lax.axis_size("space")
-    left = lax.ppermute(high, "space", [(i, i + 1) for i in range(count - 1)])
-    right = lax.ppermute(low, "space", [(i + 1, i) for i in range(count - 1)])
-    return left, right
+    inner = [(i, i + 1) for i in range(0, count - 1, 2)]
+    outer = [(i, i + 1) for i in range(1, count - 1, 2)]
+    near = lax.ppermute(near, "space", inner + [(j, i) for i, j in inner])
+    far = lax.ppermute(far, "space", outer + [(j, i) for i, j in outer])
+    return near, far
 
 
 def turned(value, distance):
@@ -352,45 +405,55 @@
     total = slices * lax.axis_size("tm")
     angles = 2.0 * np.pi * np.arange(total) / total
     waves = jnp.asarray(np.stack([np.cos(angles), np.sin(angles)]).astype(np.float32))
-    f32 = jnp.float32
-    whole = jax.ShapeDtypeStruct((slices, rows, columns), f32)
-    plane = jax.ShapeDtypeStruct((rows, columns), f32)
-    rimmed = jax.ShapeDtypeStruct((slices, FACE, LANES), f32)
-    tables = (lifts, neighbor, tags, codes)
+    f32, bf16 = jnp.float32, jnp.bfloat16
+    shape = jax.ShapeDtypeStruct
+    whole = shape((slices, rows, columns), f32)
+    plane = shape((rows, columns), f32)
+    packed = shape(((slices + 1) // 2, FACE, LANES), f32)
+    tables = (neighbor, tags, codes)
     depth = rows + 6 * FACE
-    scratch = (
+    scratch = [
         pltpu.VMEM((slices * columns // LANES, rows, LANES), f32),
-        pltpu.VMEM((depth, 2 * slices * columns), jnp.bfloat16),
-        pltpu.VMEM((rows, depth), jnp.bfloat16),
-    )
+        pltpu.VMEM((depth, 2 * slices * columns), bf16),
+    ]
     work = 4 * rows * depth * slices * columns
-
-    low, high = call(send_kernel, "ends", [rimmed] * 2, [guess])
-    left, right = halos(low, high)
-    (part,) = call(
-        first_kernel, "first", [whole],
-        [waves, guess, source_cos, source_sin, damping, volume, *tables],
-        scratch, scalars=1, flops=work,
+    end = pltpu.VMEM((slices, NF, NP * NP, LANES), f32)
+
+    near, far = call(
+        ends_kernel, "ends", [packed] * 2,
+        [guess.reshape(slices, NF, NP**3, columns)],
+        [end, end, pltpu.SemaphoreType.DMA((2,))], in_specs=[HBM],
+    )
+    near, far = exchange(near, far)
+    part, weights, rim_weights, rate = call(
+        first_kernel, "first",
+        [whole, shape((rows, depth), bf16), shape((2, rows, FACE), bf16), plane],
+        [
+            waves, guess, source_cos, source_sin, damping, volume, jnp.swapaxes(lifts, 1, 2),
+            *tables,
+        ],
+        scratch, flops=work, in_specs=[SMEM] + [VMEM] * 9,
     )
     known, carry = call(
-        carry_kernel, "carry", [whole, plane], [part, left, right, damping, *tables]
+        carry_kernel, "carry", [whole, plane], [part, near, far, rate, rim_weights, *tables]
     )
     pieces = around(carry, damping, slices)
-    state, before, low, high = call(
+    state, before, near, far = call(
         functools.partial(solve_kernel, len(pieces)), "solve",
-        [whole, plane, rimmed, rimmed], [*pieces, known, damping],
-    )
-    left, right = halos(low, high)
-    (part,) = call(
-        second_kernel, "second", [whole],
-        [waves, state, before, source_cos, source_sin, volume, *tables],
-        scratch, scalars=1, flops=work,
+        [whole, plane, packed, packed], [*pieces, known, rate],
+    )
+    near, far = exchange(near, far)
+    part, result = call(
+        second_kernel, "second", [whole, whole],
+        [waves, state, before, source_cos, source_sin, weights, *tables],
+        [*scratch, pltpu.SemaphoreType.DMA], flops=work,
+        in_specs=[SMEM] + [VMEM] * 8, out_specs=[VMEM, HBM],
     )
     (after,) = call(
-        finish_kernel, "finish", [jax.ShapeDtypeStruct(whole.shape, jnp.bfloat16)],
-        [part, left, right, *tables],
-    )
-    return state, after
+        finish_kernel, "finish", [shape(whole.shape, bf16)],
+        [part, near, far, rim_weights, *tables],
+    )
+    return result, after
 
 
 def solution(mesh):

time: 45 us -> 43.9 us (0.976)
  starting transfers between devices: 18.5 us -> 13.4 us
  local copies, waits for them, and re-layouts: 3.58 us -> 6.53 us
  other arithmetic: 0.07 us -> 0.96 us
    ppermute x4, starting transfers between devices: 11.9 us -> 7.04 us  [the longest x2 6.37 us: exchange(): far = lax.ppermute(far, 'space', outer + [(j, i) for i, j in outer])]
    unnamed x23 -> x26, local copies, waits for them, and re-layouts: 3.55 us -> 6.51 us
    add x1, other arithmetic: 0.07 us -> 0.96 us  [periodic(): entering.append(carries[k] + factor * entering[-1])]
  transfers between devices with their start and end apart: 10 -> 10, of which waited for: 6 -> 5; matrix products, arithmetic and copies ran while one was open for 3% -> 0% of each run, Pallas kernels for 10% -> 13%
where the time goes in v2:
time: 43.9 us; the launch traced here: 43.4 us
  waiting for transfers between devices  14.3 us (33%)
  starting transfers between devices  13.4 us (31%)
  Pallas kernels  7.48 us (17%)
  local copies, waits for them, and re-layouts  6.53 us (15%)
  other arithmetic  0.96 us (2%)
  between operations  0.81 us (2%)
    ppermute x6, waiting for transfers between devices, turned(): lax.ppermute(value, 'tm', [(i, (i + distance) % count) for i in range(cou...  13.8 us
    pallas_call x6, Pallas kernels, call(): pl.pallas_call(kernel, name=name, out_shape=outs, in_specs=in_specs or [V...  7.48 us
    unnamed x26, local copies, waits for them, and re-layouts  6.51 us
    ppermute x2, starting transfers between devices, exchange(): far = lax.ppermute(far, 'space', outer + [(j, i) for i, j in outer])  6.37 us
    ppermute x6, starting transfers between devices, turned(): lax.ppermute(value, 'tm', [(i, (i + distance) % count) for i in range(cou...  6.35 us
    add x1, other arithmetic, periodic(): entering.append(carries[k] + factor * entering[-1])  0.96 us
  transfers between devices with their start and end apart: 10, of which 5 were waited for; matrix products, arithmetic and copies ran while one was open for 0% of the time, Pallas kernels for 13%

profile of v2, /device:TPU:1, one launch (start us, length us, event | category | flops | bytes accessed | tf_op | source)
XLA Modules:
  0.0 43.4 jit_solution(7982631918190519209)
XLA Ops:
  0.6 1.1 %copy-done = f32[2,320,256]{2,1,0:T(8,128)S(1)} copy-done((f32[2,320,256]{2,1,0:T(8,128)S(1)}, f32[2,320,256]{2,1,0:T(8,128)}, u32[]{:S(2)}) %copy-start) | copy-done | bytes 655384
  1.7 0.1 ends.1
  1.8 0.1 collective-permute-start
  2.0 4.5 %collective-permute-start.1 = (f32[1,80,128]{2,1,0:T(8,128)S(1)}, f32[1,80,128]{2,1,0:T(8,128)S(1)}, u32[]{:S(2)}, u32[]{:S(2)}) collective-permute-start(f32[1,80,128]{2,1,0:T(8,128)S(1)} %get-tuple-element.18), channel_id=1, source_target_pairs={{1,2},{2,1},{5,6},{6,5},{9,10},{10,9},{13,14},{14,13},{17,18},{18,... | collective-permute-start | bytes 122888 | tf_op jit(solution)/shard_map/ppermute | solution.py:356
  6.5 0.0 copy-start.11
  6.5 0.0 copy-start.12
  6.5 0.6 %copy-done.11 = s32[6,256]{1,0:T(8,128)S(1)} copy-done((s32[6,256]{1,0:T(8,128)S(1)}, s32[6,256]{1,0:T(8,128)}, u32[]{:S(2)}) %copy-start.11) | copy-done | bytes 6168
  7.2 0.0 copy-done.10
  7.2 0.0 copy-done.9
  7.2 1.0 %copy-done.2 = f32[320,256]{1,0:T(8,128)S(1)} copy-done((f32[320,256]{1,0:T(8,128)S(1)}, f32[320,256]{1,0:T(8,128)}, u32[]{:S(2)}) %copy-start.2) | copy-done | bytes 327704
  8.2 1.0 %copy-done.3 = bf16[6,320,80]{1,2,0:T(8,128)(2,1)S(1)} copy-done((bf16[6,320,80]{1,2,0:T(8,128)(2,1)S(1)}, bf16[6,320,80]{1,2,0:T(8,128)(2,1)}, u32[]{:S(2)}) %copy-start.3) | copy-done | bytes 307224
  9.2 0.9 %copy-done.4 = bf16[320,320]{1,0:T(8,128)(2,1)S(1)} copy-done((bf16[320,320]{1,0:T(8,128)(2,1)S(1)}, bf16[320,320]{1,0:T(8,128)(2,1)}, u32[]{:S(2)}) %copy-start.4) | copy-done | bytes 204824
  10.1 0.9 %copy-done.5 = bf16[320,256]{1,0:T(8,128)(2,1)S(1)} copy-done((bf16[320,256]{1,0:T(8,128)(2,1)S(1)}, bf16[320,256]{1,0:T(8,128)(2,1)}, u32[]{:S(2)}) %copy-start.5) | copy-done | bytes 163864
  11.0 0.9 %copy-done.7 = bf16[320,256]{1,0:T(8,128)(2,1)S(1)} copy-done((bf16[320,256]{1,0:T(8,128)(2,1)S(1)}, bf16[320,256]{1,0:T(8,128)(2,1)}, u32[]{:S(2)}) %copy-start.7) | copy-done | bytes 163864
  11.9 2.5 %first.1 = (f32[2,320,256]{2,1,0:T(8,128)S(1)}, bf16[320,800]{1,0:T(8,128)(2,1)S(1)}, bf16[2,320,80]{2,1,0:T(8,128)(2,1)S(1)}, f32[320,256]{1,0:T(8,128)S(1)}) custom-call(f32[2,8]{1,0:T(2,128)S(1)} %copy-done.12, f32[2,320,256]{2,1,0:T(8,128)S(1)} %copy-done.1, bf16[320,256]{1,0:T(8,128)(2,1)S(1)} %copy-done.5, bf16[320,256]{1,0:T(8,128)(2,1)S(1)} %copy-done.7, ...), custom_call_target="tpu_custom_call" | custom-call | flops 524288000 | bytes 3438656 | tf_op jit(solution)/shard_map/first/pallas_call | solution.py:339
  14.5 0.5 %carry.1 = (f32[2,320,256]{2,1,0:T(8,128)S(1)}, f32[320,256]{1,0:T(8,128)S(1)}) custom-call(f32[2,320,256]{2,1,0:T(8,128)S(1)} %get-tuple-element.16.part_ref, f32[1,80,128]{2,1,0:T(8,128)S(1)} %collective-permute-done.near_ref, f32[1,80,128]{2,1,0:T(8,128)S(1)} %collective-permute-done.1.far_ref, f32[320,256]{1,0:T(8,128)S(1)} %get-tuple-element.19.rate_ref.refs_5_, ...), custom_call_target="tpu_custom_call" | custom-call | bytes 2168832 | tf_op jit(solution)/shard_map/carry/pallas_call | solution.py:339
  15.0 1.3 %collective-permute-start.2 = (f32[80,256]{1,0:T(8,128)S(1)}, f32[80,256]{1,0:T(8,128)S(1)}, u32[]{:S(2)}, u32[]{:S(2)}) collective-permute-start(f32[80,256]{1,0:T(8,128)S(1)} %get-tuple-element.34), channel_id=1, source_target_pairs={{0,4},{4,8},{8,12},{12,0},{1,5},{5,9},{9,13},{13,1},{2,6},{6,10},{... | collective-permute-start | bytes 245768 | tf_op jit(solution)/shard_map/ppermute | solution.py:362
  16.4 2.1 %collective-permute-start.4 = (f32[80,256]{1,0:T(8,128)S(1)}, f32[80,256]{1,0:T(8,128)S(1)}, u32[]{:S(2)}, u32[]{:S(2)}) collective-permute-start(f32[80,256]{1,0:T(8,128)S(1)} %get-tuple-element.35), channel_id=1, source_target_pairs={{0,12},{4,0},{8,4},{12,8},{1,13},{5,1},{9,5},{13,9},{2,14},{6,2},{... | collective-permute-start | bytes 245768 | tf_op jit(solution)/shard_map/ppermute | solution.py:362
  18.5 0.4 collective-permute-start.3
  18.9 2.4 %collective-permute-done.2 = f32[80,256]{1,0:T(8,128)S(1)} collective-permute-done((f32[80,256]{1,0:T(8,128)S(1)}, f32[80,256]{1,0:T(8,128)S(1)}, u32[]{:S(2)}, u32[]{:S(2)}) %collective-permute-start.2) | collective-permute-done | bytes 81952 | tf_op jit(solution)/shard_map/ppermute | solution.py:362
  21.2 3.6 %collective-permute-done.3 = f32[80,256]{1,0:T(8,128)S(1)} collective-permute-done((f32[80,256]{1,0:T(8,128)S(1)}, f32[80,256]{1,0:T(8,128)S(1)}, u32[]{:S(2)}, u32[]{:S(2)}) %collective-permute-start.3) | collective-permute-done | bytes 81952 | tf_op jit(solution)/shard_map/ppermute | solution.py:362
  24.8 1.0 %multiply_add_fusion = (f32[80,256]{1,0:T(8,128)S(1)}, f32[80,256]{1,0:T(8,128)S(1)}, f32[80,256]{1,0:T(8,128)S(1)}, f32[80,256]{1,0:T(8,128)S(1)}) fusion(f32[80,256]{1,0:T(8,128)S(1)} %collective-permute-done.3, f32[320,256]{1,0:T(8,128)} %damping_ref.1, s32[]{:T(128)S(6)} %select_n.17, f32[80,256]{1,0:T(8,128)S(1)} %collective-permute-done.4, ...), kind=kLoop, calls=%fused_computation.10 | loop fusion | flops 409600 | bytes 737288 | tf_op jit(solution)/shard_map/add | solution.py:375
  25.8 2.2 %collective-permute-start.7 = (f32[80,256]{1,0:T(8,128)S(1)}, f32[80,256]{1,0:T(8,128)S(1)}, u32[]{:S(2)}, u32[]{:S(2)}) collective-permute-start(f32[80,256]{1,0:T(8,128)S(1)} %get-tuple-element.30), channel_id=1, source_target_pairs={{0,12},{4,0},{8,4},{12,8},{1,13},{5,1},{9,5},{13,9},{2,14},{6,2},{... | collective-permute-start | bytes 245768 | tf_op jit(solution)/shard_map/ppermute | solution.py:362
  28.0 0.4 collective-permute-start.5
  28.3 1.6 %collective-permute-done.7.refs_3_ = f32[80,256]{1,0:T(8,128)S(1)} collective-permute-done((f32[80,256]{1,0:T(8,128)S(1)}, f32[80,256]{1,0:T(8,128)S(1)}, u32[]{:S(2)}, u32[]{:S(2)}) %collective-permute-start.7) | collective-permute-done | bytes 81952 | tf_op jit(solution)/shard_map/ppermute | solution.py:362
  29.9 6.2 %collective-permute-done.6.refs_2_ = f32[80,256]{1,0:T(8,128)S(1)} collective-permute-done((f32[80,256]{1,0:T(8,128)S(1)}, f32[80,256]{1,0:T(8,128)S(1)}, u32[]{:S(2)}, u32[]{:S(2)}) %collective-permute-start.6) | collective-permute-done | bytes 81952 | tf_op jit(solution)/shard_map/ppermute | solution.py:362
  36.2 0.2 solve.1
  36.4 0.5 %collective-permute-start.8 = (f32[1,80,128]{2,1,0:T(8,128)S(1)}, f32[1,80,128]{2,1,0:T(8,128)S(1)}, u32[]{:S(2)}, u32[]{:S(2)}) collective-permute-start(f32[1,80,128]{2,1,0:T(8,128)S(1)} %get-tuple-element.28), channel_id=1, source_target_pairs={{0,1},{2,3},{1,0},{3,2},{4,5},{6,7},{5,4},{7,6},{8,9},{10,11},{9,8... | collective-permute-start | bytes 122888 | tf_op jit(solution)/shard_map/ppermute | solution.py:355
  36.9 1.9 %collective-permute-start.9 = (f32[1,80,128]{2,1,0:T(8,128)S(1)}, f32[1,80,128]{2,1,0:T(8,128)S(1)}, u32[]{:S(2)}, u32[]{:S(2)}) collective-permute-start(f32[1,80,128]{2,1,0:T(8,128)S(1)} %get-tuple-element.29), channel_id=1, source_target_pairs={{1,2},{2,1},{5,6},{6,5},{9,10},{10,9},{13,14},{14,13},{17,18},{18,... | collective-permute-start | bytes 122888 | tf_op jit(solution)/shard_map/ppermute | solution.py:356
  38.9 2.9 %second.1 = (f32[2,320,256]{2,1,0:T(8,128)S(1)}, f32[2,320,256]{2,1,0:T(8,128)}) custom-call(f32[2,8]{1,0:T(2,128)S(1)} %copy-done.12, f32[2,320,256]{2,1,0:T(8,128)S(1)} %get-tuple-element.23.state_ref, f32[320,256]{1,0:T(8,128)S(1)} %get-tuple-element.24.before_ref, bf16[320,256]{1,0:T(8,128)(2,1)S(1)} %copy-done.6, bf16[320,256]{1,0:T(8,128)(2,1)S(1)} %copy-done.8, ...), custom_call_target="tpu_custom_call" | custom-call | flops 524288000 | bytes 3151936 | tf_op jit(solution)/shard_map/second/pallas_call | solution.py:339
  41.8 0.5 %collective-permute-done.9.far_ref = f32[1,80,128]{2,1,0:T(8,128)S(1)} collective-permute-done((f32[1,80,128]{2,1,0:T(8,128)S(1)}, f32[1,80,128]{2,1,0:T(8,128)S(1)}, u32[]{:S(2)}, u32[]{:S(2)}) %collective-permute-start.9) | collective-permute-done | bytes 40992 | tf_op jit(solution)/shard_map/ppermute | solution.py:356
  42.2 1.2 %finish.1 = bf16[2,320,256]{2,1,0:T(8,128)(2,1)} custom-call(f32[2,320,256]{2,1,0:T(8,128)S(1)} %get-tuple-element.27.part_ref, f32[1,80,128]{2,1,0:T(8,128)S(1)} %collective-permute-done.8.near_ref, f32[1,80,128]{2,1,0:T(8,128)S(1)} %collective-permute-done.9.far_ref, bf16[2,320,80]{2,1,0:T(8,128)(2,1)S(1)} %get-tuple-element.20.rim_weights_ref, ...), custom_call_target="tpu_custom_call" | custom-call | bytes 1185792 | tf_op jit(solution)/shard_map/finish/pallas_call | solution.py:339
  (22 shorter events, 0.1 us)
Async XLA Ops:
  0.6 1.1 %copy-start = (f32[2,320,256]{2,1,0:T(8,128)S(1)}, f32[2,320,256]{2,1,0:T(8,128)}, u32[]{:S(2)}) copy-start(f32[2,320,256]{2,1,0:T(8,128)} %state_ref.1) | copy-start | bytes 1966084
  1.7 4.8 %copy-start.1 = (f32[2,320,256]{2,1,0:T(8,128)S(1)}, f32[2,320,256]{2,1,0:T(8,128)}, u32[]{:S(2)}) copy-start(f32[2,320,256]{2,1,0:T(8,128)} %state_ref.1) | copy-start | bytes 1966084
  1.8 12.6 %collective-permute-start = (f32[1,80,128]{2,1,0:T(8,128)S(1)}, f32[1,80,128]{2,1,0:T(8,128)S(1)}, u32[]{:S(2)}, u32[]{:S(2)}) collective-permute-start(f32[1,80,128]{2,1,0:T(8,128)S(1)} %get-tuple-element.17), channel_id=1, source_target_pairs={{0,1},{2,3},{1,0},{3,2},{4,5},{6,7},{5,4},{7,6},{8,9},{10,11},{9,8... | collective-permute-start | bytes 122888 | tf_op jit(solution)/shard_map/ppermute | solution.py:355
  2.0 12.5 %collective-permute-start.1 = (f32[1,80,128]{2,1,0:T(8,128)S(1)}, f32[1,80,128]{2,1,0:T(8,128)S(1)}, u32[]{:S(2)}, u32[]{:S(2)}) collective-permute-start(f32[1,80,128]{2,1,0:T(8,128)S(1)} %get-tuple-element.18), channel_id=1, source_target_pairs={{1,2},{2,1},{5,6},{6,5},{9,10},{10,9},{13,14},{14,13},{17,18},{18,... | collective-permute-start | bytes 122888 | tf_op jit(solution)/shard_map/ppermute | solution.py:356
  6.5 0.7 %copy-start.11 = (s32[6,256]{1,0:T(8,128)S(1)}, s32[6,256]{1,0:T(8,128)}, u32[]{:S(2)}) copy-start(s32[6,256]{1,0:T(8,128)} %codes_ref.7) | copy-start | bytes 18436
  6.5 0.7 %copy-start.10 = (s32[6,256]{1,0:T(8,128)S(1)}, s32[6,256]{1,0:T(8,128)}, u32[]{:S(2)}) copy-start(s32[6,256]{1,0:T(8,128)} %tags_ref.7) | copy-start | bytes 18436
  6.5 0.7 %copy-start.9 = (s32[6,256]{1,0:T(8,128)S(1)}, s32[6,256]{1,0:T(8,128)}, u32[]{:S(2)}) copy-start(s32[6,256]{1,0:T(8,128)} %neighbor_ref.7) | copy-start | bytes 18436
  6.5 0.7 %copy-start.12 = (f32[2,8]{1,0:T(2,128)S(1)}, f32[2,8]{1,0:T(2,128)}, u32[]{:S(2)}) copy-start(f32[2,8]{1,0:T(2,128)} %constant.41.clone.waves_ref) | copy-start | bytes 196
  7.2 1.0 %copy-start.2 = (f32[320,256]{1,0:T(8,128)S(1)}, f32[320,256]{1,0:T(8,128)}, u32[]{:S(2)}) copy-start(f32[320,256]{1,0:T(8,128)} %damping_ref.1) | copy-start | bytes 983044
  8.2 1.0 %copy-start.3 = (bf16[6,320,80]{1,2,0:T(8,128)(2,1)S(1)}, bf16[6,320,80]{1,2,0:T(8,128)(2,1)}, u32[]{:S(2)}) copy-start(bf16[6,320,80]{1,2,0:T(8,128)(2,1)} %param.15) | copy-start | bytes 921604
  9.2 0.9 %copy-start.4 = (bf16[320,320]{1,0:T(8,128)(2,1)S(1)}, bf16[320,320]{1,0:T(8,128)(2,1)}, u32[]{:S(2)}) copy-start(bf16[320,320]{1,0:T(8,128)(2,1)} %volume_ref.1) | copy-start | bytes 614404
  10.1 0.9 %copy-start.5 = (bf16[320,256]{1,0:T(8,128)(2,1)S(1)}, bf16[320,256]{1,0:T(8,128)(2,1)}, u32[]{:S(2)}) copy-start(bf16[320,256]{1,0:T(8,128)(2,1)} %cos_ref.3) | copy-start | bytes 491524
  11.0 0.9 %copy-start.7 = (bf16[320,256]{1,0:T(8,128)(2,1)S(1)}, bf16[320,256]{1,0:T(8,128)(2,1)}, u32[]{:S(2)}) copy-start(bf16[320,256]{1,0:T(8,128)(2,1)} %sin_ref.3) | copy-start | bytes 491524
  15.0 6.2 %collective-permute-start.2 = (f32[80,256]{1,0:T(8,128)S(1)}, f32[80,256]{1,0:T(8,128)S(1)}, u32[]{:S(2)}, u32[]{:S(2)}) collective-permute-start(f32[80,256]{1,0:T(8,128)S(1)} %get-tuple-element.34), channel_id=1, source_target_pairs={{0,4},{4,8},{8,12},{12,0},{1,5},{5,9},{9,13},{13,1},{2,6},{6,10},{... | collective-permute-start | bytes 245768 | tf_op jit(solution)/shard_map/ppermute | solution.py:362
  16.4 4.8 %collective-permute-start.4 = (f32[80,256]{1,0:T(8,128)S(1)}, f32[80,256]{1,0:T(8,128)S(1)}, u32[]{:S(2)}, u32[]{:S(2)}) collective-permute-start(f32[80,256]{1,0:T(8,128)S(1)} %get-tuple-element.35), channel_id=1, source_target_pairs={{0,12},{4,0},{8,4},{12,8},{1,13},{5,1},{9,5},{13,9},{2,14},{6,2},{... | collective-permute-start | bytes 245768 | tf_op jit(solution)/shard_map/ppermute | solution.py:362
  18.5 6.4 %collective-permute-start.3 = (f32[80,256]{1,0:T(8,128)S(1)}, f32[80,256]{1,0:T(8,128)S(1)}, u32[]{:S(2)}, u32[]{:S(2)}) collective-permute-start(f32[80,256]{1,0:T(8,128)S(1)} %get-tuple-element.36), channel_id=1, source_target_pairs={{0,8},{4,12},{8,0},{12,4},{1,9},{5,13},{9,1},{13,5},{2,10},{6,14},... | collective-permute-start | bytes 245768 | tf_op jit(solution)/shard_map/ppermute | solution.py:362
  25.8 4.1 %collective-permute-start.7 = (f32[80,256]{1,0:T(8,128)S(1)}, f32[80,256]{1,0:T(8,128)S(1)}, u32[]{:S(2)}, u32[]{:S(2)}) collective-permute-start(f32[80,256]{1,0:T(8,128)S(1)} %get-tuple-element.30), channel_id=1, source_target_pairs={{0,12},{4,0},{8,4},{12,8},{1,13},{5,1},{9,5},{13,9},{2,14},{6,2},{... | collective-permute-start | bytes 245768 | tf_op jit(solution)/shard_map/ppermute | solution.py:362
  28.0 8.2 %collective-permute-start.6 = (f32[80,256]{1,0:T(8,128)S(1)}, f32[80,256]{1,0:T(8,128)S(1)}, u32[]{:S(2)}, u32[]{:S(2)}) collective-permute-start(f32[80,256]{1,0:T(8,128)S(1)} %get-tuple-element.31), channel_id=1, source_target_pairs={{0,8},{4,12},{8,0},{12,4},{1,9},{5,13},{9,1},{13,5},{2,10},{6,14},... | collective-permute-start | bytes 245768 | tf_op jit(solution)/shard_map/ppermute | solution.py:362
  28.0 8.2 %collective-permute-start.5 = (f32[80,256]{1,0:T(8,128)S(1)}, f32[80,256]{1,0:T(8,128)S(1)}, u32[]{:S(2)}, u32[]{:S(2)}) collective-permute-start(f32[80,256]{1,0:T(8,128)S(1)} %get-tuple-element.32), channel_id=1, source_target_pairs={{0,4},{4,8},{8,12},{12,0},{1,5},{5,9},{9,13},{13,1},{2,6},{6,10},{... | collective-permute-start | bytes 245768 | tf_op jit(solution)/shard_map/ppermute | solution.py:362
  36.2 2.7 %copy-start.6 = (bf16[320,256]{1,0:T(8,128)(2,1)S(1)}, bf16[320,256]{1,0:T(8,128)(2,1)}, u32[]{:S(2)}) copy-start(bf16[320,256]{1,0:T(8,128)(2,1)} %cos_ref.3) | copy-start | bytes 491524
  36.2 2.7 %copy-start.8 = (bf16[320,256]{1,0:T(8,128)(2,1)S(1)}, bf16[320,256]{1,0:T(8,128)(2,1)}, u32[]{:S(2)}) copy-start(bf16[320,256]{1,0:T(8,128)(2,1)} %sin_ref.3) | copy-start | bytes 491524
  36.4 5.4 %collective-permute-start.8 = (f32[1,80,128]{2,1,0:T(8,128)S(1)}, f32[1,80,128]{2,1,0:T(8,128)S(1)}, u32[]{:S(2)}, u32[]{:S(2)}) collective-permute-start(f32[1,80,128]{2,1,0:T(8,128)S(1)} %get-tuple-element.28), channel_id=1, source_target_pairs={{0,1},{2,3},{1,0},{3,2},{4,5},{6,7},{5,4},{7,6},{8,9},{10,11},{9,8... | collective-permute-start | bytes 122888 | tf_op jit(solution)/shard_map/ppermute | solution.py:355
  36.9 5.3 %collective-permute-start.9 = (f32[1,80,128]{2,1,0:T(8,128)S(1)}, f32[1,80,128]{2,1,0:T(8,128)S(1)}, u32[]{:S(2)}, u32[]{:S(2)}) collective-permute-start(f32[1,80,128]{2,1,0:T(8,128)S(1)} %get-tuple-element.29), channel_id=1, source_target_pairs={{1,2},{2,1},{5,6},{6,5},{9,10},{10,9},{13,14},{14,13},{17,18},{18,... | collective-permute-start | bytes 122888 | tf_op jit(solution)/shard_map/ppermute | solution.py:356

commit v3 on v2

--- a/solution.py
+++ b/solution.py
@@ -3,7 +3,6 @@
 
 import jax
 import jax.numpy as jnp
-import numpy as np
 from jax import lax
 from jax.experimental import pallas as pl
 from jax.experimental.pallas import tpu as pltpu
@@ -74,7 +73,9 @@
     return jnp.take_along_axis(value, lane_index(row), axis=1, mode="promise_in_bounds")
 
 
-def operator(state, blocks, stack, weights_ref, neighbor_ref, tags_ref, codes_ref):
+def operator(
+    state, blocks, stack, weights_ref, neighbor_ref, tags_ref, codes_ref, ahead=lambda: None
+):
     slices, rows, columns = state.shape
     count = columns // LANES
     wide = slices * columns
@@ -139,6 +140,7 @@
                 place = FACE * face
                 stack[place : place + FACE, n * LANES : (n + 1) * LANES] = high
                 stack[place : place + FACE, wide + n * LANES : wide + (n + 1) * LANES] = low
+    ahead()
     image = jnp.dot(weights_ref[...], stack[:, 0:wide], preferred_element_type=jnp.float32)
     return image + jnp.dot(
         weights_ref[...], stack[:, wide:], preferred_element_type=jnp.float32
@@ -207,30 +209,53 @@
     )
 
 
-def forcing_of(waves_ref, item, slices, cos_ref, sin_ref):
-    at = lax.axis_index("tm") * slices + item
-    return waves_ref[0, at] * cos_ref[...].astype(jnp.float32) + waves_ref[1, at] * sin_ref[
-        ...
-    ].astype(jnp.float32)
-
-
-def first_kernel(
-    waves_ref, state_ref, cos_ref, sin_ref, damping_ref, volume_ref, lifts_ref, neighbor_ref,
-    tags_ref, codes_ref, out_ref, weights_ref, rim_weights_ref, rate_ref, blocks, stack,
-):
+def wave(at, values):
+    result = jnp.float32(values[0])
+    for k in range(1, len(values)):
+        result = jnp.where(at == k, jnp.float32(values[k]), result)
+    return result
+
+
+def first_kernel(total, *refs):
+    sources = refs[:9]
+    out_ref, weights_ref, rim_weights_ref, rate_ref, forcing_ref = refs[9:14]
+    neighbor_ref, tags_ref, codes_ref = refs[14:17]
+    state_ref, cos_ref, sin_ref, damping_ref, volume_ref, lifts_ref = refs[17:23]
+    blocks, stack, semaphores = refs[23:]
+    targets = (
+        state_ref, neighbor_ref, tags_ref, codes_ref, lifts_ref, volume_ref, damping_ref,
+        cos_ref, sin_ref,
+    )
+    copies = [
+        pltpu.make_async_copy(source, target, semaphores.at[k])
+        for k, (source, target) in enumerate(zip(sources, targets))
+    ]
+    for copy in copies:
+        copy.start()
+    for copy in copies[:4]:
+        copy.wait()
     slices, _, columns = state_ref.shape
-    for face in range(6):
-        lift = lifts_ref[face].T
-        weights_ref[:, FACE * face : FACE * (face + 1)] = lift
-        if face < 2:
-            rim_weights_ref[face] = lift
-    weights_ref[:, 6 * FACE :] = volume_ref[...]
+
+    def ahead():
+        for copy in copies[4:]:
+            copy.wait()
+        for face in range(6):
+            lift = lifts_ref[face].T
+            weights_ref[:, FACE * face : FACE * (face + 1)] = lift
+            if face < 2:
+                rim_weights_ref[face] = lift
+        weights_ref[:, 6 * FACE :] = volume_ref[...]
+
+    image = operator(
+        state_ref, blocks, stack, weights_ref, neighbor_ref, tags_ref, codes_ref, ahead
+    )
     rate_ref[...] = 1.0 / (1.0 + damping_ref[...])
-    image = operator(
-        state_ref, blocks, stack, weights_ref, neighbor_ref, tags_ref, codes_ref
-    )
+    angles = [2.0 * math.pi * k / total for k in range(total)]
     for item in range(slices):
-        forcing = forcing_of(waves_ref, item, slices, cos_ref, sin_ref)
+        at = lax.axis_index("tm") * slices + item
+        forcing = wave(at, [math.cos(x) for x in angles]) * cos_ref[...].astype(jnp.float32)
+        forcing += wave(at, [math.sin(x) for x in angles]) * sin_ref[...].astype(jnp.float32)
+        forcing_ref[item] = forcing
         out_ref[item] = (
             image[:, item * columns : (item + 1) * columns]
             + forcing
@@ -239,10 +264,11 @@
 
 
 def carry_kernel(
-    part_ref, near_ref, far_ref, rate_ref, rim_weights_ref, neighbor_ref, tags_ref, codes_ref,
-    out_ref, carry_ref,
+    pieces, part_ref, near_ref, far_ref, rate_ref, rim_weights_ref, neighbor_ref, tags_ref,
+    codes_ref, out_ref, *refs
 ):
-    slices, _, columns = part_ref.shape
+    *piece_refs, carry_ref = refs
+    slices, rows, columns = part_ref.shape
     count = columns // LANES
     low, high = rim(
         near_ref, far_ref, slices, rim_weights_ref, neighbor_ref, tags_ref, codes_ref, count
@@ -261,6 +287,47 @@
             out_ref[item, :, span] = value
             carry = rate * value if carry is None else rate * (carry + value)
         carry_ref[:, span] = carry
+    if pieces == 1:
+        piece_refs[0][...] = carry_ref[...]
+    else:
+        for step in range(pieces):
+            piece_refs[step][...] = carry_ref[row_part(step, pieces, rows), :]
+
+
+def row_part(step, pieces, rows):
+    share = rows // pieces
+    return pl.ds(pl.multiple_of((lax.axis_index("tm") ^ step) * share, 8), share)
+
+
+def periodic(carries, factor):
+    count = len(carries)
+    total = carries[0]
+    for k in range(1, count):
+        total = carries[k] + factor * total
+    power = factor
+    for _ in range(count - 1):
+        power = power * factor
+    entering = [total / (1.0 - power)]
+    for k in range(count - 1):
+        entering.append(carries[k] + factor * entering[-1])
+    return entering
+
+
+def around_kernel(slices, pieces, *refs):
+    got, rate_ref = refs[:pieces], refs[pieces]
+    sent, held = refs[pieces + 1 : 2 * pieces + 1], refs[2 * pieces + 1]
+    me = lax.axis_index("tm")
+    rate = rate_ref[row_part(0, pieces, rate_ref.shape[0]), :]
+    factor = rate
+    for _ in range(slices - 1):
+        factor = factor * rate
+    for step in range(pieces):
+        held[me ^ step] = got[step][...]
+    entering = periodic([held[k] for k in range(pieces)], factor)
+    for k in range(pieces):
+        held[k] = entering[k]
+    for step in range(pieces):
+        sent[step][...] = held[me ^ step]
 
 
 def solve_kernel(pieces, *refs):
@@ -270,11 +337,8 @@
     if pieces == 1:
         before_ref[...] = piece_refs[0][...]
     else:
-        share = rows // pieces
-        me = lax.axis_index("tm")
         for step in range(pieces):
-            owner = lax.rem(me + pieces - step, pieces)
-            before_ref[pl.ds(pl.multiple_of(owner * share, 8), share), :] = piece_refs[step][...]
+            before_ref[row_part(step, pieces, rows), :] = piece_refs[step][...]
     rate = rate_ref[...]
     value = before_ref[...]
     low = []
@@ -289,8 +353,8 @@
 
 
 def second_kernel(
-    waves_ref, state_ref, before_ref, cos_ref, sin_ref, weights_ref, neighbor_ref, tags_ref,
-    codes_ref, out_ref, result_ref, blocks, stack, semaphore,
+    state_ref, before_ref, forcing_ref, weights_ref, neighbor_ref, tags_ref, codes_ref, out_ref,
+    result_ref, blocks, stack, semaphore,
 ):
     slices, _, columns = state_ref.shape
     copy = pltpu.make_async_copy(state_ref, result_ref, semaphore)
@@ -299,11 +363,10 @@
         state_ref, blocks, stack, weights_ref, neighbor_ref, tags_ref, codes_ref
     )
     for item in range(slices):
-        forcing = forcing_of(waves_ref, item, slices, cos_ref, sin_ref)
         previous = before_ref[...] if item == 0 else state_ref[item - 1]
         out_ref[item] = (
             image[:, item * columns : (item + 1) * columns]
-            + forcing
+            + forcing_ref[item]
             + (previous - state_ref[item])
         )
     copy.wait()
@@ -330,7 +393,6 @@
 
 
 VMEM = pl.BlockSpec(memory_space=pltpu.VMEM)
-SMEM = pl.BlockSpec(memory_space=pltpu.SMEM)
 HBM = pl.BlockSpec(memory_space=pltpu.HBM)
 
 
@@ -357,60 +419,23 @@
     return near, far
 
 
-def turned(value, distance):
+def swapped(value, step):
     count = lax.axis_size("tm")
-    return lax.ppermute(value, "tm", [(i, (i + distance) % count) for i in range(count)])
-
-
-def periodic(carries, factor):
-    count = len(carries)
-    total = carries[0]
-    for k in range(1, count):
-        total = carries[k] + factor * total
-    power = factor
-    for _ in range(count - 1):
-        power = power * factor
-    entering = [total / (1.0 - power)]
-    for k in range(count - 1):
-        entering.append(carries[k] + factor * entering[-1])
-    return entering
-
-
-def around(carry, damping, slices):
-    count = lax.axis_size("tm")
-    rows = carry.shape[0]
-    share = rows // count
-    me = lax.axis_index("tm")
-    rate = 1.0 / (1.0 + lax.dynamic_slice_in_dim(damping, me * share, share, 0))
-    factor = rate
-    for _ in range(slices - 1):
-        factor = factor * rate
-    if count > 8 or share % 8:
-        parts = lax.all_to_all(carry, "tm", split_axis=0, concat_axis=0, tiled=True)
-        parts = parts.reshape(count, share, -1)
-        back = jnp.concatenate(periodic([parts[k] for k in range(count)], factor), axis=0)
-        return [lax.all_to_all(back, "tm", split_axis=0, concat_axis=0, tiled=True)]
-    parts = carry.reshape(count, share, -1)
-    sent = [
-        lax.dynamic_index_in_dim(parts, lax.rem(me + d, count), 0, keepdims=False)
-        for d in range(count)
-    ]
-    got = [sent[0]] + [turned(sent[d], d) for d in range(1, count)]
-    entering = periodic([got[(count - k) % count] for k in range(count)], factor)
-    return [entering[0]] + [turned(entering[d], d) for d in range(1, count)]
+    return lax.ppermute(value, "tm", [(i, i ^ step) for i in range(count)])
+
+
+def in_hbm(value):
+    return pltpu.with_memory_space_constraint(value, pltpu.HBM)
 
 
 def local(guess, source_cos, source_sin, damping, volume, lifts, neighbor, tags, codes):
     slices, rows, columns = guess.shape
-    total = slices * lax.axis_size("tm")
-    angles = 2.0 * np.pi * np.arange(total) / total
-    waves = jnp.asarray(np.stack([np.cos(angles), np.sin(angles)]).astype(np.float32))
+    devices = lax.axis_size("tm")
     f32, bf16 = jnp.float32, jnp.bfloat16
     shape = jax.ShapeDtypeStruct
     whole = shape((slices, rows, columns), f32)
     plane = shape((rows, columns), f32)
     packed = shape(((slices + 1) // 2, FACE, LANES), f32)
-    tables = (neighbor, tags, codes)
     depth = rows + 6 * FACE
     scratch = [
         pltpu.VMEM((slices * columns // LANES, rows, LANES), f32),
@@ -418,36 +443,65 @@
     ]
     work = 4 * rows * depth * slices * columns
     end = pltpu.VMEM((slices, NF, NP * NP, LANES), f32)
+    share = rows // devices
+    pairs = devices & (devices - 1) == 0 and devices <= 8 and share % 8 == 0
+    pieces = devices if pairs else 1
+    piece = shape((rows // pieces, columns), f32)
 
     near, far = call(
         ends_kernel, "ends", [packed] * 2,
-        [guess.reshape(slices, NF, NP**3, columns)],
+        [in_hbm(guess.reshape(slices, NF, NP**3, columns))],
         [end, end, pltpu.SemaphoreType.DMA((2,))], in_specs=[HBM],
     )
     near, far = exchange(near, far)
-    part, weights, rim_weights, rate = call(
-        first_kernel, "first",
-        [whole, shape((rows, depth), bf16), shape((2, rows, FACE), bf16), plane],
+    operands = (
+        guess, neighbor, tags, codes, jnp.swapaxes(lifts, 1, 2), volume, damping, source_cos,
+        source_sin,
+    )
+    part, weights, rim_weights, rate, forcing, *tables = call(
+        functools.partial(first_kernel, slices * devices), "first",
+        [whole, shape((rows, depth), bf16), shape((2, rows, FACE), bf16), plane, whole]
+        + [shape(neighbor.shape, jnp.int32)] * 3,
+        [in_hbm(operand) for operand in operands],
         [
-            waves, guess, source_cos, source_sin, damping, volume, jnp.swapaxes(lifts, 1, 2),
-            *tables,
+            pltpu.VMEM(whole.shape, f32),
+            pltpu.VMEM(plane.shape, bf16),
+            pltpu.VMEM(plane.shape, bf16),
+            pltpu.VMEM(plane.shape, f32),
+            pltpu.VMEM(volume.shape, bf16),
+            pltpu.VMEM((6, FACE, rows), bf16),
+            *scratch,
+            pltpu.SemaphoreType.DMA((len(operands),)),
         ],
-        scratch, flops=work, in_specs=[SMEM] + [VMEM] * 9,
-    )
-    known, carry = call(
-        carry_kernel, "carry", [whole, plane], [part, near, far, rate, rim_weights, *tables]
-    )
-    pieces = around(carry, damping, slices)
+        flops=work, in_specs=[HBM] * len(operands),
+    )
+    known, *parts = call(
+        functools.partial(carry_kernel, pieces), "carry", [whole] + [piece] * pieces,
+        [part, near, far, rate, rim_weights, *tables], [pltpu.VMEM(plane.shape, f32)],
+    )
+    if pairs:
+        parts = parts[:1] + [swapped(parts[step], step) for step in range(1, pieces)]
+        parts = call(
+            functools.partial(around_kernel, slices, pieces), "around", [piece] * pieces,
+            [*parts, rate], [pltpu.VMEM((pieces, *piece.shape), f32)],
+        )
+        parts = list(parts[:1]) + [swapped(parts[step], step) for step in range(1, pieces)]
+    else:
+        me = lax.axis_index("tm")
+        factor = lax.dynamic_slice_in_dim(rate, me * share, share, 0) ** slices
+        carries = lax.all_to_all(parts[0], "tm", split_axis=0, concat_axis=0, tiled=True)
+        carries = carries.reshape(devices, share, columns)
+        back = jnp.concatenate(periodic([carries[k] for k in range(devices)], factor), axis=0)
+        parts = [lax.all_to_all(back, "tm", split_axis=0, concat_axis=0, tiled=True)]
     state, before, near, far = call(
-        functools.partial(solve_kernel, len(pieces)), "solve",
-        [whole, plane, packed, packed], [*pieces, known, rate],
+        functools.partial(solve_kernel, pieces), "solve",
+        [whole, plane, packed, packed], [*parts, known, rate],
     )
     near, far = exchange(near, far)
     part, result = call(
         second_kernel, "second", [whole, whole],
-        [waves, state, before, source_cos, source_sin, weights, *tables],
-        [*scratch, pltpu.SemaphoreType.DMA], flops=work,
-        in_specs=[SMEM] + [VMEM] * 8, out_specs=[VMEM, HBM],
+        [state, before, forcing, weights, *tables],
+        [*scratch, pltpu.SemaphoreType.DMA], flops=work, out_specs=[VMEM, HBM],
     )
     (after,) = call(
         finish_kernel, "finish", [shape(whole.shape, bf16)],

time: 43.9 us -> 37.2 us (0.85)
  local copies, waits for them, and re-layouts: 6.53 us -> 0 us
  starting transfers between devices: 13.4 us -> 15.1 us
  other arithmetic: 0.96 us -> 0 us
  waiting for transfers between devices: 14.3 us -> 13.4 us
    unnamed x26 -> x0, local copies, waits for them, and re-layouts: 6.51 us -> none
    ppermute x6, waiting for transfers between devices: 13.8 us -> 11.6 us  [swapped(): return lax.ppermute(value, 'tm', [(i, i ^ step) for i in range(count)])]
    ppermute x2, waiting for transfers between devices: 0.45 us -> 1.7 us  [exchange(): far = lax.ppermute(far, 'space', outer + [(j, i) for i, j in outer])]
    add x1 -> x0, other arithmetic: 0.96 us -> none  [periodic(): entering.append(carries[k] + factor * entering[-1])]
    ppermute x6, starting transfers between devices: 6.35 us -> 7.3 us  [swapped(): return lax.ppermute(value, 'tm', [(i, i ^ step) for i in range(count)])]
    ppermute x2, starting transfers between devices: 0.66 us -> 1.47 us  [exchange(): near = lax.ppermute(near, 'space', inner + [(j, i) for i, j in inner])]
    pallas_call x6 -> x7, Pallas kernels: 7.48 us -> 7.8 us  [call(): pl.pallas_call(kernel, name=name, out_shape=outs, in_specs=in_specs or [V...]
  transfers between devices with their start and end apart: 10 -> 10, of which waited for: 5 -> 6; matrix products, arithmetic and copies ran while one was open for 0% -> 0% of each run, Pallas kernels for 13% -> 13%
where the time goes in v3:
time: 37.2 us; the launch traced here: 37 us
  starting transfers between devices  15.1 us (41%)
  waiting for transfers between devices  13.4 us (36%)
  Pallas kernels  7.8 us (21%)
  between operations  0.72 us (2%)
    ppermute x6, waiting for transfers between devices, swapped(): return lax.ppermute(value, 'tm', [(i, i ^ step) for i in range(count)])  11.6 us
    pallas_call x7, Pallas kernels, call(): pl.pallas_call(kernel, name=name, out_shape=outs, in_specs=in_specs or [V...  7.8 us
    ppermute x6, starting transfers between devices, swapped(): return lax.ppermute(value, 'tm', [(i, i ^ step) for i in range(count)])  7.3 us
    ppermute x2, starting transfers between devices, exchange(): far = lax.ppermute(far, 'space', outer + [(j, i) for i, j in outer])  6.37 us
    ppermute x2, waiting for transfers between devices, exchange(): far = lax.ppermute(far, 'space', outer + [(j, i) for i, j in outer])  1.7 us
    ppermute x2, starting transfers between devices, exchange(): near = lax.ppermute(near, 'space', inner + [(j, i) for i, j in inner])  1.47 us
  transfers between devices with their start and end apart: 10, of which 6 were waited for; matrix products, arithmetic and copies ran while one was open for 0% of the time, Pallas kernels for 13%

profile of v3, /device:TPU:1, one launch (start us, length us, event | category | flops | bytes accessed | tf_op | source)
XLA Modules:
  0.0 37.0 jit_solution(2800759627572219787)
XLA Ops:
  0.6 1.0 %ends.1 = (f32[1,80,128]{2,1,0:T(8,128)S(1)}, f32[1,80,128]{2,1,0:T(8,128)S(1)}) custom-call(f32[2,5,64,256]{3,2,1,0:T(8,128)} %bitcast.2), custom_call_target="tpu_custom_call" | custom-call | bytes 737280 | tf_op jit(solution)/shard_map/ends/pallas_call | solution.py:401
  1.7 0.1 collective-permute-start
  1.8 4.5 %collective-permute-start.1 = (f32[1,80,128]{2,1,0:T(8,128)S(1)}, f32[1,80,128]{2,1,0:T(8,128)S(1)}, u32[]{:S(2)}, u32[]{:S(2)}) collective-permute-start(f32[1,80,128]{2,1,0:T(8,128)S(1)} %get-tuple-element.29), channel_id=1, source_target_pairs={{1,2},{2,1},{5,6},{6,5},{9,10},{10,9},{13,14},{14,13},{17,18},{18,... | collective-permute-start | bytes 122888 | tf_op jit(solution)/shard_map/ppermute | solution.py:418
  6.3 3.0 %first.1 = (f32[2,320,256]{2,1,0:T(8,128)S(1)}, bf16[320,800]{1,0:T(8,128)(2,1)S(1)}, bf16[2,320,80]{2,1,0:T(8,128)(2,1)S(1)}, f32[320,256]{1,0:T(8,128)S(1)}, f...) custom-call(f32[2,320,256]{2,1,0:T(8,128)} %refs_0_.1, ...), custom_call_target="tpu_custom_call" | custom-call | flops 524288000 | bytes 4112384 | tf_op jit(solution)/shard_map/first/pallas_call | solution.py:401
  9.3 0.0 collective-permute-done.near_ref
  9.3 0.0 collective-permute-done.1.far_ref
  9.4 0.5 %carry.1 = (f32[2,320,256]{2,1,0:T(8,128)S(1)}, f32[80,256]{1,0:T(8,128)S(1)}, f32[80,256]{1,0:T(8,128)S(1)}, f32[80,256]{1,0:T(8,128)S(1)}, f32[80,256]{1,0:T(8,128)S(1)}) custom-call(f32[2,320,256]{2,1,0:T(8,128)S(1)} %get-tuple-element.27.part_ref, f32[1,80,128]{2,1,0:T(8,128)S(1)} %collective-permute-done.near_ref, ...), custom_call_target="tpu_custom_call" | custom-call | bytes 2168832 | tf_op jit(solution)/shard_map/carry/pallas_call | solution.py:401
  9.9 1.4 %collective-permute-start.2 = (f32[80,256]{1,0:T(8,128)S(1)}, f32[80,256]{1,0:T(8,128)S(1)}, u32[]{:S(2)}, u32[]{:S(2)}) collective-permute-start(f32[80,256]{1,0:T(8,128)S(1)} %get-tuple-element.36), channel_id=1, source_target_pairs={{0,4},{4,0},{8,12},{12,8},{1,5},{5,1},{9,13},{13,9},{2,6},{6,2},{1... | collective-permute-start | bytes 245768 | tf_op jit(solution)/shard_map/ppermute | solution.py:424
  11.2 2.3 %collective-permute-start.3 = (f32[80,256]{1,0:T(8,128)S(1)}, f32[80,256]{1,0:T(8,128)S(1)}, u32[]{:S(2)}, u32[]{:S(2)}) collective-permute-start(f32[80,256]{1,0:T(8,128)S(1)} %get-tuple-element.37), channel_id=1, source_target_pairs={{0,8},{4,12},{8,0},{12,4},{1,9},{5,13},{9,1},{13,5},{2,10},{6,14},... | collective-permute-start | bytes 245768 | tf_op jit(solution)/shard_map/ppermute | solution.py:424
  13.6 0.0 collective-permute-start.4
  13.6 0.5 %collective-permute-done.2.refs_1_ = f32[80,256]{1,0:T(8,128)S(1)} collective-permute-done((f32[80,256]{1,0:T(8,128)S(1)}, f32[80,256]{1,0:T(8,128)S(1)}, u32[]{:S(2)}, u32[]{:S(2)}) %collective-permute-start.2) | collective-permute-done | bytes 81952 | tf_op jit(solution)/shard_map/ppermute | solution.py:424
  14.1 4.9 %collective-permute-done.3.refs_2_ = f32[80,256]{1,0:T(8,128)S(1)} collective-permute-done((f32[80,256]{1,0:T(8,128)S(1)}, f32[80,256]{1,0:T(8,128)S(1)}, u32[]{:S(2)}, u32[]{:S(2)}) %collective-permute-start.3) | collective-permute-done | bytes 81952 | tf_op jit(solution)/shard_map/ppermute | solution.py:424
  19.0 0.0 collective-permute-done.4.refs_3_
  19.0 0.1 around.1
  19.1 1.3 %collective-permute-start.5 = (f32[80,256]{1,0:T(8,128)S(1)}, f32[80,256]{1,0:T(8,128)S(1)}, u32[]{:S(2)}, u32[]{:S(2)}) collective-permute-start(f32[80,256]{1,0:T(8,128)S(1)} %get-tuple-element.40), channel_id=1, source_target_pairs={{0,4},{4,0},{8,12},{12,8},{1,5},{5,1},{9,13},{13,9},{2,6},{6,2},{1... | collective-permute-start | bytes 245768 | tf_op jit(solution)/shard_map/ppermute | solution.py:424
  20.4 1.3 %collective-permute-start.6 = (f32[80,256]{1,0:T(8,128)S(1)}, f32[80,256]{1,0:T(8,128)S(1)}, u32[]{:S(2)}, u32[]{:S(2)}) collective-permute-start(f32[80,256]{1,0:T(8,128)S(1)} %get-tuple-element.41), channel_id=1, source_target_pairs={{0,8},{4,12},{8,0},{12,4},{1,9},{5,13},{9,1},{13,5},{2,10},{6,14},... | collective-permute-start | bytes 245768 | tf_op jit(solution)/shard_map/ppermute | solution.py:424
  21.8 1.0 %collective-permute-start.7 = (f32[80,256]{1,0:T(8,128)S(1)}, f32[80,256]{1,0:T(8,128)S(1)}, u32[]{:S(2)}, u32[]{:S(2)}) collective-permute-start(f32[80,256]{1,0:T(8,128)S(1)} %get-tuple-element.42), channel_id=1, source_target_pairs={{0,12},{4,8},{8,4},{12,0},{1,13},{5,9},{9,5},{13,1},{2,14},{6,10},... | collective-permute-start | bytes 245768 | tf_op jit(solution)/shard_map/ppermute | solution.py:424
  22.7 0.7 %collective-permute-done.5.refs_1_ = f32[80,256]{1,0:T(8,128)S(1)} collective-permute-done((f32[80,256]{1,0:T(8,128)S(1)}, f32[80,256]{1,0:T(8,128)S(1)}, u32[]{:S(2)}, u32[]{:S(2)}) %collective-permute-start.5) | collective-permute-done | bytes 81952 | tf_op jit(solution)/shard_map/ppermute | solution.py:424
  23.4 1.8 %collective-permute-done.6.refs_2_ = f32[80,256]{1,0:T(8,128)S(1)} collective-permute-done((f32[80,256]{1,0:T(8,128)S(1)}, f32[80,256]{1,0:T(8,128)S(1)}, u32[]{:S(2)}, u32[]{:S(2)}) %collective-permute-start.6) | collective-permute-done | bytes 81952 | tf_op jit(solution)/shard_map/ppermute | solution.py:424
  25.2 3.7 %collective-permute-done.7.refs_3_ = f32[80,256]{1,0:T(8,128)S(1)} collective-permute-done((f32[80,256]{1,0:T(8,128)S(1)}, f32[80,256]{1,0:T(8,128)S(1)}, u32[]{:S(2)}, u32[]{:S(2)}) %collective-permute-start.7) | collective-permute-done | bytes 81952 | tf_op jit(solution)/shard_map/ppermute | solution.py:424
  28.9 0.2 solve.1
  29.2 1.3 %collective-permute-start.8 = (f32[1,80,128]{2,1,0:T(8,128)S(1)}, f32[1,80,128]{2,1,0:T(8,128)S(1)}, u32[]{:S(2)}, u32[]{:S(2)}) collective-permute-start(f32[1,80,128]{2,1,0:T(8,128)S(1)} %get-tuple-element.50), channel_id=1, source_target_pairs={{0,1},{2,3},{1,0},{3,2},{4,5},{6,7},{5,4},{7,6},{8,9},{10,11},{9,8... | collective-permute-start | bytes 122888 | tf_op jit(solution)/shard_map/ppermute | solution.py:417
  30.5 1.9 %collective-permute-start.9 = (f32[1,80,128]{2,1,0:T(8,128)S(1)}, f32[1,80,128]{2,1,0:T(8,128)S(1)}, u32[]{:S(2)}, u32[]{:S(2)}) collective-permute-start(f32[1,80,128]{2,1,0:T(8,128)S(1)} %get-tuple-element.51), channel_id=1, source_target_pairs={{1,2},{2,1},{5,6},{6,5},{9,10},{10,9},{13,14},{14,13},{17,18},{18,... | collective-permute-start | bytes 122888 | tf_op jit(solution)/shard_map/ppermute | solution.py:418
  32.4 1.7 %second.1 = (f32[2,320,256]{2,1,0:T(8,128)S(1)}, f32[2,320,256]{2,1,0:T(8,128)}) custom-call(f32[2,320,256]{2,1,0:T(8,128)S(1)} %get-tuple-element.44.state_ref, f32[320,256]{1,0:T(8,128)S(1)} %get-tuple-element.45.before_ref, f32[2,320,256]{2,1,0:T(8,128)S(1)} %get-tuple-element.46.forcing_ref, bf16[320,800]{1,0:T(8,128)(2,1)S(1)} %get-tuple-element.47.weights_ref, ...), custom_call_target="tpu_custom_call" | custom-call | flops 524288000 | bytes 3479552 | tf_op jit(solution)/shard_map/second/pallas_call | solution.py:401
  34.1 0.0 collective-permute-done.8.near_ref
  34.1 1.7 %collective-permute-done.9.far_ref = f32[1,80,128]{2,1,0:T(8,128)S(1)} collective-permute-done((f32[1,80,128]{2,1,0:T(8,128)S(1)}, f32[1,80,128]{2,1,0:T(8,128)S(1)}, u32[]{:S(2)}, u32[]{:S(2)}) %collective-permute-start.9) | collective-permute-done | bytes 40992 | tf_op jit(solution)/shard_map/ppermute | solution.py:418
  35.8 1.2 %finish.1 = bf16[2,320,256]{2,1,0:T(8,128)(2,1)} custom-call(f32[2,320,256]{2,1,0:T(8,128)S(1)} %get-tuple-element.49.part_ref, f32[1,80,128]{2,1,0:T(8,128)S(1)} %collective-permute-done.8.near_ref, f32[1,80,128]{2,1,0:T(8,128)S(1)} %collective-permute-done.9.far_ref, bf16[2,320,80]{2,1,0:T(8,128)(2,1)S(1)} %get-tuple-element.31.rim_weights_ref, ...), custom_call_target="tpu_custom_call" | custom-call | bytes 1185792 | tf_op jit(solution)/shard_map/finish/pallas_call | solution.py:401
Async XLA Ops:
  1.7 7.7 %collective-permute-start = (f32[1,80,128]{2,1,0:T(8,128)S(1)}, f32[1,80,128]{2,1,0:T(8,128)S(1)}, u32[]{:S(2)}, u32[]{:S(2)}) collective-permute-start(f32[1,80,128]{2,1,0:T(8,128)S(1)} %get-tuple-element.28), channel_id=1, source_target_pairs={{0,1},{2,3},{1,0},{3,2},{4,5},{6,7},{5,4},{7,6},{8,9},{10,11},{9,8... | collective-permute-start | bytes 122888 | tf_op jit(solution)/shard_map/ppermute | solution.py:417
  1.8 7.5 %collective-permute-start.1 = (f32[1,80,128]{2,1,0:T(8,128)S(1)}, f32[1,80,128]{2,1,0:T(8,128)S(1)}, u32[]{:S(2)}, u32[]{:S(2)}) collective-permute-start(f32[1,80,128]{2,1,0:T(8,128)S(1)} %get-tuple-element.29), channel_id=1, source_target_pairs={{1,2},{2,1},{5,6},{6,5},{9,10},{10,9},{13,14},{14,13},{17,18},{18,... | collective-permute-start | bytes 122888 | tf_op jit(solution)/shard_map/ppermute | solution.py:418
  9.9 4.2 %collective-permute-start.2 = (f32[80,256]{1,0:T(8,128)S(1)}, f32[80,256]{1,0:T(8,128)S(1)}, u32[]{:S(2)}, u32[]{:S(2)}) collective-permute-start(f32[80,256]{1,0:T(8,128)S(1)} %get-tuple-element.36), channel_id=1, source_target_pairs={{0,4},{4,0},{8,12},{12,8},{1,5},{5,1},{9,13},{13,9},{2,6},{6,2},{1... | collective-permute-start | bytes 245768 | tf_op jit(solution)/shard_map/ppermute | solution.py:424
  11.2 7.8 %collective-permute-start.3 = (f32[80,256]{1,0:T(8,128)S(1)}, f32[80,256]{1,0:T(8,128)S(1)}, u32[]{:S(2)}, u32[]{:S(2)}) collective-permute-start(f32[80,256]{1,0:T(8,128)S(1)} %get-tuple-element.37), channel_id=1, source_target_pairs={{0,8},{4,12},{8,0},{12,4},{1,9},{5,13},{9,1},{13,5},{2,10},{6,14},... | collective-permute-start | bytes 245768 | tf_op jit(solution)/shard_map/ppermute | solution.py:424
  13.6 5.4 %collective-permute-start.4 = (f32[80,256]{1,0:T(8,128)S(1)}, f32[80,256]{1,0:T(8,128)S(1)}, u32[]{:S(2)}, u32[]{:S(2)}) collective-permute-start(f32[80,256]{1,0:T(8,128)S(1)} %get-tuple-element.38), channel_id=1, source_target_pairs={{0,12},{4,8},{8,4},{12,0},{1,13},{5,9},{9,5},{13,1},{2,14},{6,10},... | collective-permute-start | bytes 245768 | tf_op jit(solution)/shard_map/ppermute | solution.py:424
  19.1 4.3 %collective-permute-start.5 = (f32[80,256]{1,0:T(8,128)S(1)}, f32[80,256]{1,0:T(8,128)S(1)}, u32[]{:S(2)}, u32[]{:S(2)}) collective-permute-start(f32[80,256]{1,0:T(8,128)S(1)} %get-tuple-element.40), channel_id=1, source_target_pairs={{0,4},{4,0},{8,12},{12,8},{1,5},{5,1},{9,13},{13,9},{2,6},{6,2},{1... | collective-permute-start | bytes 245768 | tf_op jit(solution)/shard_map/ppermute | solution.py:424
  20.4 4.8 %collective-permute-start.6 = (f32[80,256]{1,0:T(8,128)S(1)}, f32[80,256]{1,0:T(8,128)S(1)}, u32[]{:S(2)}, u32[]{:S(2)}) collective-permute-start(f32[80,256]{1,0:T(8,128)S(1)} %get-tuple-element.41), channel_id=1, source_target_pairs={{0,8},{4,12},{8,0},{12,4},{1,9},{5,13},{9,1},{13,5},{2,10},{6,14},... | collective-permute-start | bytes 245768 | tf_op jit(solution)/shard_map/ppermute | solution.py:424
  21.8 7.2 %collective-permute-start.7 = (f32[80,256]{1,0:T(8,128)S(1)}, f32[80,256]{1,0:T(8,128)S(1)}, u32[]{:S(2)}, u32[]{:S(2)}) collective-permute-start(f32[80,256]{1,0:T(8,128)S(1)} %get-tuple-element.42), channel_id=1, source_target_pairs={{0,12},{4,8},{8,4},{12,0},{1,13},{5,9},{9,5},{13,1},{2,14},{6,10},... | collective-permute-start | bytes 245768 | tf_op jit(solution)/shard_map/ppermute | solution.py:424
  29.2 4.9 %collective-permute-start.8 = (f32[1,80,128]{2,1,0:T(8,128)S(1)}, f32[1,80,128]{2,1,0:T(8,128)S(1)}, u32[]{:S(2)}, u32[]{:S(2)}) collective-permute-start(f32[1,80,128]{2,1,0:T(8,128)S(1)} %get-tuple-element.50), channel_id=1, source_target_pairs={{0,1},{2,3},{1,0},{3,2},{4,5},{6,7},{5,4},{7,6},{8,9},{10,11},{9,8... | collective-permute-start | bytes 122888 | tf_op jit(solution)/shard_map/ppermute | solution.py:417
  30.5 5.3 %collective-permute-start.9 = (f32[1,80,128]{2,1,0:T(8,128)S(1)}, f32[1,80,128]{2,1,0:T(8,128)S(1)}, u32[]{:S(2)}, u32[]{:S(2)}) collective-permute-start(f32[1,80,128]{2,1,0:T(8,128)S(1)} %get-tuple-element.51), channel_id=1, source_target_pairs={{1,2},{2,1},{5,6},{6,5},{9,10},{10,9},{13,14},{14,13},{17,18},{18,... | collective-permute-start | bytes 122888 | tf_op jit(solution)/shard_map/ppermute | solution.py:418

commit v4 on v3

--- a/solution.py
+++ b/solution.py
@@ -373,15 +373,17 @@
 
 
 def finish_kernel(
-    part_ref, near_ref, far_ref, rim_weights_ref, neighbor_ref, tags_ref, codes_ref, out_ref
+    part_ref, near_ref, far_ref, rim_weights_ref, neighbor_ref, tags_ref, codes_ref, out_ref,
+    held, semaphores,
 ):
     slices, _, columns = part_ref.shape
     count = columns // LANES
     low, high = rim(
         near_ref, far_ref, slices, rim_weights_ref, neighbor_ref, tags_ref, codes_ref, count
     )
+    copies = []
     for block in range(count):
-        span = slice(block * LANES, (block + 1) * LANES)
+        span = pl.ds(block * LANES, LANES)
         for item in range(slices):
             value = part_ref[item, :, span]
             piece = slice(item * LANES, (item + 1) * LANES)
@@ -389,7 +391,14 @@
                 value = value + low[:, piece]
             if block == count - 1:
                 value = value + high[:, piece]
-            out_ref[item, :, span] = value.astype(out_ref.dtype)
+            held[item, :, span] = value.astype(held.dtype)
+        copy = pltpu.make_async_copy(
+            held.at[:, :, span], out_ref.at[:, :, span], semaphores.at[block]
+        )
+        copy.start()
+        copies.append(copy)
+    for copy in copies:
+        copy.wait()
 
 
 VMEM = pl.BlockSpec(memory_space=pltpu.VMEM)
@@ -413,7 +422,7 @@
 def exchange(near, far):
     count = lax.axis_size("space")
     inner = [(i, i + 1) for i in range(0, count - 1, 2)]
-    outer = [(i, i + 1) for i in range(1, count - 1, 2)]
+    outer = [(i, (i + 1) % count) for i in range(1, count, 2)]
     near = lax.ppermute(near, "space", inner + [(j, i) for i, j in inner])
     far = lax.ppermute(far, "space", outer + [(j, i) for i, j in outer])
     return near, far
@@ -506,6 +515,8 @@
     (after,) = call(
         finish_kernel, "finish", [shape(whole.shape, bf16)],
         [part, near, far, rim_weights, *tables],
+        [pltpu.VMEM(whole.shape, bf16), pltpu.SemaphoreType.DMA((columns // LANES,))],
+        out_specs=[HBM],
     )
     return result, after
 

time: 37.2 us -> 34.9 us (0.938)
  waiting for transfers between devices: 13.4 us -> 10.6 us
  starting transfers between devices: 15.1 us -> 15.6 us
    ppermute x2, starting transfers between devices: 6.37 us -> 3.11 us  [exchange(): far = lax.ppermute(far, 'space', outer + [(j, i) for i, j in outer])]
    ppermute x2, starting transfers between devices: 1.47 us -> 3.97 us  [exchange(): near = lax.ppermute(near, 'space', inner + [(j, i) for i, j in inner])]
    ppermute x6, waiting for transfers between devices: 11.6 us -> 9.29 us  [swapped(): return lax.ppermute(value, 'tm', [(i, i ^ step) for i in range(count)])]
    ppermute x6, starting transfers between devices: 7.3 us -> 8.53 us  [swapped(): return lax.ppermute(value, 'tm', [(i, i ^ step) for i in range(count)])]
    ppermute x2, waiting for transfers between devices: 1.7 us -> 1.26 us  [exchange(): far = lax.ppermute(far, 'space', outer + [(j, i) for i, j in outer])]
  transfers between devices with their start and end apart: 10 -> 10, of which waited for: 6 -> 5; matrix products, arithmetic and copies ran while one was open for 0% -> 0% of each run, Pallas kernels for 13% -> 14%
where the time goes in v4:
time: 34.9 us; the launch traced here: 34.7 us
  starting transfers between devices  15.6 us (45%)
  waiting for transfers between devices  10.6 us (30%)
  Pallas kernels  7.79 us (22%)
  between operations  0.7 us (2%)
    ppermute x6, waiting for transfers between devices, swapped(): return lax.ppermute(value, 'tm', [(i, i ^ step) for i in range(count)])  9.29 us
    ppermute x6, starting transfers between devices, swapped(): return lax.ppermute(value, 'tm', [(i, i ^ step) for i in range(count)])  8.53 us
    pallas_call x7, Pallas kernels, call(): pl.pallas_call(kernel, name=name, out_shape=outs, in_specs=in_specs or [V...  7.79 us
    ppermute x2, starting transfers between devices, exchange(): near = lax.ppermute(near, 'space', inner + [(j, i) for i, j in inner])  3.97 us
    ppermute x2, starting transfers between devices, exchange(): far = lax.ppermute(far, 'space', outer + [(j, i) for i, j in outer])  3.11 us
    ppermute x2, waiting for transfers between devices, exchange(): far = lax.ppermute(far, 'space', outer + [(j, i) for i, j in outer])  1.26 us
  transfers between devices with their start and end apart: 10, of which 5 were waited for; matrix products, arithmetic and copies ran while one was open for 0% of the time, Pallas kernels for 14%

profile of v4, /device:TPU:1, one launch (start us, length us, event | category | flops | bytes accessed | tf_op | source)
XLA Modules:
  0.0 34.7 jit_solution(5604010840234450879)
XLA Ops:
  0.6 1.0 %ends.1 = (f32[1,80,128]{2,1,0:T(8,128)S(1)}, f32[1,80,128]{2,1,0:T(8,128)S(1)}) custom-call(f32[2,5,64,256]{3,2,1,0:T(8,128)} %bitcast.2), custom_call_target="tpu_custom_call" | custom-call | bytes 737280 | tf_op jit(solution)/shard_map/ends/pallas_call | solution.py:410
  1.7 0.1 collective-permute-start
  1.8 2.6 %collective-permute-start.1 = (f32[1,80,128]{2,1,0:T(8,128)S(1)}, f32[1,80,128]{2,1,0:T(8,128)S(1)}, u32[]{:S(2)}, u32[]{:S(2)}) collective-permute-start(f32[1,80,128]{2,1,0:T(8,128)S(1)} %get-tuple-element.29), channel_id=1, source_target_pairs={{1,2},{3,0},{2,1},{0,3},{5,6},{7,4},{6,5},{4,7},{9,10},{11,8},{10,... | collective-permute-start | bytes 122888 | tf_op jit(solution)/shard_map/ppermute | solution.py:427
  4.4 3.0 %first.1 = (f32[2,320,256]{2,1,0:T(8,128)S(1)}, bf16[320,800]{1,0:T(8,128)(2,1)S(1)}, bf16[2,320,80]{2,1,0:T(8,128)(2,1)S(1)}, f32[320,256]{1,0:T(8,128)S(1)}, f...) custom-call(f32[2,320,256]{2,1,0:T(8,128)} %refs_0_.1, ...), custom_call_target="tpu_custom_call" | custom-call | flops 524288000 | bytes 4112384 | tf_op jit(solution)/shard_map/first/pallas_call | solution.py:410
  7.5 0.0 collective-permute-done.near_ref
  7.5 0.0 collective-permute-done.1.far_ref
  7.5 0.5 %carry.1 = (f32[2,320,256]{2,1,0:T(8,128)S(1)}, f32[80,256]{1,0:T(8,128)S(1)}, f32[80,256]{1,0:T(8,128)S(1)}, f32[80,256]{1,0:T(8,128)S(1)}, f32[80,256]{1,0:T(8,128)S(1)}) custom-call(f32[2,320,256]{2,1,0:T(8,128)S(1)} %get-tuple-element.27.part_ref, f32[1,80,128]{2,1,0:T(8,128)S(1)} %collective-permute-done.near_ref, ...), custom_call_target="tpu_custom_call" | custom-call | bytes 2168832 | tf_op jit(solution)/shard_map/carry/pallas_call | solution.py:410
  8.0 1.4 %collective-permute-start.2 = (f32[80,256]{1,0:T(8,128)S(1)}, f32[80,256]{1,0:T(8,128)S(1)}, u32[]{:S(2)}, u32[]{:S(2)}) collective-permute-start(f32[80,256]{1,0:T(8,128)S(1)} %get-tuple-element.36), channel_id=1, source_target_pairs={{0,4},{4,0},{8,12},{12,8},{1,5},{5,1},{9,13},{13,9},{2,6},{6,2},{1... | collective-permute-start | bytes 245768 | tf_op jit(solution)/shard_map/ppermute | solution.py:433
  9.4 2.3 %collective-permute-start.3 = (f32[80,256]{1,0:T(8,128)S(1)}, f32[80,256]{1,0:T(8,128)S(1)}, u32[]{:S(2)}, u32[]{:S(2)}) collective-permute-start(f32[80,256]{1,0:T(8,128)S(1)} %get-tuple-element.37), channel_id=1, source_target_pairs={{0,8},{4,12},{8,0},{12,4},{1,9},{5,13},{9,1},{13,5},{2,10},{6,14},... | collective-permute-start | bytes 245768 | tf_op jit(solution)/shard_map/ppermute | solution.py:433
  11.7 0.0 collective-permute-start.4
  11.7 0.0 collective-permute-done.2.refs_1_
  11.7 2.0 %collective-permute-done.3.refs_2_ = f32[80,256]{1,0:T(8,128)S(1)} collective-permute-done((f32[80,256]{1,0:T(8,128)S(1)}, f32[80,256]{1,0:T(8,128)S(1)}, u32[]{:S(2)}, u32[]{:S(2)}) %collective-permute-start.3) | collective-permute-done | bytes 81952 | tf_op jit(solution)/shard_map/ppermute | solution.py:433
  13.7 3.2 %collective-permute-done.4.refs_3_ = f32[80,256]{1,0:T(8,128)S(1)} collective-permute-done((f32[80,256]{1,0:T(8,128)S(1)}, f32[80,256]{1,0:T(8,128)S(1)}, u32[]{:S(2)}, u32[]{:S(2)}) %collective-permute-start.4) | collective-permute-done | bytes 81952 | tf_op jit(solution)/shard_map/ppermute | solution.py:433
  16.9 0.1 around.1
  17.0 2.7 %collective-permute-start.5 = (f32[80,256]{1,0:T(8,128)S(1)}, f32[80,256]{1,0:T(8,128)S(1)}, u32[]{:S(2)}, u32[]{:S(2)}) collective-permute-start(f32[80,256]{1,0:T(8,128)S(1)} %get-tuple-element.40), channel_id=1, source_target_pairs={{0,4},{4,0},{8,12},{12,8},{1,5},{5,1},{9,13},{13,9},{2,6},{6,2},{1... | collective-permute-start | bytes 245768 | tf_op jit(solution)/shard_map/ppermute | solution.py:433
  19.7 0.4 %collective-permute-start.6 = (f32[80,256]{1,0:T(8,128)S(1)}, f32[80,256]{1,0:T(8,128)S(1)}, u32[]{:S(2)}, u32[]{:S(2)}) collective-permute-start(f32[80,256]{1,0:T(8,128)S(1)} %get-tuple-element.41), channel_id=1, source_target_pairs={{0,8},{4,12},{8,0},{12,4},{1,9},{5,13},{9,1},{13,5},{2,10},{6,14},... | collective-permute-start | bytes 245768 | tf_op jit(solution)/shard_map/ppermute | solution.py:433
  20.1 1.7 %collective-permute-start.7 = (f32[80,256]{1,0:T(8,128)S(1)}, f32[80,256]{1,0:T(8,128)S(1)}, u32[]{:S(2)}, u32[]{:S(2)}) collective-permute-start(f32[80,256]{1,0:T(8,128)S(1)} %get-tuple-element.42), channel_id=1, source_target_pairs={{0,12},{4,8},{8,4},{12,0},{1,13},{5,9},{9,5},{13,1},{2,14},{6,10},... | collective-permute-start | bytes 245768 | tf_op jit(solution)/shard_map/ppermute | solution.py:433
  21.9 0.0 collective-permute-done.5.refs_1_
  21.9 4.0 %collective-permute-done.6.refs_2_ = f32[80,256]{1,0:T(8,128)S(1)} collective-permute-done((f32[80,256]{1,0:T(8,128)S(1)}, f32[80,256]{1,0:T(8,128)S(1)}, u32[]{:S(2)}, u32[]{:S(2)}) %collective-permute-start.6) | collective-permute-done | bytes 81952 | tf_op jit(solution)/shard_map/ppermute | solution.py:433
  25.9 0.1 collective-permute-done.7.refs_3_
  26.0 0.2 solve.1
  26.2 3.8 %collective-permute-start.8 = (f32[1,80,128]{2,1,0:T(8,128)S(1)}, f32[1,80,128]{2,1,0:T(8,128)S(1)}, u32[]{:S(2)}, u32[]{:S(2)}) collective-permute-start(f32[1,80,128]{2,1,0:T(8,128)S(1)} %get-tuple-element.50), channel_id=1, source_target_pairs={{0,1},{2,3},{1,0},{3,2},{4,5},{6,7},{5,4},{7,6},{8,9},{10,11},{9,8... | collective-permute-start | bytes 122888 | tf_op jit(solution)/shard_map/ppermute | solution.py:426
  30.0 0.5 %collective-permute-start.9 = (f32[1,80,128]{2,1,0:T(8,128)S(1)}, f32[1,80,128]{2,1,0:T(8,128)S(1)}, u32[]{:S(2)}, u32[]{:S(2)}) collective-permute-start(f32[1,80,128]{2,1,0:T(8,128)S(1)} %get-tuple-element.51), channel_id=1, source_target_pairs={{1,2},{3,0},{2,1},{0,3},{5,6},{7,4},{6,5},{4,7},{9,10},{11,8},{10,... | collective-permute-start | bytes 122888 | tf_op jit(solution)/shard_map/ppermute | solution.py:427
  30.5 1.7 %second.1 = (f32[2,320,256]{2,1,0:T(8,128)S(1)}, f32[2,320,256]{2,1,0:T(8,128)}) custom-call(f32[2,320,256]{2,1,0:T(8,128)S(1)} %get-tuple-element.44.state_ref, f32[320,256]{1,0:T(8,128)S(1)} %get-tuple-element.45.before_ref, f32[2,320,256]{2,1,0:T(8,128)S(1)} %get-tuple-element.46.forcing_ref, bf16[320,800]{1,0:T(8,128)(2,1)S(1)} %get-tuple-element.47.weights_ref, ...), custom_call_target="tpu_custom_call" | custom-call | flops 524288000 | bytes 3479552 | tf_op jit(solution)/shard_map/second/pallas_call | solution.py:410
  32.2 0.0 collective-permute-done.8.near_ref
  32.2 1.3 %collective-permute-done.9.far_ref = f32[1,80,128]{2,1,0:T(8,128)S(1)} collective-permute-done((f32[1,80,128]{2,1,0:T(8,128)S(1)}, f32[1,80,128]{2,1,0:T(8,128)S(1)}, u32[]{:S(2)}, u32[]{:S(2)}) %collective-permute-start.9) | collective-permute-done | bytes 40992 | tf_op jit(solution)/shard_map/ppermute | solution.py:427
  33.5 1.2 %finish.1 = bf16[2,320,256]{2,1,0:T(8,128)(2,1)} custom-call(f32[2,320,256]{2,1,0:T(8,128)S(1)} %get-tuple-element.49.part_ref, f32[1,80,128]{2,1,0:T(8,128)S(1)} %collective-permute-done.8.near_ref, f32[1,80,128]{2,1,0:T(8,128)S(1)} %collective-permute-done.9.far_ref, bf16[2,320,80]{2,1,0:T(8,128)(2,1)S(1)} %get-tuple-element.31.rim_weights_ref, ...), custom_call_target="tpu_custom_call" | custom-call | bytes 1185792 | tf_op jit(solution)/shard_map/finish/pallas_call | solution.py:410
Async XLA Ops:
  1.7 5.8 %collective-permute-start = (f32[1,80,128]{2,1,0:T(8,128)S(1)}, f32[1,80,128]{2,1,0:T(8,128)S(1)}, u32[]{:S(2)}, u32[]{:S(2)}) collective-permute-start(f32[1,80,128]{2,1,0:T(8,128)S(1)} %get-tuple-element.28), channel_id=1, source_target_pairs={{0,1},{2,3},{1,0},{3,2},{4,5},{6,7},{5,4},{7,6},{8,9},{10,11},{9,8... | collective-permute-start | bytes 122888 | tf_op jit(solution)/shard_map/ppermute | solution.py:426
  1.8 5.7 %collective-permute-start.1 = (f32[1,80,128]{2,1,0:T(8,128)S(1)}, f32[1,80,128]{2,1,0:T(8,128)S(1)}, u32[]{:S(2)}, u32[]{:S(2)}) collective-permute-start(f32[1,80,128]{2,1,0:T(8,128)S(1)} %get-tuple-element.29), channel_id=1, source_target_pairs={{1,2},{3,0},{2,1},{0,3},{5,6},{7,4},{6,5},{4,7},{9,10},{11,8},{10,... | collective-permute-start | bytes 122888 | tf_op jit(solution)/shard_map/ppermute | solution.py:427
  8.0 3.7 %collective-permute-start.2 = (f32[80,256]{1,0:T(8,128)S(1)}, f32[80,256]{1,0:T(8,128)S(1)}, u32[]{:S(2)}, u32[]{:S(2)}) collective-permute-start(f32[80,256]{1,0:T(8,128)S(1)} %get-tuple-element.36), channel_id=1, source_target_pairs={{0,4},{4,0},{8,12},{12,8},{1,5},{5,1},{9,13},{13,9},{2,6},{6,2},{1... | collective-permute-start | bytes 245768 | tf_op jit(solution)/shard_map/ppermute | solution.py:433
  9.4 4.4 %collective-permute-start.3 = (f32[80,256]{1,0:T(8,128)S(1)}, f32[80,256]{1,0:T(8,128)S(1)}, u32[]{:S(2)}, u32[]{:S(2)}) collective-permute-start(f32[80,256]{1,0:T(8,128)S(1)} %get-tuple-element.37), channel_id=1, source_target_pairs={{0,8},{4,12},{8,0},{12,4},{1,9},{5,13},{9,1},{13,5},{2,10},{6,14},... | collective-permute-start | bytes 245768 | tf_op jit(solution)/shard_map/ppermute | solution.py:433
  11.7 5.2 %collective-permute-start.4 = (f32[80,256]{1,0:T(8,128)S(1)}, f32[80,256]{1,0:T(8,128)S(1)}, u32[]{:S(2)}, u32[]{:S(2)}) collective-permute-start(f32[80,256]{1,0:T(8,128)S(1)} %get-tuple-element.38), channel_id=1, source_target_pairs={{0,12},{4,8},{8,4},{12,0},{1,13},{5,9},{9,5},{13,1},{2,14},{6,10},... | collective-permute-start | bytes 245768 | tf_op jit(solution)/shard_map/ppermute | solution.py:433
  17.0 4.8 %collective-permute-start.5 = (f32[80,256]{1,0:T(8,128)S(1)}, f32[80,256]{1,0:T(8,128)S(1)}, u32[]{:S(2)}, u32[]{:S(2)}) collective-permute-start(f32[80,256]{1,0:T(8,128)S(1)} %get-tuple-element.40), channel_id=1, source_target_pairs={{0,4},{4,0},{8,12},{12,8},{1,5},{5,1},{9,13},{13,9},{2,6},{6,2},{1... | collective-permute-start | bytes 245768 | tf_op jit(solution)/shard_map/ppermute | solution.py:433
  19.7 6.2 %collective-permute-start.6 = (f32[80,256]{1,0:T(8,128)S(1)}, f32[80,256]{1,0:T(8,128)S(1)}, u32[]{:S(2)}, u32[]{:S(2)}) collective-permute-start(f32[80,256]{1,0:T(8,128)S(1)} %get-tuple-element.41), channel_id=1, source_target_pairs={{0,8},{4,12},{8,0},{12,4},{1,9},{5,13},{9,1},{13,5},{2,10},{6,14},... | collective-permute-start | bytes 245768 | tf_op jit(solution)/shard_map/ppermute | solution.py:433
  20.1 5.8 %collective-permute-start.7 = (f32[80,256]{1,0:T(8,128)S(1)}, f32[80,256]{1,0:T(8,128)S(1)}, u32[]{:S(2)}, u32[]{:S(2)}) collective-permute-start(f32[80,256]{1,0:T(8,128)S(1)} %get-tuple-element.42), channel_id=1, source_target_pairs={{0,12},{4,8},{8,4},{12,0},{1,13},{5,9},{9,5},{13,1},{2,14},{6,10},... | collective-permute-start | bytes 245768 | tf_op jit(solution)/shard_map/ppermute | solution.py:433
  26.2 6.0 %collective-permute-start.8 = (f32[1,80,128]{2,1,0:T(8,128)S(1)}, f32[1,80,128]{2,1,0:T(8,128)S(1)}, u32[]{:S(2)}, u32[]{:S(2)}) collective-permute-start(f32[1,80,128]{2,1,0:T(8,128)S(1)} %get-tuple-element.50), channel_id=1, source_target_pairs={{0,1},{2,3},{1,0},{3,2},{4,5},{6,7},{5,4},{7,6},{8,9},{10,11},{9,8... | collective-permute-start | bytes 122888 | tf_op jit(solution)/shard_map/ppermute | solution.py:426
  30.0 3.4 %collective-permute-start.9 = (f32[1,80,128]{2,1,0:T(8,128)S(1)}, f32[1,80,128]{2,1,0:T(8,128)S(1)}, u32[]{:S(2)}, u32[]{:S(2)}) collective-permute-start(f32[1,80,128]{2,1,0:T(8,128)S(1)} %get-tuple-element.51), channel_id=1, source_target_pairs={{1,2},{3,0},{2,1},{0,3},{5,6},{7,4},{6,5},{4,7},{9,10},{11,8},{10,... | collective-permute-start | bytes 122888 | tf_op jit(solution)/shard_map/ppermute | solution.py:427

commit v5 on v4

--- a/solution.py
+++ b/solution.py
@@ -290,8 +290,12 @@
     if pieces == 1:
         piece_refs[0][...] = carry_ref[...]
     else:
-        for step in range(pieces):
-            piece_refs[step][...] = carry_ref[row_part(step, pieces, rows), :]
+        for step, piece_ref in zip(steps(pieces), piece_refs):
+            piece_ref[...] = carry_ref[row_part(step, pieces, rows), :]
+
+
+def steps(pieces):
+    return list(range(pieces))[:1] + list(range(1, pieces))[-1:] + list(range(1, pieces - 1))
 
 
 def row_part(step, pieces, rows):
@@ -321,13 +325,13 @@
     factor = rate
     for _ in range(slices - 1):
         factor = factor * rate
-    for step in range(pieces):
-        held[me ^ step] = got[step][...]
+    for step, piece_ref in zip(steps(pieces), got):
+        held[me ^ step] = piece_ref[...]
     entering = periodic([held[k] for k in range(pieces)], factor)
     for k in range(pieces):
         held[k] = entering[k]
-    for step in range(pieces):
-        sent[step][...] = held[me ^ step]
+    for step, piece_ref in zip(steps(pieces), sent):
+        piece_ref[...] = held[me ^ step]
 
 
 def solve_kernel(pieces, *refs):
@@ -337,8 +341,8 @@
     if pieces == 1:
         before_ref[...] = piece_refs[0][...]
     else:
-        for step in range(pieces):
-            before_ref[row_part(step, pieces, rows), :] = piece_refs[step][...]
+        for step, piece_ref in zip(steps(pieces), piece_refs):
+            before_ref[row_part(step, pieces, rows), :] = piece_ref[...]
     rate = rate_ref[...]
     value = before_ref[...]
     low = []
@@ -429,6 +433,8 @@
 
 
 def swapped(value, step):
+    if step == 0:
+        return value
     count = lax.axis_size("tm")
     return lax.ppermute(value, "tm", [(i, i ^ step) for i in range(count)])
 
@@ -489,12 +495,12 @@
         [part, near, far, rate, rim_weights, *tables], [pltpu.VMEM(plane.shape, f32)],
     )
     if pairs:
-        parts = parts[:1] + [swapped(parts[step], step) for step in range(1, pieces)]
+        parts = [swapped(part, step) for step, part in zip(steps(pieces), parts)]
         parts = call(
             functools.partial(around_kernel, slices, pieces), "around", [piece] * pieces,
             [*parts, rate], [pltpu.VMEM((pieces, *piece.shape), f32)],
         )
-        parts = list(parts[:1]) + [swapped(parts[step], step) for step in range(1, pieces)]
+        parts = [swapped(part, step) for step, part in zip(steps(pieces), parts)]
     else:
         me = lax.axis_index("tm")
         factor = lax.dynamic_slice_in_dim(rate, me * share, share, 0) ** slices

time: 34.9 us -> 32.9 us (0.943)
  starting transfers between devices: 15.6 us -> 13.2 us
  waiting for transfers between devices: 10.6 us -> 11 us
    ppermute x2, starting transfers between devices: 3.97 us -> 2.18 us  [exchange(): near = lax.ppermute(near, 'space', inner + [(j, i) for i, j in inner])]
    ppermute x6, starting transfers between devices: 8.53 us -> 7.37 us  [swapped(): return lax.ppermute(value, 'tm', [(i, i ^ step) for i in range(count)])]
    ppermute x6, waiting for transfers between devices: 9.29 us -> 10.3 us  [swapped(): return lax.ppermute(value, 'tm', [(i, i ^ step) for i in range(count)])]
    ppermute x2, starting transfers between devices: 3.11 us -> 3.66 us  [exchange(): far = lax.ppermute(far, 'space', outer + [(j, i) for i, j in outer])]
    ppermute x2, waiting for transfers between devices: 1.26 us -> 0.72 us  [exchange(): far = lax.ppermute(far, 'space', outer + [(j, i) for i, j in outer])]
  transfers between devices with their start and end apart: 10 -> 10, of which waited for: 5 -> 6; matrix products, arithmetic and copies ran while one was open for 0% -> 0% of each run, Pallas kernels for 14% -> 14%
where the time goes in v5:
time: 32.9 us; the launch traced here: 32.7 us
  starting transfers between devices  13.2 us (40%)
  waiting for transfers between devices  11 us (33%)
  Pallas kernels  7.78 us (24%)
  between operations  0.71 us (2%)
    ppermute x6, waiting for transfers between devices, swapped(): return lax.ppermute(value, 'tm', [(i, i ^ step) for i in range(count)])  10.3 us
    pallas_call x7, Pallas kernels, call(): pl.pallas_call(kernel, name=name, out_shape=outs, in_specs=in_specs or [V...  7.78 us
    ppermute x6, starting transfers between devices, swapped(): return lax.ppermute(value, 'tm', [(i, i ^ step) for i in range(count)])  7.37 us
    ppermute x2, starting transfers between devices, exchange(): far = lax.ppermute(far, 'space', outer + [(j, i) for i, j in outer])  3.66 us
    ppermute x2, starting transfers between devices, exchange(): near = lax.ppermute(near, 'space', inner + [(j, i) for i, j in inner])  2.18 us
    ppermute x2, waiting for transfers between devices, exchange(): far = lax.ppermute(far, 'space', outer + [(j, i) for i, j in outer])  0.72 us
  transfers between devices with their start and end apart: 10, of which 6 were waited for; matrix products, arithmetic and copies ran while one was open for 0% of the time, Pallas kernels for 14%

profile of v5, /device:TPU:1, one launch (start us, length us, event | category | flops | bytes accessed | tf_op | source)
XLA Modules:
  0.0 32.7 jit_solution(7725233050066746074)
XLA Ops:
  0.6 1.0 %ends.1 = (f32[1,80,128]{2,1,0:T(8,128)S(1)}, f32[1,80,128]{2,1,0:T(8,128)S(1)}) custom-call(f32[2,5,64,256]{3,2,1,0:T(8,128)} %bitcast.2), custom_call_target="tpu_custom_call" | custom-call | bytes 737280 | tf_op jit(solution)/shard_map/ends/pallas_call | solution.py:414
  1.7 0.1 collective-permute-start
  1.8 2.6 %collective-permute-start.1 = (f32[1,80,128]{2,1,0:T(8,128)S(1)}, f32[1,80,128]{2,1,0:T(8,128)S(1)}, u32[]{:S(2)}, u32[]{:S(2)}) collective-permute-start(f32[1,80,128]{2,1,0:T(8,128)S(1)} %get-tuple-element.29), channel_id=1, source_target_pairs={{1,2},{3,0},{2,1},{0,3},{5,6},{7,4},{6,5},{4,7},{9,10},{11,8},{10,... | collective-permute-start | bytes 122888 | tf_op jit(solution)/shard_map/ppermute | solution.py:431
  4.4 3.0 %first.1 = (f32[2,320,256]{2,1,0:T(8,128)S(1)}, bf16[320,800]{1,0:T(8,128)(2,1)S(1)}, bf16[2,320,80]{2,1,0:T(8,128)(2,1)S(1)}, f32[320,256]{1,0:T(8,128)S(1)}, f...) custom-call(f32[2,320,256]{2,1,0:T(8,128)} %refs_0_.1, ...), custom_call_target="tpu_custom_call" | custom-call | flops 524288000 | bytes 4112384 | tf_op jit(solution)/shard_map/first/pallas_call | solution.py:414
  7.5 0.0 collective-permute-done.near_ref
  7.5 0.0 collective-permute-done.1.far_ref
  7.5 0.5 %carry.1 = (f32[2,320,256]{2,1,0:T(8,128)S(1)}, f32[80,256]{1,0:T(8,128)S(1)}, f32[80,256]{1,0:T(8,128)S(1)}, f32[80,256]{1,0:T(8,128)S(1)}, f32[80,256]{1,0:T(8,128)S(1)}) custom-call(f32[2,320,256]{2,1,0:T(8,128)S(1)} %get-tuple-element.27.part_ref, f32[1,80,128]{2,1,0:T(8,128)S(1)} %collective-permute-done.near_ref, ...), custom_call_target="tpu_custom_call" | custom-call | bytes 2168832 | tf_op jit(solution)/shard_map/carry/pallas_call | solution.py:414
  8.0 3.4 %collective-permute-start.2 = (f32[80,256]{1,0:T(8,128)S(1)}, f32[80,256]{1,0:T(8,128)S(1)}, u32[]{:S(2)}, u32[]{:S(2)}) collective-permute-start(f32[80,256]{1,0:T(8,128)S(1)} %get-tuple-element.36), channel_id=1, source_target_pairs={{0,12},{4,8},{8,4},{12,0},{1,13},{5,9},{9,5},{13,1},{2,14},{6,10},... | collective-permute-start | bytes 245768 | tf_op jit(solution)/shard_map/ppermute | solution.py:439
  11.4 0.0 collective-permute-start.3
  11.4 0.4 %collective-permute-start.4 = (f32[80,256]{1,0:T(8,128)S(1)}, f32[80,256]{1,0:T(8,128)S(1)}, u32[]{:S(2)}, u32[]{:S(2)}) collective-permute-start(f32[80,256]{1,0:T(8,128)S(1)} %get-tuple-element.38), channel_id=1, source_target_pairs={{0,8},{4,12},{8,0},{12,4},{1,9},{5,13},{9,1},{13,5},{2,10},{6,14},... | collective-permute-start | bytes 245768 | tf_op jit(solution)/shard_map/ppermute | solution.py:439
  11.8 1.8 %collective-permute-done.2.refs_1_ = f32[80,256]{1,0:T(8,128)S(1)} collective-permute-done((f32[80,256]{1,0:T(8,128)S(1)}, f32[80,256]{1,0:T(8,128)S(1)}, u32[]{:S(2)}, u32[]{:S(2)}) %collective-permute-start.2) | collective-permute-done | bytes 81952 | tf_op jit(solution)/shard_map/ppermute | solution.py:439
  13.6 3.1 %collective-permute-done.3.refs_2_ = f32[80,256]{1,0:T(8,128)S(1)} collective-permute-done((f32[80,256]{1,0:T(8,128)S(1)}, f32[80,256]{1,0:T(8,128)S(1)}, u32[]{:S(2)}, u32[]{:S(2)}) %collective-permute-start.3) | collective-permute-done | bytes 81952 | tf_op jit(solution)/shard_map/ppermute | solution.py:439
  16.7 0.0 collective-permute-done.4.refs_3_
  16.7 0.1 around.1
  16.9 3.2 %collective-permute-start.5 = (f32[80,256]{1,0:T(8,128)S(1)}, f32[80,256]{1,0:T(8,128)S(1)}, u32[]{:S(2)}, u32[]{:S(2)}) collective-permute-start(f32[80,256]{1,0:T(8,128)S(1)} %get-tuple-element.40), channel_id=1, source_target_pairs={{0,12},{4,8},{8,4},{12,0},{1,13},{5,9},{9,5},{13,1},{2,14},{6,10},... | collective-permute-start | bytes 245768 | tf_op jit(solution)/shard_map/ppermute | solution.py:439
  20.1 0.0 collective-permute-start.6
  20.1 0.4 %collective-permute-start.7 = (f32[80,256]{1,0:T(8,128)S(1)}, f32[80,256]{1,0:T(8,128)S(1)}, u32[]{:S(2)}, u32[]{:S(2)}) collective-permute-start(f32[80,256]{1,0:T(8,128)S(1)} %get-tuple-element.42), channel_id=1, source_target_pairs={{0,8},{4,12},{8,0},{12,4},{1,9},{5,13},{9,1},{13,5},{2,10},{6,14},... | collective-permute-start | bytes 245768 | tf_op jit(solution)/shard_map/ppermute | solution.py:439
  20.5 1.5 %collective-permute-done.5.refs_1_ = f32[80,256]{1,0:T(8,128)S(1)} collective-permute-done((f32[80,256]{1,0:T(8,128)S(1)}, f32[80,256]{1,0:T(8,128)S(1)}, u32[]{:S(2)}, u32[]{:S(2)}) %collective-permute-start.5) | collective-permute-done | bytes 81952 | tf_op jit(solution)/shard_map/ppermute | solution.py:439
  22.0 1.4 %collective-permute-done.6.refs_2_ = f32[80,256]{1,0:T(8,128)S(1)} collective-permute-done((f32[80,256]{1,0:T(8,128)S(1)}, f32[80,256]{1,0:T(8,128)S(1)}, u32[]{:S(2)}, u32[]{:S(2)}) %collective-permute-start.6) | collective-permute-done | bytes 81952 | tf_op jit(solution)/shard_map/ppermute | solution.py:439
  23.4 2.4 %collective-permute-done.7.refs_3_ = f32[80,256]{1,0:T(8,128)S(1)} collective-permute-done((f32[80,256]{1,0:T(8,128)S(1)}, f32[80,256]{1,0:T(8,128)S(1)}, u32[]{:S(2)}, u32[]{:S(2)}) %collective-permute-start.7) | collective-permute-done | bytes 81952 | tf_op jit(solution)/shard_map/ppermute | solution.py:439
  25.8 0.2 solve.1
  26.0 2.1 %collective-permute-start.8 = (f32[1,80,128]{2,1,0:T(8,128)S(1)}, f32[1,80,128]{2,1,0:T(8,128)S(1)}, u32[]{:S(2)}, u32[]{:S(2)}) collective-permute-start(f32[1,80,128]{2,1,0:T(8,128)S(1)} %get-tuple-element.50), channel_id=1, source_target_pairs={{0,1},{2,3},{1,0},{3,2},{4,5},{6,7},{5,4},{7,6},{8,9},{10,11},{9,8... | collective-permute-start | bytes 122888 | tf_op jit(solution)/shard_map/ppermute | solution.py:430
  28.1 1.0 %collective-permute-start.9 = (f32[1,80,128]{2,1,0:T(8,128)S(1)}, f32[1,80,128]{2,1,0:T(8,128)S(1)}, u32[]{:S(2)}, u32[]{:S(2)}) collective-permute-start(f32[1,80,128]{2,1,0:T(8,128)S(1)} %get-tuple-element.51), channel_id=1, source_target_pairs={{1,2},{3,0},{2,1},{0,3},{5,6},{7,4},{6,5},{4,7},{9,10},{11,8},{10,... | collective-permute-start | bytes 122888 | tf_op jit(solution)/shard_map/ppermute | solution.py:431
  29.1 1.7 %second.1 = (f32[2,320,256]{2,1,0:T(8,128)S(1)}, f32[2,320,256]{2,1,0:T(8,128)}) custom-call(f32[2,320,256]{2,1,0:T(8,128)S(1)} %get-tuple-element.44.state_ref, f32[320,256]{1,0:T(8,128)S(1)} %get-tuple-element.45.before_ref, f32[2,320,256]{2,1,0:T(8,128)S(1)} %get-tuple-element.46.forcing_ref, bf16[320,800]{1,0:T(8,128)(2,1)S(1)} %get-tuple-element.47.weights_ref, ...), custom_call_target="tpu_custom_call" | custom-call | flops 524288000 | bytes 3479552 | tf_op jit(solution)/shard_map/second/pallas_call | solution.py:414
  30.8 0.0 collective-permute-done.8.near_ref
  30.8 0.7 %collective-permute-done.9.far_ref = f32[1,80,128]{2,1,0:T(8,128)S(1)} collective-permute-done((f32[1,80,128]{2,1,0:T(8,128)S(1)}, f32[1,80,128]{2,1,0:T(8,128)S(1)}, u32[]{:S(2)}, u32[]{:S(2)}) %collective-permute-start.9) | collective-permute-done | bytes 40992 | tf_op jit(solution)/shard_map/ppermute | solution.py:431
  31.5 1.2 %finish.1 = bf16[2,320,256]{2,1,0:T(8,128)(2,1)} custom-call(f32[2,320,256]{2,1,0:T(8,128)S(1)} %get-tuple-element.49.part_ref, f32[1,80,128]{2,1,0:T(8,128)S(1)} %collective-permute-done.8.near_ref, f32[1,80,128]{2,1,0:T(8,128)S(1)} %collective-permute-done.9.far_ref, bf16[2,320,80]{2,1,0:T(8,128)(2,1)S(1)} %get-tuple-element.31.rim_weights_ref, ...), custom_call_target="tpu_custom_call" | custom-call | bytes 1185792 | tf_op jit(solution)/shard_map/finish/pallas_call | solution.py:414
Async XLA Ops:
  1.7 5.8 %collective-permute-start = (f32[1,80,128]{2,1,0:T(8,128)S(1)}, f32[1,80,128]{2,1,0:T(8,128)S(1)}, u32[]{:S(2)}, u32[]{:S(2)}) collective-permute-start(f32[1,80,128]{2,1,0:T(8,128)S(1)} %get-tuple-element.28), channel_id=1, source_target_pairs={{0,1},{2,3},{1,0},{3,2},{4,5},{6,7},{5,4},{7,6},{8,9},{10,11},{9,8... | collective-permute-start | bytes 122888 | tf_op jit(solution)/shard_map/ppermute | solution.py:430
  1.8 5.7 %collective-permute-start.1 = (f32[1,80,128]{2,1,0:T(8,128)S(1)}, f32[1,80,128]{2,1,0:T(8,128)S(1)}, u32[]{:S(2)}, u32[]{:S(2)}) collective-permute-start(f32[1,80,128]{2,1,0:T(8,128)S(1)} %get-tuple-element.29), channel_id=1, source_target_pairs={{1,2},{3,0},{2,1},{0,3},{5,6},{7,4},{6,5},{4,7},{9,10},{11,8},{10,... | collective-permute-start | bytes 122888 | tf_op jit(solution)/shard_map/ppermute | solution.py:431
  8.0 5.6 %collective-permute-start.2 = (f32[80,256]{1,0:T(8,128)S(1)}, f32[80,256]{1,0:T(8,128)S(1)}, u32[]{:S(2)}, u32[]{:S(2)}) collective-permute-start(f32[80,256]{1,0:T(8,128)S(1)} %get-tuple-element.36), channel_id=1, source_target_pairs={{0,12},{4,8},{8,4},{12,0},{1,13},{5,9},{9,5},{13,1},{2,14},{6,10},... | collective-permute-start | bytes 245768 | tf_op jit(solution)/shard_map/ppermute | solution.py:439
  11.4 5.3 %collective-permute-start.3 = (f32[80,256]{1,0:T(8,128)S(1)}, f32[80,256]{1,0:T(8,128)S(1)}, u32[]{:S(2)}, u32[]{:S(2)}) collective-permute-start(f32[80,256]{1,0:T(8,128)S(1)} %get-tuple-element.37), channel_id=1, source_target_pairs={{0,4},{4,0},{8,12},{12,8},{1,5},{5,1},{9,13},{13,9},{2,6},{6,2},{1... | collective-permute-start | bytes 245768 | tf_op jit(solution)/shard_map/ppermute | solution.py:439
  11.4 5.3 %collective-permute-start.4 = (f32[80,256]{1,0:T(8,128)S(1)}, f32[80,256]{1,0:T(8,128)S(1)}, u32[]{:S(2)}, u32[]{:S(2)}) collective-permute-start(f32[80,256]{1,0:T(8,128)S(1)} %get-tuple-element.38), channel_id=1, source_target_pairs={{0,8},{4,12},{8,0},{12,4},{1,9},{5,13},{9,1},{13,5},{2,10},{6,14},... | collective-permute-start | bytes 245768 | tf_op jit(solution)/shard_map/ppermute | solution.py:439
  16.9 5.2 %collective-permute-start.5 = (f32[80,256]{1,0:T(8,128)S(1)}, f32[80,256]{1,0:T(8,128)S(1)}, u32[]{:S(2)}, u32[]{:S(2)}) collective-permute-start(f32[80,256]{1,0:T(8,128)S(1)} %get-tuple-element.40), channel_id=1, source_target_pairs={{0,12},{4,8},{8,4},{12,0},{1,13},{5,9},{9,5},{13,1},{2,14},{6,10},... | collective-permute-start | bytes 245768 | tf_op jit(solution)/shard_map/ppermute | solution.py:439
  20.1 3.3 %collective-permute-start.6 = (f32[80,256]{1,0:T(8,128)S(1)}, f32[80,256]{1,0:T(8,128)S(1)}, u32[]{:S(2)}, u32[]{:S(2)}) collective-permute-start(f32[80,256]{1,0:T(8,128)S(1)} %get-tuple-element.41), channel_id=1, source_target_pairs={{0,4},{4,0},{8,12},{12,8},{1,5},{5,1},{9,13},{13,9},{2,6},{6,2},{1... | collective-permute-start | bytes 245768 | tf_op jit(solution)/shard_map/ppermute | solution.py:439
  20.1 5.7 %collective-permute-start.7 = (f32[80,256]{1,0:T(8,128)S(1)}, f32[80,256]{1,0:T(8,128)S(1)}, u32[]{:S(2)}, u32[]{:S(2)}) collective-permute-start(f32[80,256]{1,0:T(8,128)S(1)} %get-tuple-element.42), channel_id=1, source_target_pairs={{0,8},{4,12},{8,0},{12,4},{1,9},{5,13},{9,1},{13,5},{2,10},{6,14},... | collective-permute-start | bytes 245768 | tf_op jit(solution)/shard_map/ppermute | solution.py:439
  26.0 4.8 %collective-permute-start.8 = (f32[1,80,128]{2,1,0:T(8,128)S(1)}, f32[1,80,128]{2,1,0:T(8,128)S(1)}, u32[]{:S(2)}, u32[]{:S(2)}) collective-permute-start(f32[1,80,128]{2,1,0:T(8,128)S(1)} %get-tuple-element.50), channel_id=1, source_target_pairs={{0,1},{2,3},{1,0},{3,2},{4,5},{6,7},{5,4},{7,6},{8,9},{10,11},{9,8... | collective-permute-start | bytes 122888 | tf_op jit(solution)/shard_map/ppermute | solution.py:430
  28.1 3.4 %collective-permute-start.9 = (f32[1,80,128]{2,1,0:T(8,128)S(1)}, f32[1,80,128]{2,1,0:T(8,128)S(1)}, u32[]{:S(2)}, u32[]{:S(2)}) collective-permute-start(f32[1,80,128]{2,1,0:T(8,128)S(1)} %get-tuple-element.51), channel_id=1, source_target_pairs={{1,2},{3,0},{2,1},{0,3},{5,6},{7,4},{6,5},{4,7},{9,10},{11,8},{10,... | collective-permute-start | bytes 122888 | tf_op jit(solution)/shard_map/ppermute | solution.py:431

commit v6 on v4

--- a/solution.py
+++ b/solution.py
@@ -74,7 +74,8 @@
 
 
 def operator(
-    state, blocks, stack, weights_ref, neighbor_ref, tags_ref, codes_ref, ahead=lambda: None
+    state, blocks, stack, weights_ref, neighbor_ref, tags_ref, codes_ref,
+    ready=lambda: None, ahead=lambda: None,
 ):
     slices, rows, columns = state.shape
     count = columns // LANES
@@ -89,6 +90,7 @@
             high, low = split(value)
             stack[base:, n * LANES : (n + 1) * LANES] = high
             stack[base:, wide + n * LANES : wide + (n + 1) * LANES] = low
+    ready()
     for item in range(slices):
         cubes = []
         turned = []
@@ -151,7 +153,7 @@
     return (lax.axis_index("space") & 1) == 0
 
 
-def rim(near, far, slices, rim_weights_ref, neighbor_ref, tags_ref, codes_ref, count):
+def rim(far, near, slices, rim_weights_ref, neighbor_ref, tags_ref, codes_ref, count):
     lane = lax.broadcasted_iota(jnp.int32, (1, LANES), 1)
     even = even_place()
     result = []
@@ -175,7 +177,7 @@
     return result
 
 
-def send(low, high, near_ref, far_ref):
+def send(low, high, far_ref, near_ref):
     slices = len(low)
     lane = lax.broadcasted_iota(jnp.int32, (FACE, LANES), 1)
     even = even_place()
@@ -187,7 +189,7 @@
         far_ref[item // 2] = jnp.where(even, first, last)
 
 
-def ends_kernel(state_ref, near_ref, far_ref, low, high, semaphore):
+def ends_kernel(state_ref, far_ref, near_ref, held_ref, low, high, semaphore):
     slices, _, _, columns = state_ref.shape
     copies = [
         pltpu.make_async_copy(
@@ -196,17 +198,19 @@
         pltpu.make_async_copy(
             state_ref.at[:, :, pl.ds(48, 16), pl.ds(columns - LANES, LANES)], high, semaphore.at[1]
         ),
+        pltpu.make_async_copy(state_ref, held_ref, semaphore.at[2]),
     ]
     for copy in copies:
         copy.start()
-    for copy in copies:
+    for copy in copies[:2]:
         copy.wait()
     send(
         [low[item].reshape(FACE, LANES) for item in range(slices)],
         [high[item].reshape(FACE, LANES) for item in range(slices)],
+        far_ref,
         near_ref,
-        far_ref,
-    )
+    )
+    copies[2].wait()
 
 
 def wave(at, values):
@@ -216,15 +220,14 @@
     return result
 
 
-def first_kernel(total, *refs):
-    sources = refs[:9]
-    out_ref, weights_ref, rim_weights_ref, rate_ref, forcing_ref = refs[9:14]
-    neighbor_ref, tags_ref, codes_ref = refs[14:17]
-    state_ref, cos_ref, sin_ref, damping_ref, volume_ref, lifts_ref = refs[17:23]
-    blocks, stack, semaphores = refs[23:]
+def first_kernel(total, state_ref, *refs):
+    sources = refs[:8]
+    out_ref, weights_ref, rim_weights_ref, rate_ref, forcing_ref = refs[8:13]
+    neighbor_ref, tags_ref, codes_ref = refs[13:16]
+    cos_ref, sin_ref, damping_ref, volume_ref, lifts_ref = refs[16:21]
+    blocks, stack, semaphores = refs[21:]
     targets = (
-        state_ref, neighbor_ref, tags_ref, codes_ref, lifts_ref, volume_ref, damping_ref,
-        cos_ref, sin_ref,
+        neighbor_ref, tags_ref, codes_ref, lifts_ref, volume_ref, damping_ref, cos_ref, sin_ref,
     )
     copies = [
         pltpu.make_async_copy(source, target, semaphores.at[k])
@@ -232,12 +235,14 @@
     ]
     for copy in copies:
         copy.start()
-    for copy in copies[:4]:
-        copy.wait()
     slices, _, columns = state_ref.shape
 
+    def ready():
+        for copy in copies[:3]:
+            copy.wait()
+
     def ahead():
-        for copy in copies[4:]:
+        for copy in copies[3:]:
             copy.wait()
         for face in range(6):
             lift = lifts_ref[face].T
@@ -247,7 +252,7 @@
         weights_ref[:, 6 * FACE :] = volume_ref[...]
 
     image = operator(
-        state_ref, blocks, stack, weights_ref, neighbor_ref, tags_ref, codes_ref, ahead
+        state_ref, blocks, stack, weights_ref, neighbor_ref, tags_ref, codes_ref, ready, ahead
     )
     rate_ref[...] = 1.0 / (1.0 + damping_ref[...])
     angles = [2.0 * math.pi * k / total for k in range(total)]
@@ -264,14 +269,14 @@
 
 
 def carry_kernel(
-    pieces, part_ref, near_ref, far_ref, rate_ref, rim_weights_ref, neighbor_ref, tags_ref,
+    pieces, part_ref, far_ref, near_ref, rate_ref, rim_weights_ref, neighbor_ref, tags_ref,
     codes_ref, out_ref, *refs
 ):
     *piece_refs, carry_ref = refs
     slices, rows, columns = part_ref.shape
     count = columns // LANES
     low, high = rim(
-        near_ref, far_ref, slices, rim_weights_ref, neighbor_ref, tags_ref, codes_ref, count
+        far_ref, near_ref, slices, rim_weights_ref, neighbor_ref, tags_ref, codes_ref, count
     )
     for block in range(count):
         span = slice(block * LANES, (block + 1) * LANES)
@@ -290,13 +295,13 @@
     if pieces == 1:
         piece_refs[0][...] = carry_ref[...]
     else:
-        for step in range(pieces):
-            piece_refs[step][...] = carry_ref[row_part(step, pieces, rows), :]
-
-
-def row_part(step, pieces, rows):
-    share = rows // pieces
-    return pl.ds(pl.multiple_of((lax.axis_index("tm") ^ step) * share, 8), share)
+        for part in range(pieces):
+            piece_refs[part][...] = carry_ref[row_part(part, rows // pieces), :]
+
+
+def row_part(part, share):
+    mine = lax.axis_index("tm") & 1
+    return pl.ds(pl.multiple_of(((part & 2) + (mine ^ (part & 1))) * share, 8), share)
 
 
 def periodic(carries, factor):
@@ -313,32 +318,47 @@
     return entering
 
 
-def around_kernel(slices, pieces, *refs):
-    got, rate_ref = refs[:pieces], refs[pieces]
-    sent, held = refs[pieces + 1 : 2 * pieces + 1], refs[2 * pieces + 1]
-    me = lax.axis_index("tm")
-    rate = rate_ref[row_part(0, pieces, rate_ref.shape[0]), :]
+def power(rate_ref, part, share, slices):
+    rate = rate_ref[row_part(part, share), :]
     factor = rate
     for _ in range(slices - 1):
         factor = factor * rate
-    for step in range(pieces):
-        held[me ^ step] = got[step][...]
-    entering = periodic([held[k] for k in range(pieces)], factor)
-    for k in range(pieces):
-        held[k] = entering[k]
-    for step in range(pieces):
-        sent[step][...] = held[me ^ step]
+    return factor
+
+
+def ordered(own, other):
+    first = (lax.axis_index("tm") & 1) == 0
+    return jnp.where(first, own, other), jnp.where(first, other, own)
+
+
+def pair_kernel(slices, part, own_ref, other_ref, rate_ref, out_ref):
+    factor = power(rate_ref, part, own_ref.shape[0], slices)
+    early, late = ordered(own_ref[...], other_ref[...])
+    out_ref[...] = late + factor * early
+
+
+def enter_kernel(
+    slices, part, own_ref, other_ref, here_ref, there_ref, rate_ref, keep_ref, send_ref
+):
+    factor = power(rate_ref, part, own_ref.shape[0], slices)
+    square = factor * factor
+    early, _ = ordered(own_ref[...], other_ref[...])
+    enter = (there_ref[...] + square * here_ref[...]) / (1.0 - square * square)
+    later = early + factor * enter
+    own, other = ordered(enter, later)
+    keep_ref[...] = own
+    send_ref[...] = other
 
 
 def solve_kernel(pieces, *refs):
     piece_refs = refs[:pieces]
-    right_ref, rate_ref, state_ref, before_ref, near_ref, far_ref = refs[pieces:]
+    right_ref, rate_ref, state_ref, before_ref, far_ref, near_ref = refs[pieces:]
     slices, rows, columns = right_ref.shape
     if pieces == 1:
         before_ref[...] = piece_refs[0][...]
     else:
-        for step in range(pieces):
-            before_ref[row_part(step, pieces, rows), :] = piece_refs[step][...]
+        for part in range(pieces):
+            before_ref[row_part(part, rows // pieces), :] = piece_refs[part][...]
     rate = rate_ref[...]
     value = before_ref[...]
     low = []
@@ -349,7 +369,7 @@
         cube = value.reshape(NF, NP**3, columns)
         low.append(cube[:, 0:16, 0:LANES].reshape(FACE, LANES))
         high.append(cube[:, 48:64, columns - LANES :].reshape(FACE, LANES))
-    send(low, high, near_ref, far_ref)
+    send(low, high, far_ref, near_ref)
 
 
 def second_kernel(
@@ -373,13 +393,13 @@
 
 
 def finish_kernel(
-    part_ref, near_ref, far_ref, rim_weights_ref, neighbor_ref, tags_ref, codes_ref, out_ref,
+    part_ref, far_ref, near_ref, rim_weights_ref, neighbor_ref, tags_ref, codes_ref, out_ref,
     held, semaphores,
 ):
     slices, _, columns = part_ref.shape
     count = columns // LANES
     low, high = rim(
-        near_ref, far_ref, slices, rim_weights_ref, neighbor_ref, tags_ref, codes_ref, count
+        far_ref, near_ref, slices, rim_weights_ref, neighbor_ref, tags_ref, codes_ref, count
     )
     copies = []
     for block in range(count):
@@ -419,13 +439,13 @@
     )(*args)
 
 
-def exchange(near, far):
+def exchange(far, near):
     count = lax.axis_size("space")
     inner = [(i, i + 1) for i in range(0, count - 1, 2)]
     outer = [(i, (i + 1) % count) for i in range(1, count, 2)]
+    far = lax.ppermute(far, "space", outer + [(j, i) for i, j in outer])
     near = lax.ppermute(near, "space", inner + [(j, i) for i, j in inner])
-    far = lax.ppermute(far, "space", outer + [(j, i) for i, j in outer])
-    return near, far
+    return far, near
 
 
 def swapped(value, step):
@@ -453,27 +473,26 @@
     work = 4 * rows * depth * slices * columns
     end = pltpu.VMEM((slices, NF, NP * NP, LANES), f32)
     share = rows // devices
-    pairs = devices & (devices - 1) == 0 and devices <= 8 and share % 8 == 0
+    pairs = devices == 4 and share % 8 == 0
     pieces = devices if pairs else 1
     piece = shape((rows // pieces, columns), f32)
 
-    near, far = call(
-        ends_kernel, "ends", [packed] * 2,
-        [in_hbm(guess.reshape(slices, NF, NP**3, columns))],
-        [end, end, pltpu.SemaphoreType.DMA((2,))], in_specs=[HBM],
-    )
-    near, far = exchange(near, far)
+    cube = guess.reshape(slices, NF, NP**3, columns)
+    far, near, held = call(
+        ends_kernel, "ends", [packed, packed, shape(cube.shape, f32)], [in_hbm(cube)],
+        [end, end, pltpu.SemaphoreType.DMA((3,))], in_specs=[HBM],
+    )
+    far, near = exchange(far, near)
     operands = (
-        guess, neighbor, tags, codes, jnp.swapaxes(lifts, 1, 2), volume, damping, source_cos,
+        neighbor, tags, codes, jnp.swapaxes(lifts, 1, 2), volume, damping, source_cos,
         source_sin,
     )
     part, weights, rim_weights, rate, forcing, *tables = call(
         functools.partial(first_kernel, slices * devices), "first",
         [whole, shape((rows, depth), bf16), shape((2, rows, FACE), bf16), plane, whole]
         + [shape(neighbor.shape, jnp.int32)] * 3,
-        [in_hbm(operand) for operand in operands],
+        [held.reshape(guess.shape)] + [in_hbm(operand) for operand in operands],
         [
-            pltpu.VMEM(whole.shape, f32),
             pltpu.VMEM(plane.shape, bf16),
             pltpu.VMEM(plane.shape, bf16),
             pltpu.VMEM(plane.shape, f32),
@@ -482,19 +501,29 @@
             *scratch,
             pltpu.SemaphoreType.DMA((len(operands),)),
         ],
-        flops=work, in_specs=[HBM] * len(operands),
+        flops=work, in_specs=[VMEM] + [HBM] * len(operands),
     )
     known, *parts = call(
         functools.partial(carry_kernel, pieces), "carry", [whole] + [piece] * pieces,
-        [part, near, far, rate, rim_weights, *tables], [pltpu.VMEM(plane.shape, f32)],
+        [part, far, near, rate, rim_weights, *tables], [pltpu.VMEM(plane.shape, f32)],
     )
     if pairs:
-        parts = parts[:1] + [swapped(parts[step], step) for step in range(1, pieces)]
-        parts = call(
-            functools.partial(around_kernel, slices, pieces), "around", [piece] * pieces,
-            [*parts, rate], [pltpu.VMEM((pieces, *piece.shape), f32)],
-        )
-        parts = list(parts[:1]) + [swapped(parts[step], step) for step in range(1, pieces)]
+        around = []
+        others = [swapped(parts[k + 1], 1) for k in (0, 2)]
+        for k in (0, 2):
+            (here,) = call(
+                functools.partial(pair_kernel, slices, k), "pair", [piece],
+                [parts[k], others[k // 2], rate],
+            )
+            around.append((here, swapped(here, 2)))
+        own = parts[::2]
+        parts = []
+        for k in (0, 2):
+            keep, pass_on = call(
+                functools.partial(enter_kernel, slices, k), "enter", [piece] * 2,
+                [own[k // 2], others[k // 2], *around[k // 2], rate],
+            )
+            parts += [keep, swapped(pass_on, 1)]
     else:
         me = lax.axis_index("tm")
         factor = lax.dynamic_slice_in_dim(rate, me * share, share, 0) ** slices
@@ -502,11 +531,11 @@
         carries = carries.reshape(devices, share, columns)
         back = jnp.concatenate(periodic([carries[k] for k in range(devices)], factor), axis=0)
         parts = [lax.all_to_all(back, "tm", split_axis=0, concat_axis=0, tiled=True)]
-    state, before, near, far = call(
+    state, before, far, near = call(
         functools.partial(solve_kernel, pieces), "solve",
         [whole, plane, packed, packed], [*parts, known, rate],
     )
-    near, far = exchange(near, far)
+    far, near = exchange(far, near)
     part, result = call(
         second_kernel, "second", [whole, whole],
         [state, before, forcing, weights, *tables],
@@ -514,7 +543,7 @@
     )
     (after,) = call(
         finish_kernel, "finish", [shape(whole.shape, bf16)],
-        [part, near, far, rim_weights, *tables],
+        [part, far, near, rim_weights, *tables],
         [pltpu.VMEM(whole.shape, bf16), pltpu.SemaphoreType.DMA((columns // LANES,))],
         out_specs=[HBM],
     )

time: 34.9 us -> 32.4 us (0.928)
  the two profiles are of different devices: /device:TPU:1 before, /device:TPU:0 now
where the time goes in v6:
time: 32.4 us; the launch traced here: 32.2 us
  starting transfers between devices  13.4 us (41%)
  waiting for transfers between devices  10.5 us (32%)
  Pallas kernels  7.6 us (23%)
  between operations  0.72 us (2%)
    ppermute x6, waiting for transfers between devices, swapped(): return lax.ppermute(value, 'tm', [(i, i ^ step) for i in range(count)])  9.86 us
    ppermute x6, starting transfers between devices, swapped(): return lax.ppermute(value, 'tm', [(i, i ^ step) for i in range(count)])  8.74 us
    pallas_call x10, Pallas kernels, call(): pl.pallas_call(kernel, name=name, out_shape=outs, in_specs=in_specs or [V...  7.6 us
    ppermute x2, starting transfers between devices, exchange(): far = lax.ppermute(far, 'space', outer + [(j, i) for i, j in outer])  2.51 us
    ppermute x2, starting transfers between devices, exchange(): near = lax.ppermute(near, 'space', inner + [(j, i) for i, j in inner])  2.09 us
  transfers between devices with their start and end apart: 10, of which 5 were waited for; matrix products, arithmetic and copies ran while one was open for 0% of the time, Pallas kernels for 14%

profile of v6, /device:TPU:0, one launch (start us, length us, event | category | flops | bytes accessed | tf_op | source)
XLA Modules:
  0.0 32.2 jit_solution(7859789601638930755)
XLA Ops:
  0.6 1.2 %ends.1 = (f32[1,80,128]{2,1,0:T(8,128)S(1)}, f32[1,80,128]{2,1,0:T(8,128)S(1)}, f32[2,5,64,256]{3,2,1,0:T(8,128)S(1)}) custom-call(f32[2,5,64,256]{3,2,1,0:T(8,128)} %bitcast.4), custom_call_target="tpu_custom_call" | custom-call | bytes 1392640 | tf_op jit(solution)/shard_map/ends/pallas_call | solution.py:430
  1.8 2.4 %collective-permute-start = (f32[1,80,128]{2,1,0:T(8,128)S(1)}, f32[1,80,128]{2,1,0:T(8,128)S(1)}, u32[]{:S(2)}, u32[]{:S(2)}) collective-permute-start(f32[1,80,128]{2,1,0:T(8,128)S(1)} %get-tuple-element.30), channel_id=1, source_target_pairs={{1,2},{3,0},{2,1},{0,3},{5,6},{7,4},{6,5},{4,7},{9,10},{11,8},{10,... | collective-permute-start | bytes 122888 | tf_op jit(solution)/shard_map/ppermute | solution.py:446
  4.3 0.7 %collective-permute-start.1 = (f32[1,80,128]{2,1,0:T(8,128)S(1)}, f32[1,80,128]{2,1,0:T(8,128)S(1)}, u32[]{:S(2)}, u32[]{:S(2)}) collective-permute-start(f32[1,80,128]{2,1,0:T(8,128)S(1)} %get-tuple-element.31), channel_id=1, source_target_pairs={{0,1},{2,3},{1,0},{3,2},{4,5},{6,7},{5,4},{7,6},{8,9},{10,11},{9,8... | collective-permute-start | bytes 122888 | tf_op jit(solution)/shard_map/ppermute | solution.py:447
  5.0 2.6 %first.1 = (f32[2,320,256]{2,1,0:T(8,128)S(1)}, bf16[320,800]{1,0:T(8,128)(2,1)S(1)}, bf16[2,320,80]{2,1,0:T(8,128)(2,1)S(1)}, f32[320,256]{1,0:T(8,128)S(1)}, f...) custom-call(f32[2,320,256]{2,1,0:T(8,128)S(1)} %bitcast.3, ...), custom_call_target="tpu_custom_call" | custom-call | flops 524288000 | bytes 4112384 | tf_op jit(solution)/shard_map/first/pallas_call | solution.py:430
  7.6 0.0 collective-permute-done.far_ref
  7.6 0.0 collective-permute-done.1.near_ref
  7.6 0.5 %carry.1 = (f32[2,320,256]{2,1,0:T(8,128)S(1)}, f32[80,256]{1,0:T(8,128)S(1)}, f32[80,256]{1,0:T(8,128)S(1)}, f32[80,256]{1,0:T(8,128)S(1)}, f32[80,256]{1,0:T(8,128)S(1)}) custom-call(f32[2,320,256]{2,1,0:T(8,128)S(1)} %get-tuple-element.29.part_ref, f32[1,80,128]{2,1,0:T(8,128)S(1)} %collective-permute-done.far_ref, ...), custom_call_target="tpu_custom_call" | custom-call | bytes 2168832 | tf_op jit(solution)/shard_map/carry/pallas_call | solution.py:430
  8.2 1.6 %collective-permute-start.2 = (f32[80,256]{1,0:T(8,128)S(1)}, f32[80,256]{1,0:T(8,128)S(1)}, u32[]{:S(2)}, u32[]{:S(2)}) collective-permute-start(f32[80,256]{1,0:T(8,128)S(1)} %get-tuple-element.38), channel_id=1, source_target_pairs={{0,4},{4,0},{8,12},{12,8},{1,5},{5,1},{9,13},{13,9},{2,6},{6,2},{1... | collective-permute-start | bytes 245768 | tf_op jit(solution)/shard_map/ppermute | solution.py:453
  9.8 0.4 %collective-permute-start.5 = (f32[80,256]{1,0:T(8,128)S(1)}, f32[80,256]{1,0:T(8,128)S(1)}, u32[]{:S(2)}, u32[]{:S(2)}) collective-permute-start(f32[80,256]{1,0:T(8,128)S(1)} %get-tuple-element.42), channel_id=1, source_target_pairs={{0,4},{4,0},{8,12},{12,8},{1,5},{5,1},{9,13},{13,9},{2,6},{6,2},{1... | collective-permute-start | bytes 245768 | tf_op jit(solution)/shard_map/ppermute | solution.py:453
  10.3 3.0 %collective-permute-done.2.other_ref = f32[80,256]{1,0:T(8,128)S(1)} collective-permute-done((f32[80,256]{1,0:T(8,128)S(1)}, f32[80,256]{1,0:T(8,128)S(1)}, u32[]{:S(2)}, u32[]{:S(2)}) %collective-permute-start.2) | collective-permute-done | bytes 81952 | tf_op jit(solution)/shard_map/ppermute | solution.py:453
  13.3 2.7 %collective-permute-start.3 = (f32[80,256]{1,0:T(8,128)S(1)}, f32[80,256]{1,0:T(8,128)S(1)}, u32[]{:S(2)}, u32[]{:S(2)}) collective-permute-start(f32[80,256]{1,0:T(8,128)S(1)} %pair.2.here_ref), channel_id=1, source_target_pairs={{0,8},{4,12},{8,0},{12,4},{1,9},{5,13},{9,1},{13,5},{2,10},{6,14},... | collective-permute-start | bytes 245768 | tf_op jit(solution)/shard_map/ppermute | solution.py:453
  15.9 0.0 collective-permute-done.5.other_ref
  15.9 1.6 %collective-permute-start.6 = (f32[80,256]{1,0:T(8,128)S(1)}, f32[80,256]{1,0:T(8,128)S(1)}, u32[]{:S(2)}, u32[]{:S(2)}) collective-permute-start(f32[80,256]{1,0:T(8,128)S(1)} %pair.3.here_ref), channel_id=1, source_target_pairs={{0,8},{4,12},{8,0},{12,4},{1,9},{5,13},{9,1},{13,5},{2,10},{6,14},... | collective-permute-start | bytes 245768 | tf_op jit(solution)/shard_map/ppermute | solution.py:453
  17.5 3.6 %collective-permute-done.3.there_ref = f32[80,256]{1,0:T(8,128)S(1)} collective-permute-done((f32[80,256]{1,0:T(8,128)S(1)}, f32[80,256]{1,0:T(8,128)S(1)}, u32[]{:S(2)}, u32[]{:S(2)}) %collective-permute-start.3) | collective-permute-done | bytes 81952 | tf_op jit(solution)/shard_map/ppermute | solution.py:453
  21.1 1.3 %collective-permute-start.4 = (f32[80,256]{1,0:T(8,128)S(1)}, f32[80,256]{1,0:T(8,128)S(1)}, u32[]{:S(2)}, u32[]{:S(2)}) collective-permute-start(f32[80,256]{1,0:T(8,128)S(1)} %get-tuple-element.40), channel_id=1, source_target_pairs={{0,4},{4,0},{8,12},{12,8},{1,5},{5,1},{9,13},{13,9},{2,6},{6,2},{1... | collective-permute-start | bytes 245768 | tf_op jit(solution)/shard_map/ppermute | solution.py:453
  22.4 0.0 collective-permute-done.6.there_ref
  22.4 1.2 %collective-permute-start.7 = (f32[80,256]{1,0:T(8,128)S(1)}, f32[80,256]{1,0:T(8,128)S(1)}, u32[]{:S(2)}, u32[]{:S(2)}) collective-permute-start(f32[80,256]{1,0:T(8,128)S(1)} %get-tuple-element.44), channel_id=1, source_target_pairs={{0,4},{4,0},{8,12},{12,8},{1,5},{5,1},{9,13},{13,9},{2,6},{6,2},{1... | collective-permute-start | bytes 245768 | tf_op jit(solution)/shard_map/ppermute | solution.py:453
  23.6 2.0 %collective-permute-done.4.refs_1_ = f32[80,256]{1,0:T(8,128)S(1)} collective-permute-done((f32[80,256]{1,0:T(8,128)S(1)}, f32[80,256]{1,0:T(8,128)S(1)}, u32[]{:S(2)}, u32[]{:S(2)}) %collective-permute-start.4) | collective-permute-done | bytes 81952 | tf_op jit(solution)/shard_map/ppermute | solution.py:453
  25.6 1.3 %collective-permute-done.7.refs_3_ = f32[80,256]{1,0:T(8,128)S(1)} collective-permute-done((f32[80,256]{1,0:T(8,128)S(1)}, f32[80,256]{1,0:T(8,128)S(1)}, u32[]{:S(2)}, u32[]{:S(2)}) %collective-permute-start.7) | collective-permute-done | bytes 81952 | tf_op jit(solution)/shard_map/ppermute | solution.py:453
  27.0 0.2 solve.1
  27.2 0.1 collective-permute-start.8
  27.2 1.4 %collective-permute-start.9 = (f32[1,80,128]{2,1,0:T(8,128)S(1)}, f32[1,80,128]{2,1,0:T(8,128)S(1)}, u32[]{:S(2)}, u32[]{:S(2)}) collective-permute-start(f32[1,80,128]{2,1,0:T(8,128)S(1)} %get-tuple-element.53), channel_id=1, source_target_pairs={{0,1},{2,3},{1,0},{3,2},{4,5},{6,7},{5,4},{7,6},{8,9},{10,11},{9,8... | collective-permute-start | bytes 122888 | tf_op jit(solution)/shard_map/ppermute | solution.py:447
  28.7 1.7 %second.1 = (f32[2,320,256]{2,1,0:T(8,128)S(1)}, f32[2,320,256]{2,1,0:T(8,128)}) custom-call(f32[2,320,256]{2,1,0:T(8,128)S(1)} %get-tuple-element.46.state_ref, f32[320,256]{1,0:T(8,128)S(1)} %get-tuple-element.47.before_ref, f32[2,320,256]{2,1,0:T(8,128)S(1)} %get-tuple-element.48.forcing_ref, bf16[320,800]{1,0:T(8,128)(2,1)S(1)} %get-tuple-element.49.weights_ref, ...), custom_call_target="tpu_custom_call" | custom-call | flops 524288000 | bytes 3479552 | tf_op jit(solution)/shard_map/second/pallas_call | solution.py:430
  30.3 0.6 %collective-permute-done.8.far_ref = f32[1,80,128]{2,1,0:T(8,128)S(1)} collective-permute-done((f32[1,80,128]{2,1,0:T(8,128)S(1)}, f32[1,80,128]{2,1,0:T(8,128)S(1)}, u32[]{:S(2)}, u32[]{:S(2)}) %collective-permute-start.8) | collective-permute-done | bytes 40992 | tf_op jit(solution)/shard_map/ppermute | solution.py:446
  31.0 0.0 collective-permute-done.9.near_ref
  31.0 1.2 %finish.1 = bf16[2,320,256]{2,1,0:T(8,128)(2,1)} custom-call(f32[2,320,256]{2,1,0:T(8,128)S(1)} %get-tuple-element.51.part_ref, f32[1,80,128]{2,1,0:T(8,128)S(1)} %collective-permute-done.8.far_ref, f32[1,80,128]{2,1,0:T(8,128)S(1)} %collective-permute-done.9.near_ref, bf16[2,320,80]{2,1,0:T(8,128)(2,1)S(1)} %get-tuple-element.33.rim_weights_ref, ...), custom_call_target="tpu_custom_call" | custom-call | bytes 1185792 | tf_op jit(solution)/shard_map/finish/pallas_call | solution.py:430
  (4 shorter events, 0.1 us)
Async XLA Ops:
  1.8 5.8 %collective-permute-start = (f32[1,80,128]{2,1,0:T(8,128)S(1)}, f32[1,80,128]{2,1,0:T(8,128)S(1)}, u32[]{:S(2)}, u32[]{:S(2)}) collective-permute-start(f32[1,80,128]{2,1,0:T(8,128)S(1)} %get-tuple-element.30), channel_id=1, source_target_pairs={{1,2},{3,0},{2,1},{0,3},{5,6},{7,4},{6,5},{4,7},{9,10},{11,8},{10,... | collective-permute-start | bytes 122888 | tf_op jit(solution)/shard_map/ppermute | solution.py:446
  4.3 3.3 %collective-permute-start.1 = (f32[1,80,128]{2,1,0:T(8,128)S(1)}, f32[1,80,128]{2,1,0:T(8,128)S(1)}, u32[]{:S(2)}, u32[]{:S(2)}) collective-permute-start(f32[1,80,128]{2,1,0:T(8,128)S(1)} %get-tuple-element.31), channel_id=1, source_target_pairs={{0,1},{2,3},{1,0},{3,2},{4,5},{6,7},{5,4},{7,6},{8,9},{10,11},{9,8... | collective-permute-start | bytes 122888 | tf_op jit(solution)/shard_map/ppermute | solution.py:447
  8.2 5.0 %collective-permute-start.2 = (f32[80,256]{1,0:T(8,128)S(1)}, f32[80,256]{1,0:T(8,128)S(1)}, u32[]{:S(2)}, u32[]{:S(2)}) collective-permute-start(f32[80,256]{1,0:T(8,128)S(1)} %get-tuple-element.38), channel_id=1, source_target_pairs={{0,4},{4,0},{8,12},{12,8},{1,5},{5,1},{9,13},{13,9},{2,6},{6,2},{1... | collective-permute-start | bytes 245768 | tf_op jit(solution)/shard_map/ppermute | solution.py:453
  9.8 6.1 %collective-permute-start.5 = (f32[80,256]{1,0:T(8,128)S(1)}, f32[80,256]{1,0:T(8,128)S(1)}, u32[]{:S(2)}, u32[]{:S(2)}) collective-permute-start(f32[80,256]{1,0:T(8,128)S(1)} %get-tuple-element.42), channel_id=1, source_target_pairs={{0,4},{4,0},{8,12},{12,8},{1,5},{5,1},{9,13},{13,9},{2,6},{6,2},{1... | collective-permute-start | bytes 245768 | tf_op jit(solution)/shard_map/ppermute | solution.py:453
  13.3 7.8 %collective-permute-start.3 = (f32[80,256]{1,0:T(8,128)S(1)}, f32[80,256]{1,0:T(8,128)S(1)}, u32[]{:S(2)}, u32[]{:S(2)}) collective-permute-start(f32[80,256]{1,0:T(8,128)S(1)} %pair.2.here_ref), channel_id=1, source_target_pairs={{0,8},{4,12},{8,0},{12,4},{1,9},{5,13},{9,1},{13,5},{2,10},{6,14},... | collective-permute-start | bytes 245768 | tf_op jit(solution)/shard_map/ppermute | solution.py:453
  15.9 6.5 %collective-permute-start.6 = (f32[80,256]{1,0:T(8,128)S(1)}, f32[80,256]{1,0:T(8,128)S(1)}, u32[]{:S(2)}, u32[]{:S(2)}) collective-permute-start(f32[80,256]{1,0:T(8,128)S(1)} %pair.3.here_ref), channel_id=1, source_target_pairs={{0,8},{4,12},{8,0},{12,4},{1,9},{5,13},{9,1},{13,5},{2,10},{6,14},... | collective-permute-start | bytes 245768 | tf_op jit(solution)/shard_map/ppermute | solution.py:453
  21.1 4.5 %collective-permute-start.4 = (f32[80,256]{1,0:T(8,128)S(1)}, f32[80,256]{1,0:T(8,128)S(1)}, u32[]{:S(2)}, u32[]{:S(2)}) collective-permute-start(f32[80,256]{1,0:T(8,128)S(1)} %get-tuple-element.40), channel_id=1, source_target_pairs={{0,4},{4,0},{8,12},{12,8},{1,5},{5,1},{9,13},{13,9},{2,6},{6,2},{1... | collective-permute-start | bytes 245768 | tf_op jit(solution)/shard_map/ppermute | solution.py:453
  22.4 4.5 %collective-permute-start.7 = (f32[80,256]{1,0:T(8,128)S(1)}, f32[80,256]{1,0:T(8,128)S(1)}, u32[]{:S(2)}, u32[]{:S(2)}) collective-permute-start(f32[80,256]{1,0:T(8,128)S(1)} %get-tuple-element.44), channel_id=1, source_target_pairs={{0,4},{4,0},{8,12},{12,8},{1,5},{5,1},{9,13},{13,9},{2,6},{6,2},{1... | collective-permute-start | bytes 245768 | tf_op jit(solution)/shard_map/ppermute | solution.py:453
  27.2 3.8 %collective-permute-start.8 = (f32[1,80,128]{2,1,0:T(8,128)S(1)}, f32[1,80,128]{2,1,0:T(8,128)S(1)}, u32[]{:S(2)}, u32[]{:S(2)}) collective-permute-start(f32[1,80,128]{2,1,0:T(8,128)S(1)} %get-tuple-element.52), channel_id=1, source_target_pairs={{1,2},{3,0},{2,1},{0,3},{5,6},{7,4},{6,5},{4,7},{9,10},{11,8},{10,... | collective-permute-start | bytes 122888 | tf_op jit(solution)/shard_map/ppermute | solution.py:446
  27.2 3.7 %collective-permute-start.9 = (f32[1,80,128]{2,1,0:T(8,128)S(1)}, f32[1,80,128]{2,1,0:T(8,128)S(1)}, u32[]{:S(2)}, u32[]{:S(2)}) collective-permute-start(f32[1,80,128]{2,1,0:T(8,128)S(1)} %get-tuple-element.53), channel_id=1, source_target_pairs={{0,1},{2,3},{1,0},{3,2},{4,5},{6,7},{5,4},{7,6},{8,9},{10,11},{9,8... | collective-permute-start | bytes 122888 | tf_op jit(solution)/shard_map/ppermute | solution.py:447

commit v7 on v6

--- a/solution.py
+++ b/solution.py
@@ -177,16 +177,49 @@
     return result
 
 
-def send(low, high, far_ref, near_ref):
+def packed(low, high):
+    lane = lax.broadcasted_iota(jnp.int32, (FACE, LANES), 1)
+    first = jnp.where(lane < HALF, low[0], pltpu.roll(low[1], HALF, axis=1))
+    last = jnp.where(lane < HALF, pltpu.roll(high[0], HALF, axis=1), high[1])
+    return first, last
+
+
+def send(low, high, near_ref, far_ref=None):
     slices = len(low)
-    lane = lax.broadcasted_iota(jnp.int32, (FACE, LANES), 1)
     even = even_place()
     for item in range(0, slices, 2):
         other = min(item + 1, slices - 1)
-        first = jnp.where(lane < HALF, low[item], pltpu.roll(low[other], HALF, axis=1))
-        last = jnp.where(lane < HALF, pltpu.roll(high[item], HALF, axis=1), high[other])
+        first, last = packed([low[item], low[other]], [high[item], high[other]])
         near_ref[item // 2] = jnp.where(even, last, first)
-        far_ref[item // 2] = jnp.where(even, first, last)
+        if far_ref is not None:
+            far_ref[item // 2] = jnp.where(even, first, last)
+
+
+def spread_kernel(
+    keep0_ref, pass0_ref, keep3_ref, pass3_ref, edges_ref, others_ref, rate_ref, far_ref,
+    far_pass_ref,
+):
+    columns = keep0_ref.shape[1]
+    even = even_place()
+    rate = jnp.where(
+        even,
+        rate_ref[:, 0:16, 0:LANES].reshape(FACE, LANES),
+        rate_ref[:, 48:64, columns - LANES :].reshape(FACE, LANES),
+    )
+    lane = lax.broadcasted_iota(jnp.int32, (FACE, LANES), 1)
+    for low_ref, high_ref, ends_ref, to_ref in (
+        (keep0_ref, keep3_ref, edges_ref, far_ref),
+        (pass0_ref, pass3_ref, others_ref, far_pass_ref),
+    ):
+        ends = jnp.where(even, ends_ref[0], ends_ref[1])
+        turned = pltpu.roll(ends, HALF, axis=1)
+        enter = jnp.where(even, low_ref[:, 0:LANES], high_ref[:, columns - LANES :])
+        early = rate * (enter + jnp.where(even, ends, turned))
+        late = rate * (early + jnp.where(even, turned, ends))
+        turned = pltpu.roll(jnp.where(even, late, early), HALF, axis=1)
+        to_ref[0] = jnp.where(
+            lane < HALF, jnp.where(even, early, turned), jnp.where(even, turned, late)
+        )
 
 
 def ends_kernel(state_ref, far_ref, near_ref, held_ref, low, high, semaphore):
@@ -207,8 +240,8 @@
     send(
         [low[item].reshape(FACE, LANES) for item in range(slices)],
         [high[item].reshape(FACE, LANES) for item in range(slices)],
+        near_ref,
         far_ref,
-        near_ref,
     )
     copies[2].wait()
 
@@ -272,7 +305,7 @@
     pieces, part_ref, far_ref, near_ref, rate_ref, rim_weights_ref, neighbor_ref, tags_ref,
     codes_ref, out_ref, *refs
 ):
-    *piece_refs, carry_ref = refs
+    *piece_refs, edges_ref, carry_ref = refs
     slices, rows, columns = part_ref.shape
     count = columns // LANES
     low, high = rim(
@@ -291,17 +324,24 @@
                 value = value + high[:, piece]
             out_ref[item, :, span] = value
             carry = rate * value if carry is None else rate * (carry + value)
-        carry_ref[:, span] = carry
+        carry_ref[:, :, span] = carry.reshape(NF, NP**3, LANES)
     if pieces == 1:
-        piece_refs[0][...] = carry_ref[...]
-    else:
-        for part in range(pieces):
-            piece_refs[part][...] = carry_ref[row_part(part, rows // pieces), :]
-
-
-def row_part(part, share):
-    mine = lax.axis_index("tm") & 1
-    return pl.ds(pl.multiple_of(((part & 2) + (mine ^ (part & 1))) * share, 8), share)
+        piece_refs[0][...] = carry_ref[...].reshape(rows, columns)
+        edges_ref[...] = jnp.zeros_like(edges_ref)
+        return
+    for part in range(pieces):
+        piece_refs[part][...] = carry_ref[:, row_part(part), :].reshape(FACE, columns)
+    edges = []
+    for item in range(slices):
+        first = end_trace(out_ref[item, :, 0:LANES].reshape(NF, NP**3, LANES), 0)
+        last = end_trace(out_ref[item, :, columns - LANES :].reshape(NF, NP**3, LANES), 1)
+        edges.append((first, last))
+    edges_ref[0], edges_ref[1] = packed(*zip(*edges))
+
+
+def row_part(part):
+    half = (lax.axis_index("tm") & 1) ^ (part & 1)
+    return pl.ds(pl.multiple_of((half if part < 2 else 3 - half) * 16, 16), 16)
 
 
 def periodic(carries, factor):
@@ -318,8 +358,8 @@
     return entering
 
 
-def power(rate_ref, part, share, slices):
-    rate = rate_ref[row_part(part, share), :]
+def power(rate_ref, part, slices):
+    rate = rate_ref[:, row_part(part), :].reshape(FACE, rate_ref.shape[2])
     factor = rate
     for _ in range(slices - 1):
         factor = factor * rate
@@ -332,7 +372,7 @@
 
 
 def pair_kernel(slices, part, own_ref, other_ref, rate_ref, out_ref):
-    factor = power(rate_ref, part, own_ref.shape[0], slices)
+    factor = power(rate_ref, part, slices)
     early, late = ordered(own_ref[...], other_ref[...])
     out_ref[...] = late + factor * early
 
@@ -340,7 +380,7 @@
 def enter_kernel(
     slices, part, own_ref, other_ref, here_ref, there_ref, rate_ref, keep_ref, send_ref
 ):
-    factor = power(rate_ref, part, own_ref.shape[0], slices)
+    factor = power(rate_ref, part, slices)
     square = factor * factor
     early, _ = ordered(own_ref[...], other_ref[...])
     enter = (there_ref[...] + square * here_ref[...]) / (1.0 - square * square)
@@ -352,15 +392,15 @@
 
 def solve_kernel(pieces, *refs):
     piece_refs = refs[:pieces]
-    right_ref, rate_ref, state_ref, before_ref, far_ref, near_ref = refs[pieces:]
+    right_ref, rate_ref, state_ref, before_ref, near_ref, *far_refs = refs[pieces:]
     slices, rows, columns = right_ref.shape
     if pieces == 1:
-        before_ref[...] = piece_refs[0][...]
+        before_ref[...] = piece_refs[0][...].reshape(before_ref.shape)
     else:
         for part in range(pieces):
-            before_ref[row_part(part, rows // pieces), :] = piece_refs[part][...]
+            before_ref[:, row_part(part), :] = piece_refs[part][...].reshape(NF, 16, columns)
     rate = rate_ref[...]
-    value = before_ref[...]
+    value = before_ref[...].reshape(rows, columns)
     low = []
     high = []
     for item in range(slices):
@@ -369,7 +409,7 @@
         cube = value.reshape(NF, NP**3, columns)
         low.append(cube[:, 0:16, 0:LANES].reshape(FACE, LANES))
         high.append(cube[:, 48:64, columns - LANES :].reshape(FACE, LANES))
-    send(low, high, far_ref, near_ref)
+    send(low, high, near_ref, *far_refs)
 
 
 def second_kernel(
@@ -383,7 +423,7 @@
         state_ref, blocks, stack, weights_ref, neighbor_ref, tags_ref, codes_ref
     )
     for item in range(slices):
-        previous = before_ref[...] if item == 0 else state_ref[item - 1]
+        previous = before_ref[...].reshape(state_ref.shape[1:]) if item == 0 else state_ref[item - 1]
         out_ref[item] = (
             image[:, item * columns : (item + 1) * columns]
             + forcing_ref[item]
@@ -393,13 +433,15 @@
 
 
 def finish_kernel(
-    part_ref, far_ref, near_ref, rim_weights_ref, neighbor_ref, tags_ref, codes_ref, out_ref,
+    part_ref, far_ref, far_pass_ref, near_ref, rim_weights_ref, neighbor_ref, tags_ref, codes_ref, out_ref,
     held, semaphores,
 ):
     slices, _, columns = part_ref.shape
     count = columns // LANES
+    first = (lax.axis_index("tm") & 1) == 0
+    far = jnp.where(first, far_ref[...], far_pass_ref[...])
     low, high = rim(
-        far_ref, near_ref, slices, rim_weights_ref, neighbor_ref, tags_ref, codes_ref, count
+        far, near_ref, slices, rim_weights_ref, neighbor_ref, tags_ref, codes_ref, count
     )
     copies = []
     for block in range(count):
@@ -439,13 +481,22 @@
     )(*args)
 
 
-def exchange(far, near):
+def near_exchange(near):
+    pairs = [(i, i + 1) for i in range(0, lax.axis_size("space") - 1, 2)]
+    return lax.ppermute(near, "space", pairs + [(j, i) for i, j in pairs])
+
+
+def far_exchange(far, across=False):
     count = lax.axis_size("space")
-    inner = [(i, i + 1) for i in range(0, count - 1, 2)]
-    outer = [(i, (i + 1) % count) for i in range(1, count, 2)]
-    far = lax.ppermute(far, "space", outer + [(j, i) for i, j in outer])
-    near = lax.ppermute(near, "space", inner + [(j, i) for i, j in inner])
-    return far, near
+    pairs = [(i, (i + 1) % count) for i in range(1, count, 2)]
+    pairs += [(j, i) for i, j in pairs]
+    if not across:
+        return lax.ppermute(far, "space", pairs)
+    places = range(lax.axis_size("tm"))
+    return lax.ppermute(
+        far, ("tm", "space"),
+        [(k * count + i, (k ^ 1) * count + j) for k in places for i, j in pairs],
+    )
 
 
 def swapped(value, step):
@@ -464,7 +515,9 @@
     shape = jax.ShapeDtypeStruct
     whole = shape((slices, rows, columns), f32)
     plane = shape((rows, columns), f32)
-    packed = shape(((slices + 1) // 2, FACE, LANES), f32)
+    halo = shape(((slices + 1) // 2, FACE, LANES), f32)
+    edge = shape((2, FACE, LANES), f32)
+    split_rows = shape((NF, NP**3, columns), f32)
     depth = rows + 6 * FACE
     scratch = [
         pltpu.VMEM((slices * columns // LANES, rows, LANES), f32),
@@ -473,16 +526,16 @@
     work = 4 * rows * depth * slices * columns
     end = pltpu.VMEM((slices, NF, NP * NP, LANES), f32)
     share = rows // devices
-    pairs = devices == 4 and share % 8 == 0
+    pairs = devices == 4 and slices == 2
     pieces = devices if pairs else 1
     piece = shape((rows // pieces, columns), f32)
 
     cube = guess.reshape(slices, NF, NP**3, columns)
     far, near, held = call(
-        ends_kernel, "ends", [packed, packed, shape(cube.shape, f32)], [in_hbm(cube)],
+        ends_kernel, "ends", [halo, halo, shape(cube.shape, f32)], [in_hbm(cube)],
         [end, end, pltpu.SemaphoreType.DMA((3,))], in_specs=[HBM],
     )
-    far, near = exchange(far, near)
+    far, near = far_exchange(far), near_exchange(near)
     operands = (
         neighbor, tags, codes, jnp.swapaxes(lifts, 1, 2), volume, damping, source_cos,
         source_sin,
@@ -503,27 +556,35 @@
         ],
         flops=work, in_specs=[VMEM] + [HBM] * len(operands),
     )
-    known, *parts = call(
-        functools.partial(carry_kernel, pieces), "carry", [whole] + [piece] * pieces,
-        [part, far, near, rate, rim_weights, *tables], [pltpu.VMEM(plane.shape, f32)],
+    known, *parts, edges = call(
+        functools.partial(carry_kernel, pieces), "carry", [whole] + [piece] * pieces + [edge],
+        [part, far, near, rate, rim_weights, *tables], [pltpu.VMEM(split_rows.shape, f32)],
     )
     if pairs:
         around = []
+        rates = rate.reshape(split_rows.shape)
         others = [swapped(parts[k + 1], 1) for k in (0, 2)]
         for k in (0, 2):
             (here,) = call(
                 functools.partial(pair_kernel, slices, k), "pair", [piece],
-                [parts[k], others[k // 2], rate],
+                [parts[k], others[k // 2], rates],
             )
             around.append((here, swapped(here, 2)))
+        passed = swapped(edges, 1)
         own = parts[::2]
         parts = []
+        entering = []
         for k in (0, 2):
             keep, pass_on = call(
                 functools.partial(enter_kernel, slices, k), "enter", [piece] * 2,
-                [own[k // 2], others[k // 2], *around[k // 2], rate],
+                [own[k // 2], others[k // 2], *around[k // 2], rates],
             )
+            entering += [keep, pass_on]
             parts += [keep, swapped(pass_on, 1)]
+        far, far_pass = call(
+            spread_kernel, "spread", [halo] * 2, [*entering, edges, passed, rates]
+        )
+        halos = [far_exchange(far), far_exchange(far_pass, True)]
     else:
         me = lax.axis_index("tm")
         factor = lax.dynamic_slice_in_dim(rate, me * share, share, 0) ** slices
@@ -531,11 +592,13 @@
         carries = carries.reshape(devices, share, columns)
         back = jnp.concatenate(periodic([carries[k] for k in range(devices)], factor), axis=0)
         parts = [lax.all_to_all(back, "tm", split_axis=0, concat_axis=0, tiled=True)]
-    state, before, far, near = call(
+    state, before, near, *far = call(
         functools.partial(solve_kernel, pieces), "solve",
-        [whole, plane, packed, packed], [*parts, known, rate],
-    )
-    far, near = exchange(far, near)
+        [whole, split_rows, halo] + [halo] * (not pairs), [*parts, known, rate],
+    )
+    if not pairs:
+        halos = [far_exchange(far[0])] * 2
+    near = near_exchange(near)
     part, result = call(
         second_kernel, "second", [whole, whole],
         [state, before, forcing, weights, *tables],
@@ -543,7 +606,7 @@
     )
     (after,) = call(
         finish_kernel, "finish", [shape(whole.shape, bf16)],
-        [part, far, near, rim_weights, *tables],
+        [part, *halos, near, rim_weights, *tables],
         [pltpu.VMEM(whole.shape, bf16), pltpu.SemaphoreType.DMA((columns // LANES,))],
         out_specs=[HBM],
     )

time: 32.4 us -> 30.8 us (0.951)
  the two profiles are of different devices: /device:TPU:0 before, /device:TPU:1 now
where the time goes in v7:
time: 30.8 us; the launch traced here: 30.6 us
  starting transfers between devices  16.8 us (55%)
  Pallas kernels  7.78 us (25%)
  waiting for transfers between devices  5.35 us (17%)
  between operations  0.72 us (2%)
    ppermute x7, starting transfers between devices, swapped(): return lax.ppermute(value, 'tm', [(i, i ^ step) for i in range(count)])  8.16 us
    pallas_call x11, Pallas kernels, call(): pl.pallas_call(kernel, name=name, out_shape=outs, in_specs=in_specs or [V...  7.78 us
    ppermute x2, starting transfers between devices, far_exchange(): return lax.ppermute(far, 'space', pairs)  6.6 us
    ppermute x7, waiting for transfers between devices, swapped(): return lax.ppermute(value, 'tm', [(i, i ^ step) for i in range(count)])  4.92 us
    ppermute x2, starting transfers between devices, near_exchange(): return lax.ppermute(near, 'space', pairs + [(j, i) for i, j in pairs])  1.8 us
  transfers between devices with their start and end apart: 12, of which 3 were waited for; matrix products, arithmetic and copies ran while one was open for 0% of the time, Pallas kernels for 16%

profile of v7, /device:TPU:1, one launch (start us, length us, event | category | flops | bytes accessed | tf_op | source)
XLA Modules:
  0.0 30.6 jit_solution(14931758784563863789)
XLA Ops:
  0.6 1.2 %ends.1 = (f32[1,80,128]{2,1,0:T(8,128)S(1)}, f32[1,80,128]{2,1,0:T(8,128)S(1)}, f32[2,5,64,256]{3,2,1,0:T(8,128)S(1)}) custom-call(f32[2,5,64,256]{3,2,1,0:T(8,128)} %bitcast.10), custom_call_target="tpu_custom_call" | custom-call | bytes 1392640 | tf_op jit(solution)/shard_map/ends/pallas_call | solution.py:472
  1.8 2.7 %collective-permute-start = (f32[1,80,128]{2,1,0:T(8,128)S(1)}, f32[1,80,128]{2,1,0:T(8,128)S(1)}, u32[]{:S(2)}, u32[]{:S(2)}) collective-permute-start(f32[1,80,128]{2,1,0:T(8,128)S(1)} %get-tuple-element.32), channel_id=1, source_target_pairs={{1,2},{3,0},{2,1},{0,3},{5,6},{7,4},{6,5},{4,7},{9,10},{11,8},{10,... | collective-permute-start | bytes 122888 | tf_op jit(solution)/shard_map/ppermute | solution.py:494
  4.5 0.0 collective-permute-start.1
  4.5 2.6 %first.1 = (f32[2,320,256]{2,1,0:T(8,128)S(1)}, bf16[320,800]{1,0:T(8,128)(2,1)S(1)}, bf16[2,320,80]{2,1,0:T(8,128)(2,1)S(1)}, f32[320,256]{1,0:T(8,128)S(1)}, f...) custom-call(f32[2,320,256]{2,1,0:T(8,128)S(1)} %bitcast.9, ...), custom_call_target="tpu_custom_call" | custom-call | flops 524288000 | bytes 4112384 | tf_op jit(solution)/shard_map/first/pallas_call | solution.py:472
  7.2 0.0 collective-permute-done.far_ref
  7.2 0.0 collective-permute-done.1.near_ref
  7.2 0.6 %carry.1 = (f32[2,320,256]{2,1,0:T(8,128)S(1)}, f32[80,256]{1,0:T(8,128)S(1)}, f32[80,256]{1,0:T(8,128)S(1)}, f32[80,256]{1,0:T(8,128)S(1)}, f32[80,256]{1,0:T(8,128)S(1)}, /*index=5*/f32[2,80,128]{2,1,0:T(8,128)S(1)}) custom-call(f32[2,320,256]{2,1,0:T(8,128)S(1)} %get-tuple-element.31.part_ref, f32[1,80,128]{2,1,0:T(8,128)S(1)} %collective-permute-done.far_ref, ...), custom_call_target="tpu_custom_call" | custom-call | bytes 2250752 | tf_op jit(solution)/shard_map/carry/pallas_call | solution.py:472
  7.7 1.3 %collective-permute-start.2 = (f32[80,256]{1,0:T(8,128)S(1)}, f32[80,256]{1,0:T(8,128)S(1)}, u32[]{:S(2)}, u32[]{:S(2)}) collective-permute-start(f32[80,256]{1,0:T(8,128)S(1)} %get-tuple-element.40), channel_id=1, source_target_pairs={{0,4},{4,0},{8,12},{12,8},{1,5},{5,1},{9,13},{13,9},{2,6},{6,2},{1... | collective-permute-start | bytes 245768 | tf_op jit(solution)/shard_map/ppermute | solution.py:504
  9.1 0.2 collective-permute-start.5
  9.3 1.8 %collective-permute-done.2.other_ref = f32[80,256]{1,0:T(8,128)S(1)} collective-permute-done((f32[80,256]{1,0:T(8,128)S(1)}, f32[80,256]{1,0:T(8,128)S(1)}, u32[]{:S(2)}, u32[]{:S(2)}) %collective-permute-start.2) | collective-permute-done | bytes 81952 | tf_op jit(solution)/shard_map/ppermute | solution.py:504
  11.1 2.4 %collective-permute-start.3 = (f32[80,256]{1,0:T(8,128)S(1)}, f32[80,256]{1,0:T(8,128)S(1)}, u32[]{:S(2)}, u32[]{:S(2)}) collective-permute-start(f32[80,256]{1,0:T(8,128)S(1)} %pair.2.here_ref), channel_id=1, source_target_pairs={{0,8},{4,12},{8,0},{12,4},{1,9},{5,13},{9,1},{13,5},{2,10},{6,14},... | collective-permute-start | bytes 245768 | tf_op jit(solution)/shard_map/ppermute | solution.py:504
  13.5 0.0 collective-permute-done.5.other_ref
  13.5 2.3 %collective-permute-start.6 = (f32[80,256]{1,0:T(8,128)S(1)}, f32[80,256]{1,0:T(8,128)S(1)}, u32[]{:S(2)}, u32[]{:S(2)}) collective-permute-start(f32[80,256]{1,0:T(8,128)S(1)} %pair.3.here_ref), channel_id=1, source_target_pairs={{0,8},{4,12},{8,0},{12,4},{1,9},{5,13},{9,1},{13,5},{2,10},{6,14},... | collective-permute-start | bytes 245768 | tf_op jit(solution)/shard_map/ppermute | solution.py:504
  15.8 1.0 %collective-permute-start.8 = (f32[2,80,128]{2,1,0:T(8,128)S(1)}, f32[2,80,128]{2,1,0:T(8,128)S(1)}, u32[]{:S(2)}, u32[]{:S(2)}) collective-permute-start(f32[2,80,128]{2,1,0:T(8,128)S(1)} %get-tuple-element.54.edges_ref), channel_id=1, source_target_pairs={{0,4},{4,0},{8,12},{12,8},{1,5},{5,1},{9,13},{13,9},{2,6},{6,2},{1... | collective-permute-start | bytes 245768 | tf_op jit(solution)/shard_map/ppermute | solution.py:504
  16.7 0.0 collective-permute-done.3.there_ref
  16.8 0.6 %collective-permute-start.4 = (f32[80,256]{1,0:T(8,128)S(1)}, f32[80,256]{1,0:T(8,128)S(1)}, u32[]{:S(2)}, u32[]{:S(2)}) collective-permute-start(f32[80,256]{1,0:T(8,128)S(1)} %get-tuple-element.42.pass0_ref), channel_id=1, source_target_pairs={{0,4},{4,0},{8,12},{12,8},{1,5},{5,1},{9,13},{13,9},{2,6},{6,2},{1... | collective-permute-start | bytes 245768 | tf_op jit(solution)/shard_map/ppermute | solution.py:504
  17.4 3.1 %collective-permute-done.6.there_ref = f32[80,256]{1,0:T(8,128)S(1)} collective-permute-done((f32[80,256]{1,0:T(8,128)S(1)}, f32[80,256]{1,0:T(8,128)S(1)}, u32[]{:S(2)}, u32[]{:S(2)}) %collective-permute-start.6) | collective-permute-done | bytes 81952 | tf_op jit(solution)/shard_map/ppermute | solution.py:504
  20.5 0.5 %collective-permute-start.7 = (f32[80,256]{1,0:T(8,128)S(1)}, f32[80,256]{1,0:T(8,128)S(1)}, u32[]{:S(2)}, u32[]{:S(2)}) collective-permute-start(f32[80,256]{1,0:T(8,128)S(1)} %get-tuple-element.46.pass3_ref), channel_id=1, source_target_pairs={{0,4},{4,0},{8,12},{12,8},{1,5},{5,1},{9,13},{13,9},{2,6},{6,2},{1... | collective-permute-start | bytes 245768 | tf_op jit(solution)/shard_map/ppermute | solution.py:504
  21.0 0.0 collective-permute-done.8.others_ref
  21.0 0.2 spread.1
  21.1 3.9 %collective-permute-start.9 = (f32[1,80,128]{2,1,0:T(8,128)S(1)}, f32[1,80,128]{2,1,0:T(8,128)S(1)}, u32[]{:S(2)}, u32[]{:S(2)}) collective-permute-start(f32[1,80,128]{2,1,0:T(8,128)S(1)} %get-tuple-element.55), channel_id=1, source_target_pairs={{1,2},{3,0},{2,1},{0,3},{5,6},{7,4},{6,5},{4,7},{9,10},{11,8},{10,... | collective-permute-start | bytes 122888 | tf_op jit(solution)/shard_map/ppermute | solution.py:494
  25.1 0.2 collective-permute-start.10
  25.3 0.0 collective-permute-done.4.refs_1_
  25.3 0.0 collective-permute-done.7.refs_3_
  25.3 0.2 solve.1
  25.5 1.8 %collective-permute-start.11 = (f32[1,80,128]{2,1,0:T(8,128)S(1)}, f32[1,80,128]{2,1,0:T(8,128)S(1)}, u32[]{:S(2)}, u32[]{:S(2)}) collective-permute-start(f32[1,80,128]{2,1,0:T(8,128)S(1)} %get-tuple-element.57), channel_id=1, source_target_pairs={{0,1},{2,3},{1,0},{3,2},{4,5},{6,7},{5,4},{7,6},{8,9},{10,11},{9,8... | collective-permute-start | bytes 122888 | tf_op jit(solution)/shard_map/ppermute | solution.py:486
  27.3 1.7 %second.1 = (f32[2,320,256]{2,1,0:T(8,128)S(1)}, f32[2,320,256]{2,1,0:T(8,128)}) custom-call(f32[2,320,256]{2,1,0:T(8,128)S(1)} %get-tuple-element.48.state_ref, f32[5,64,256]{2,1,0:T(8,128)S(1)} %get-tuple-element.49.before_ref, f32[2,320,256]{2,1,0:T(8,128)S(1)} %get-tuple-element.50.forcing_ref, bf16[320,800]{1,0:T(8,128)(2,1)S(1)} %get-tuple-element.51.weights_ref, ...), custom_call_target="tpu_custom_call" | custom-call | flops 524288000 | bytes 3479552 | tf_op jit(solution)/shard_map/second/pallas_call | solution.py:472
  29.0 0.0 collective-permute-done.9.far_ref
  29.0 0.4 %collective-permute-done.10.far_pass_ref = f32[1,80,128]{2,1,0:T(8,128)S(1)} collective-permute-done((f32[1,80,128]{2,1,0:T(8,128)S(1)}, f32[1,80,128]{2,1,0:T(8,128)S(1)}, u32[]{:S(2)}, u32[]{:S(2)}) %collective-permute-start.10) | collective-permute-done | bytes 40992 | tf_op jit(solution)/shard_map/ppermute | solution.py:496
  29.4 0.0 collective-permute-done.11.near_ref
  29.4 1.2 %finish.1 = bf16[2,320,256]{2,1,0:T(8,128)(2,1)} custom-call(f32[2,320,256]{2,1,0:T(8,128)S(1)} %get-tuple-element.53.part_ref, f32[1,80,128]{2,1,0:T(8,128)S(1)} %collective-permute-done.9.far_ref, f32[1,80,128]{2,1,0:T(8,128)S(1)} %collective-permute-done.10.far_pass_ref, f32[1,80,128]{2,1,0:T(8,128)S(1)} %collective-permute-done.11.near_ref, ...), custom_call_target="tpu_custom_call" | custom-call | bytes 1226752 | tf_op jit(solution)/shard_map/finish/pallas_call | solution.py:472
  (4 shorter events, 0.1 us)
Async XLA Ops:
  1.8 5.3 %collective-permute-start = (f32[1,80,128]{2,1,0:T(8,128)S(1)}, f32[1,80,128]{2,1,0:T(8,128)S(1)}, u32[]{:S(2)}, u32[]{:S(2)}) collective-permute-start(f32[1,80,128]{2,1,0:T(8,128)S(1)} %get-tuple-element.32), channel_id=1, source_target_pairs={{1,2},{3,0},{2,1},{0,3},{5,6},{7,4},{6,5},{4,7},{9,10},{11,8},{10,... | collective-permute-start | bytes 122888 | tf_op jit(solution)/shard_map/ppermute | solution.py:494
  4.5 2.7 %collective-permute-start.1 = (f32[1,80,128]{2,1,0:T(8,128)S(1)}, f32[1,80,128]{2,1,0:T(8,128)S(1)}, u32[]{:S(2)}, u32[]{:S(2)}) collective-permute-start(f32[1,80,128]{2,1,0:T(8,128)S(1)} %get-tuple-element.33), channel_id=1, source_target_pairs={{0,1},{2,3},{1,0},{3,2},{4,5},{6,7},{5,4},{7,6},{8,9},{10,11},{9,8... | collective-permute-start | bytes 122888 | tf_op jit(solution)/shard_map/ppermute | solution.py:486
  7.7 3.3 %collective-permute-start.2 = (f32[80,256]{1,0:T(8,128)S(1)}, f32[80,256]{1,0:T(8,128)S(1)}, u32[]{:S(2)}, u32[]{:S(2)}) collective-permute-start(f32[80,256]{1,0:T(8,128)S(1)} %get-tuple-element.40), channel_id=1, source_target_pairs={{0,4},{4,0},{8,12},{12,8},{1,5},{5,1},{9,13},{13,9},{2,6},{6,2},{1... | collective-permute-start | bytes 245768 | tf_op jit(solution)/shard_map/ppermute | solution.py:504
  9.1 4.4 %collective-permute-start.5 = (f32[80,256]{1,0:T(8,128)S(1)}, f32[80,256]{1,0:T(8,128)S(1)}, u32[]{:S(2)}, u32[]{:S(2)}) collective-permute-start(f32[80,256]{1,0:T(8,128)S(1)} %get-tuple-element.44), channel_id=1, source_target_pairs={{0,4},{4,0},{8,12},{12,8},{1,5},{5,1},{9,13},{13,9},{2,6},{6,2},{1... | collective-permute-start | bytes 245768 | tf_op jit(solution)/shard_map/ppermute | solution.py:504
  11.1 5.6 %collective-permute-start.3 = (f32[80,256]{1,0:T(8,128)S(1)}, f32[80,256]{1,0:T(8,128)S(1)}, u32[]{:S(2)}, u32[]{:S(2)}) collective-permute-start(f32[80,256]{1,0:T(8,128)S(1)} %pair.2.here_ref), channel_id=1, source_target_pairs={{0,8},{4,12},{8,0},{12,4},{1,9},{5,13},{9,1},{13,5},{2,10},{6,14},... | collective-permute-start | bytes 245768 | tf_op jit(solution)/shard_map/ppermute | solution.py:504
  13.5 6.9 %collective-permute-start.6 = (f32[80,256]{1,0:T(8,128)S(1)}, f32[80,256]{1,0:T(8,128)S(1)}, u32[]{:S(2)}, u32[]{:S(2)}) collective-permute-start(f32[80,256]{1,0:T(8,128)S(1)} %pair.3.here_ref), channel_id=1, source_target_pairs={{0,8},{4,12},{8,0},{12,4},{1,9},{5,13},{9,1},{13,5},{2,10},{6,14},... | collective-permute-start | bytes 245768 | tf_op jit(solution)/shard_map/ppermute | solution.py:504
  15.8 5.2 %collective-permute-start.8 = (f32[2,80,128]{2,1,0:T(8,128)S(1)}, f32[2,80,128]{2,1,0:T(8,128)S(1)}, u32[]{:S(2)}, u32[]{:S(2)}) collective-permute-start(f32[2,80,128]{2,1,0:T(8,128)S(1)} %get-tuple-element.54.edges_ref), channel_id=1, source_target_pairs={{0,4},{4,0},{8,12},{12,8},{1,5},{5,1},{9,13},{13,9},{2,6},{6,2},{1... | collective-permute-start | bytes 245768 | tf_op jit(solution)/shard_map/ppermute | solution.py:504
  16.8 8.5 %collective-permute-start.4 = (f32[80,256]{1,0:T(8,128)S(1)}, f32[80,256]{1,0:T(8,128)S(1)}, u32[]{:S(2)}, u32[]{:S(2)}) collective-permute-start(f32[80,256]{1,0:T(8,128)S(1)} %get-tuple-element.42.pass0_ref), channel_id=1, source_target_pairs={{0,4},{4,0},{8,12},{12,8},{1,5},{5,1},{9,13},{13,9},{2,6},{6,2},{1... | collective-permute-start | bytes 245768 | tf_op jit(solution)/shard_map/ppermute | solution.py:504
  20.5 4.8 %collective-permute-start.7 = (f32[80,256]{1,0:T(8,128)S(1)}, f32[80,256]{1,0:T(8,128)S(1)}, u32[]{:S(2)}, u32[]{:S(2)}) collective-permute-start(f32[80,256]{1,0:T(8,128)S(1)} %get-tuple-element.46.pass3_ref), channel_id=1, source_target_pairs={{0,4},{4,0},{8,12},{12,8},{1,5},{5,1},{9,13},{13,9},{2,6},{6,2},{1... | collective-permute-start | bytes 245768 | tf_op jit(solution)/shard_map/ppermute | solution.py:504
  21.1 7.8 %collective-permute-start.9 = (f32[1,80,128]{2,1,0:T(8,128)S(1)}, f32[1,80,128]{2,1,0:T(8,128)S(1)}, u32[]{:S(2)}, u32[]{:S(2)}) collective-permute-start(f32[1,80,128]{2,1,0:T(8,128)S(1)} %get-tuple-element.55), channel_id=1, source_target_pairs={{1,2},{3,0},{2,1},{0,3},{5,6},{7,4},{6,5},{4,7},{9,10},{11,8},{10,... | collective-permute-start | bytes 122888 | tf_op jit(solution)/shard_map/ppermute | solution.py:494
  25.1 4.3 %collective-permute-start.10 = (f32[1,80,128]{2,1,0:T(8,128)S(1)}, f32[1,80,128]{2,1,0:T(8,128)S(1)}, u32[]{:S(2)}, u32[]{:S(2)}) collective-permute-start(f32[1,80,128]{2,1,0:T(8,128)S(1)} %get-tuple-element.56), channel_id=1, source_target_pairs={{1,6},{3,4},{2,5},{0,7},{5,2},{7,0},{6,1},{4,3},{9,14},{11,12},{10... | collective-permute-start | bytes 122888 | tf_op jit(solution)/shard_map/ppermute | solution.py:496
  25.5 3.9 %collective-permute-start.11 = (f32[1,80,128]{2,1,0:T(8,128)S(1)}, f32[1,80,128]{2,1,0:T(8,128)S(1)}, u32[]{:S(2)}, u32[]{:S(2)}) collective-permute-start(f32[1,80,128]{2,1,0:T(8,128)S(1)} %get-tuple-element.57), channel_id=1, source_target_pairs={{0,1},{2,3},{1,0},{3,2},{4,5},{6,7},{5,4},{7,6},{8,9},{10,11},{9,8... | collective-permute-start | bytes 122888 | tf_op jit(solution)/shard_map/ppermute | solution.py:486

commit v8 on v7

--- a/solution.py
+++ b/solution.py
@@ -196,8 +196,8 @@
 
 
 def spread_kernel(
-    keep0_ref, pass0_ref, keep3_ref, pass3_ref, edges_ref, others_ref, rate_ref, far_ref,
-    far_pass_ref,
+    keep0_ref, pass0_ref, keep3_ref, pass3_ref, edges_ref, others_ref, rate_ref, far_pass_ref,
+    far_ref,
 ):
     columns = keep0_ref.shape[1]
     even = even_place()
@@ -433,7 +433,7 @@
 
 
 def finish_kernel(
-    part_ref, far_ref, far_pass_ref, near_ref, rim_weights_ref, neighbor_ref, tags_ref, codes_ref, out_ref,
+    part_ref, far_pass_ref, far_ref, near_ref, rim_weights_ref, neighbor_ref, tags_ref, codes_ref, out_ref,
     held, semaphores,
 ):
     slices, _, columns = part_ref.shape
@@ -581,10 +581,10 @@
             )
             entering += [keep, pass_on]
             parts += [keep, swapped(pass_on, 1)]
-        far, far_pass = call(
+        far_pass, far = call(
             spread_kernel, "spread", [halo] * 2, [*entering, edges, passed, rates]
         )
-        halos = [far_exchange(far), far_exchange(far_pass, True)]
+        halos = [far_exchange(far_pass, True), far_exchange(far)]
     else:
         me = lax.axis_index("tm")
         factor = lax.dynamic_slice_in_dim(rate, me * share, share, 0) ** slices

time: 30.8 us -> 30.6 us (level)
  waiting for transfers between devices: 5.35 us -> 4.93 us
    ppermute x2, starting transfers between devices: 6.6 us -> 2.67 us  [far_exchange(): return lax.ppermute(far, 'space', pairs)]
    ppermute x1, starting transfers between devices: 0.2 us -> 4.06 us  [far_exchange(): lax.ppermute(far, ('tm', 'space'), [(k * count + i, (k ^ 1) * count + j)...]
    ppermute x1, waiting for transfers between devices: 0.42 us -> 0.01 us  [far_exchange(): lax.ppermute(far, ('tm', 'space'), [(k * count + i, (k ^ 1) * count + j)...]
  transfers between devices with their start and end apart: 12 -> 12, of which waited for: 3 -> 2; matrix products, arithmetic and copies ran while one was open for 0% -> 0% of each run, Pallas kernels for 16% -> 16%
where the time goes in v8:
time: 30.6 us; the launch traced here: 30.2 us
  starting transfers between devices  16.8 us (55%)
  Pallas kernels  7.79 us (25%)
  waiting for transfers between devices  4.93 us (16%)
  between operations  0.73 us (2%)
    ppermute x7, starting transfers between devices, swapped(): return lax.ppermute(value, 'tm', [(i, i ^ step) for i in range(count)])  8.16 us
    pallas_call x11, Pallas kernels, call(): pl.pallas_call(kernel, name=name, out_shape=outs, in_specs=in_specs or [V...  7.79 us
    ppermute x7, waiting for transfers between devices, swapped(): return lax.ppermute(value, 'tm', [(i, i ^ step) for i in range(count)])  4.92 us
    ppermute x1, starting transfers between devices, far_exchange(): lax.ppermute(far, ('tm', 'space'), [(k * count + i, (k ^ 1) * count + j)...  4.06 us
    ppermute x2, starting transfers between devices, far_exchange(): return lax.ppermute(far, 'space', pairs)  2.67 us
    ppermute x2, starting transfers between devices, near_exchange(): return lax.ppermute(near, 'space', pairs + [(j, i) for i, j in pairs])  1.87 us
  transfers between devices with their start and end apart: 12, of which 2 were waited for; matrix products, arithmetic and copies ran while one was open for 0% of the time, Pallas kernels for 16%

profile of v8, /device:TPU:1, one launch (start us, length us, event | category | flops | bytes accessed | tf_op | source)
XLA Modules:
  0.0 30.2 jit_solution(17881709035226367735)
XLA Ops:
  0.6 1.2 %ends.1 = (f32[1,80,128]{2,1,0:T(8,128)S(1)}, f32[1,80,128]{2,1,0:T(8,128)S(1)}, f32[2,5,64,256]{3,2,1,0:T(8,128)S(1)}) custom-call(f32[2,5,64,256]{3,2,1,0:T(8,128)} %bitcast.10), custom_call_target="tpu_custom_call" | custom-call | bytes 1392640 | tf_op jit(solution)/shard_map/ends/pallas_call | solution.py:472
  1.8 2.7 %collective-permute-start = (f32[1,80,128]{2,1,0:T(8,128)S(1)}, f32[1,80,128]{2,1,0:T(8,128)S(1)}, u32[]{:S(2)}, u32[]{:S(2)}) collective-permute-start(f32[1,80,128]{2,1,0:T(8,128)S(1)} %get-tuple-element.32), channel_id=1, source_target_pairs={{1,2},{3,0},{2,1},{0,3},{5,6},{7,4},{6,5},{4,7},{9,10},{11,8},{10,... | collective-permute-start | bytes 122888 | tf_op jit(solution)/shard_map/ppermute | solution.py:494
  4.5 0.0 collective-permute-start.1
  4.5 2.6 %first.1 = (f32[2,320,256]{2,1,0:T(8,128)S(1)}, bf16[320,800]{1,0:T(8,128)(2,1)S(1)}, bf16[2,320,80]{2,1,0:T(8,128)(2,1)S(1)}, f32[320,256]{1,0:T(8,128)S(1)}, f...) custom-call(f32[2,320,256]{2,1,0:T(8,128)S(1)} %bitcast.9, ...), custom_call_target="tpu_custom_call" | custom-call | flops 524288000 | bytes 4112384 | tf_op jit(solution)/shard_map/first/pallas_call | solution.py:472
  7.2 0.0 collective-permute-done.far_ref
  7.2 0.0 collective-permute-done.1.near_ref
  7.2 0.6 %carry.1 = (f32[2,320,256]{2,1,0:T(8,128)S(1)}, f32[80,256]{1,0:T(8,128)S(1)}, f32[80,256]{1,0:T(8,128)S(1)}, f32[80,256]{1,0:T(8,128)S(1)}, f32[80,256]{1,0:T(8,128)S(1)}, /*index=5*/f32[2,80,128]{2,1,0:T(8,128)S(1)}) custom-call(f32[2,320,256]{2,1,0:T(8,128)S(1)} %get-tuple-element.31.part_ref, f32[1,80,128]{2,1,0:T(8,128)S(1)} %collective-permute-done.far_ref, ...), custom_call_target="tpu_custom_call" | custom-call | bytes 2250752 | tf_op jit(solution)/shard_map/carry/pallas_call | solution.py:472
  7.7 1.3 %collective-permute-start.2 = (f32[80,256]{1,0:T(8,128)S(1)}, f32[80,256]{1,0:T(8,128)S(1)}, u32[]{:S(2)}, u32[]{:S(2)}) collective-permute-start(f32[80,256]{1,0:T(8,128)S(1)} %get-tuple-element.40), channel_id=1, source_target_pairs={{0,4},{4,0},{8,12},{12,8},{1,5},{5,1},{9,13},{13,9},{2,6},{6,2},{1... | collective-permute-start | bytes 245768 | tf_op jit(solution)/shard_map/ppermute | solution.py:504
  9.1 0.2 collective-permute-start.5
  9.3 1.8 %collective-permute-done.2.other_ref = f32[80,256]{1,0:T(8,128)S(1)} collective-permute-done((f32[80,256]{1,0:T(8,128)S(1)}, f32[80,256]{1,0:T(8,128)S(1)}, u32[]{:S(2)}, u32[]{:S(2)}) %collective-permute-start.2) | collective-permute-done | bytes 81952 | tf_op jit(solution)/shard_map/ppermute | solution.py:504
  11.1 2.4 %collective-permute-start.3 = (f32[80,256]{1,0:T(8,128)S(1)}, f32[80,256]{1,0:T(8,128)S(1)}, u32[]{:S(2)}, u32[]{:S(2)}) collective-permute-start(f32[80,256]{1,0:T(8,128)S(1)} %pair.2.here_ref), channel_id=1, source_target_pairs={{0,8},{4,12},{8,0},{12,4},{1,9},{5,13},{9,1},{13,5},{2,10},{6,14},... | collective-permute-start | bytes 245768 | tf_op jit(solution)/shard_map/ppermute | solution.py:504
  13.5 0.0 collective-permute-done.5.other_ref
  13.5 2.3 %collective-permute-start.6 = (f32[80,256]{1,0:T(8,128)S(1)}, f32[80,256]{1,0:T(8,128)S(1)}, u32[]{:S(2)}, u32[]{:S(2)}) collective-permute-start(f32[80,256]{1,0:T(8,128)S(1)} %pair.3.here_ref), channel_id=1, source_target_pairs={{0,8},{4,12},{8,0},{12,4},{1,9},{5,13},{9,1},{13,5},{2,10},{6,14},... | collective-permute-start | bytes 245768 | tf_op jit(solution)/shard_map/ppermute | solution.py:504
  15.8 1.0 %collective-permute-start.8 = (f32[2,80,128]{2,1,0:T(8,128)S(1)}, f32[2,80,128]{2,1,0:T(8,128)S(1)}, u32[]{:S(2)}, u32[]{:S(2)}) collective-permute-start(f32[2,80,128]{2,1,0:T(8,128)S(1)} %get-tuple-element.54.edges_ref), channel_id=1, source_target_pairs={{0,4},{4,0},{8,12},{12,8},{1,5},{5,1},{9,13},{13,9},{2,6},{6,2},{1... | collective-permute-start | bytes 245768 | tf_op jit(solution)/shard_map/ppermute | solution.py:504
  16.7 0.0 collective-permute-done.3.there_ref
  16.8 0.6 %collective-permute-start.4 = (f32[80,256]{1,0:T(8,128)S(1)}, f32[80,256]{1,0:T(8,128)S(1)}, u32[]{:S(2)}, u32[]{:S(2)}) collective-permute-start(f32[80,256]{1,0:T(8,128)S(1)} %get-tuple-element.42.pass0_ref), channel_id=1, source_target_pairs={{0,4},{4,0},{8,12},{12,8},{1,5},{5,1},{9,13},{13,9},{2,6},{6,2},{1... | collective-permute-start | bytes 245768 | tf_op jit(solution)/shard_map/ppermute | solution.py:504
  17.4 3.1 %collective-permute-done.6.there_ref = f32[80,256]{1,0:T(8,128)S(1)} collective-permute-done((f32[80,256]{1,0:T(8,128)S(1)}, f32[80,256]{1,0:T(8,128)S(1)}, u32[]{:S(2)}, u32[]{:S(2)}) %collective-permute-start.6) | collective-permute-done | bytes 81952 | tf_op jit(solution)/shard_map/ppermute | solution.py:504
  20.5 0.5 %collective-permute-start.7 = (f32[80,256]{1,0:T(8,128)S(1)}, f32[80,256]{1,0:T(8,128)S(1)}, u32[]{:S(2)}, u32[]{:S(2)}) collective-permute-start(f32[80,256]{1,0:T(8,128)S(1)} %get-tuple-element.46.pass3_ref), channel_id=1, source_target_pairs={{0,4},{4,0},{8,12},{12,8},{1,5},{5,1},{9,13},{13,9},{2,6},{6,2},{1... | collective-permute-start | bytes 245768 | tf_op jit(solution)/shard_map/ppermute | solution.py:504
  21.0 0.0 collective-permute-done.8.others_ref
  21.0 0.2 spread.1
  21.1 4.1 %collective-permute-start.9 = (f32[1,80,128]{2,1,0:T(8,128)S(1)}, f32[1,80,128]{2,1,0:T(8,128)S(1)}, u32[]{:S(2)}, u32[]{:S(2)}) collective-permute-start(f32[1,80,128]{2,1,0:T(8,128)S(1)} %get-tuple-element.55), channel_id=1, source_target_pairs={{1,6},{3,4},{2,5},{0,7},{5,2},{7,0},{6,1},{4,3},{9,14},{11,12},{10... | collective-permute-start | bytes 122888 | tf_op jit(solution)/shard_map/ppermute | solution.py:496
  25.2 0.0 collective-permute-start.10
  25.2 0.0 collective-permute-done.4.refs_1_
  25.2 0.0 collective-permute-done.7.refs_3_
  25.2 0.2 solve.1
  25.4 1.9 %collective-permute-start.11 = (f32[1,80,128]{2,1,0:T(8,128)S(1)}, f32[1,80,128]{2,1,0:T(8,128)S(1)}, u32[]{:S(2)}, u32[]{:S(2)}) collective-permute-start(f32[1,80,128]{2,1,0:T(8,128)S(1)} %get-tuple-element.57), channel_id=1, source_target_pairs={{0,1},{2,3},{1,0},{3,2},{4,5},{6,7},{5,4},{7,6},{8,9},{10,11},{9,8... | collective-permute-start | bytes 122888 | tf_op jit(solution)/shard_map/ppermute | solution.py:486
  27.3 1.7 %second.1 = (f32[2,320,256]{2,1,0:T(8,128)S(1)}, f32[2,320,256]{2,1,0:T(8,128)}) custom-call(f32[2,320,256]{2,1,0:T(8,128)S(1)} %get-tuple-element.48.state_ref, f32[5,64,256]{2,1,0:T(8,128)S(1)} %get-tuple-element.49.before_ref, f32[2,320,256]{2,1,0:T(8,128)S(1)} %get-tuple-element.50.forcing_ref, bf16[320,800]{1,0:T(8,128)(2,1)S(1)} %get-tuple-element.51.weights_ref, ...), custom_call_target="tpu_custom_call" | custom-call | flops 524288000 | bytes 3479552 | tf_op jit(solution)/shard_map/second/pallas_call | solution.py:472
  29.0 0.0 collective-permute-done.9.far_pass_ref
  29.0 0.0 collective-permute-done.10.far_ref
  29.0 0.0 collective-permute-done.11.near_ref
  29.0 1.2 %finish.1 = bf16[2,320,256]{2,1,0:T(8,128)(2,1)} custom-call(f32[2,320,256]{2,1,0:T(8,128)S(1)} %get-tuple-element.53.part_ref, f32[1,80,128]{2,1,0:T(8,128)S(1)} %collective-permute-done.9.far_pass_ref, f32[1,80,128]{2,1,0:T(8,128)S(1)} %collective-permute-done.10.far_ref, f32[1,80,128]{2,1,0:T(8,128)S(1)} %collective-permute-done.11.near_ref, ...), custom_call_target="tpu_custom_call" | custom-call | bytes 1226752 | tf_op jit(solution)/shard_map/finish/pallas_call | solution.py:472
  (4 shorter events, 0.1 us)
Async XLA Ops:
  1.8 5.3 %collective-permute-start = (f32[1,80,128]{2,1,0:T(8,128)S(1)}, f32[1,80,128]{2,1,0:T(8,128)S(1)}, u32[]{:S(2)}, u32[]{:S(2)}) collective-permute-start(f32[1,80,128]{2,1,0:T(8,128)S(1)} %get-tuple-element.32), channel_id=1, source_target_pairs={{1,2},{3,0},{2,1},{0,3},{5,6},{7,4},{6,5},{4,7},{9,10},{11,8},{10,... | collective-permute-start | bytes 122888 | tf_op jit(solution)/shard_map/ppermute | solution.py:494
  4.5 2.7 %collective-permute-start.1 = (f32[1,80,128]{2,1,0:T(8,128)S(1)}, f32[1,80,128]{2,1,0:T(8,128)S(1)}, u32[]{:S(2)}, u32[]{:S(2)}) collective-permute-start(f32[1,80,128]{2,1,0:T(8,128)S(1)} %get-tuple-element.33), channel_id=1, source_target_pairs={{0,1},{2,3},{1,0},{3,2},{4,5},{6,7},{5,4},{7,6},{8,9},{10,11},{9,8... | collective-permute-start | bytes 122888 | tf_op jit(solution)/shard_map/ppermute | solution.py:486
  7.7 3.3 %collective-permute-start.2 = (f32[80,256]{1,0:T(8,128)S(1)}, f32[80,256]{1,0:T(8,128)S(1)}, u32[]{:S(2)}, u32[]{:S(2)}) collective-permute-start(f32[80,256]{1,0:T(8,128)S(1)} %get-tuple-element.40), channel_id=1, source_target_pairs={{0,4},{4,0},{8,12},{12,8},{1,5},{5,1},{9,13},{13,9},{2,6},{6,2},{1... | collective-permute-start | bytes 245768 | tf_op jit(solution)/shard_map/ppermute | solution.py:504
  9.1 4.4 %collective-permute-start.5 = (f32[80,256]{1,0:T(8,128)S(1)}, f32[80,256]{1,0:T(8,128)S(1)}, u32[]{:S(2)}, u32[]{:S(2)}) collective-permute-start(f32[80,256]{1,0:T(8,128)S(1)} %get-tuple-element.44), channel_id=1, source_target_pairs={{0,4},{4,0},{8,12},{12,8},{1,5},{5,1},{9,13},{13,9},{2,6},{6,2},{1... | collective-permute-start | bytes 245768 | tf_op jit(solution)/shard_map/ppermute | solution.py:504
  11.1 5.6 %collective-permute-start.3 = (f32[80,256]{1,0:T(8,128)S(1)}, f32[80,256]{1,0:T(8,128)S(1)}, u32[]{:S(2)}, u32[]{:S(2)}) collective-permute-start(f32[80,256]{1,0:T(8,128)S(1)} %pair.2.here_ref), channel_id=1, source_target_pairs={{0,8},{4,12},{8,0},{12,4},{1,9},{5,13},{9,1},{13,5},{2,10},{6,14},... | collective-permute-start | bytes 245768 | tf_op jit(solution)/shard_map/ppermute | solution.py:504
  13.5 6.9 %collective-permute-start.6 = (f32[80,256]{1,0:T(8,128)S(1)}, f32[80,256]{1,0:T(8,128)S(1)}, u32[]{:S(2)}, u32[]{:S(2)}) collective-permute-start(f32[80,256]{1,0:T(8,128)S(1)} %pair.3.here_ref), channel_id=1, source_target_pairs={{0,8},{4,12},{8,0},{12,4},{1,9},{5,13},{9,1},{13,5},{2,10},{6,14},... | collective-permute-start | bytes 245768 | tf_op jit(solution)/shard_map/ppermute | solution.py:504
  15.8 5.2 %collective-permute-start.8 = (f32[2,80,128]{2,1,0:T(8,128)S(1)}, f32[2,80,128]{2,1,0:T(8,128)S(1)}, u32[]{:S(2)}, u32[]{:S(2)}) collective-permute-start(f32[2,80,128]{2,1,0:T(8,128)S(1)} %get-tuple-element.54.edges_ref), channel_id=1, source_target_pairs={{0,4},{4,0},{8,12},{12,8},{1,5},{5,1},{9,13},{13,9},{2,6},{6,2},{1... | collective-permute-start | bytes 245768 | tf_op jit(solution)/shard_map/ppermute | solution.py:504
  16.8 8.4 %collective-permute-start.4 = (f32[80,256]{1,0:T(8,128)S(1)}, f32[80,256]{1,0:T(8,128)S(1)}, u32[]{:S(2)}, u32[]{:S(2)}) collective-permute-start(f32[80,256]{1,0:T(8,128)S(1)} %get-tuple-element.42.pass0_ref), channel_id=1, source_target_pairs={{0,4},{4,0},{8,12},{12,8},{1,5},{5,1},{9,13},{13,9},{2,6},{6,2},{1... | collective-permute-start | bytes 245768 | tf_op jit(solution)/shard_map/ppermute | solution.py:504
  20.5 4.7 %collective-permute-start.7 = (f32[80,256]{1,0:T(8,128)S(1)}, f32[80,256]{1,0:T(8,128)S(1)}, u32[]{:S(2)}, u32[]{:S(2)}) collective-permute-start(f32[80,256]{1,0:T(8,128)S(1)} %get-tuple-element.46.pass3_ref), channel_id=1, source_target_pairs={{0,4},{4,0},{8,12},{12,8},{1,5},{5,1},{9,13},{13,9},{2,6},{6,2},{1... | collective-permute-start | bytes 245768 | tf_op jit(solution)/shard_map/ppermute | solution.py:504
  21.1 7.8 %collective-permute-start.9 = (f32[1,80,128]{2,1,0:T(8,128)S(1)}, f32[1,80,128]{2,1,0:T(8,128)S(1)}, u32[]{:S(2)}, u32[]{:S(2)}) collective-permute-start(f32[1,80,128]{2,1,0:T(8,128)S(1)} %get-tuple-element.55), channel_id=1, source_target_pairs={{1,6},{3,4},{2,5},{0,7},{5,2},{7,0},{6,1},{4,3},{9,14},{11,12},{10... | collective-permute-start | bytes 122888 | tf_op jit(solution)/shard_map/ppermute | solution.py:496
  25.2 3.8 %collective-permute-start.10 = (f32[1,80,128]{2,1,0:T(8,128)S(1)}, f32[1,80,128]{2,1,0:T(8,128)S(1)}, u32[]{:S(2)}, u32[]{:S(2)}) collective-permute-start(f32[1,80,128]{2,1,0:T(8,128)S(1)} %get-tuple-element.56), channel_id=1, source_target_pairs={{1,2},{3,0},{2,1},{0,3},{5,6},{7,4},{6,5},{4,7},{9,10},{11,8},{10,... | collective-permute-start | bytes 122888 | tf_op jit(solution)/shard_map/ppermute | solution.py:494
  25.4 3.6 %collective-permute-start.11 = (f32[1,80,128]{2,1,0:T(8,128)S(1)}, f32[1,80,128]{2,1,0:T(8,128)S(1)}, u32[]{:S(2)}, u32[]{:S(2)}) collective-permute-start(f32[1,80,128]{2,1,0:T(8,128)S(1)} %get-tuple-element.57), channel_id=1, source_target_pairs={{0,1},{2,3},{1,0},{3,2},{4,5},{6,7},{5,4},{7,6},{8,9},{10,11},{9,8... | collective-permute-start | bytes 122888 | tf_op jit(solution)/shard_map/ppermute | solution.py:486

commit v9 on v8

--- a/solution.py
+++ b/solution.py
@@ -171,7 +171,14 @@
             taken = gather_lanes(halo, target + HALF * (item % 2))
             pieces.append(split(jnp.where(use, oriented(taken, plan), 0.0)))
         both = jnp.concatenate([p[0] for p in pieces] + [p[1] for p in pieces], axis=1)
-        product = jnp.dot(rim_weights_ref[face], both, preferred_element_type=jnp.float32)
+        middle = rim_weights_ref.shape[1] // 2
+        product = jnp.concatenate(
+            [
+                jnp.dot(rim_weights_ref[face, part], both, preferred_element_type=jnp.float32)
+                for part in (slice(0, middle), slice(middle, 2 * middle))
+            ],
+            axis=0,
+        )
         wide = slices * LANES
         result.append(product[:, :wide] + product[:, wide:])
     return result

time: 30.6 us -> 30.5 us (level)
  no operation moved by 1% of the time
where the time goes in v9:
time: 30.5 us; the launch traced here: 30.1 us
  starting transfers between devices  16.7 us (55%)
  Pallas kernels  7.67 us (25%)
  waiting for transfers between devices  4.94 us (16%)
  between operations  0.73 us (2%)
    ppermute x7, starting transfers between devices, swapped(): return lax.ppermute(value, 'tm', [(i, i ^ step) for i in range(count)])  8.16 us
    pallas_call x11, Pallas kernels, call(): pl.pallas_call(kernel, name=name, out_shape=outs, in_specs=in_specs or [V...  7.67 us
    ppermute x7, waiting for transfers between devices, swapped(): return lax.ppermute(value, 'tm', [(i, i ^ step) for i in range(count)])  4.93 us
    ppermute x1, starting transfers between devices, far_exchange(): lax.ppermute(far, ('tm', 'space'), [(k * count + i, (k ^ 1) * count + j)...  4.04 us
    ppermute x2, starting transfers between devices, far_exchange(): return lax.ppermute(far, 'space', pairs)  2.67 us
    ppermute x2, starting transfers between devices, near_exchange(): return lax.ppermute(near, 'space', pairs + [(j, i) for i, j in pairs])  1.87 us
  transfers between devices with their start and end apart: 12, of which 2 were waited for; matrix products, arithmetic and copies ran while one was open for 0% of the time, Pallas kernels for 16%

profile of v9, /device:TPU:1, one launch (start us, length us, event | category | flops | bytes accessed | tf_op | source)
XLA Modules:
  0.0 30.1 jit_solution(12393240685361386873)
XLA Ops:
  0.6 1.2 %ends.1 = (f32[1,80,128]{2,1,0:T(8,128)S(1)}, f32[1,80,128]{2,1,0:T(8,128)S(1)}, f32[2,5,64,256]{3,2,1,0:T(8,128)S(1)}) custom-call(f32[2,5,64,256]{3,2,1,0:T(8,128)} %bitcast.10), custom_call_target="tpu_custom_call" | custom-call | bytes 1392640 | tf_op jit(solution)/shard_map/ends/pallas_call | solution.py:479
  1.8 2.7 %collective-permute-start = (f32[1,80,128]{2,1,0:T(8,128)S(1)}, f32[1,80,128]{2,1,0:T(8,128)S(1)}, u32[]{:S(2)}, u32[]{:S(2)}) collective-permute-start(f32[1,80,128]{2,1,0:T(8,128)S(1)} %get-tuple-element.32), channel_id=1, source_target_pairs={{1,2},{3,0},{2,1},{0,3},{5,6},{7,4},{6,5},{4,7},{9,10},{11,8},{10,... | collective-permute-start | bytes 122888 | tf_op jit(solution)/shard_map/ppermute | solution.py:501
  4.5 0.0 collective-permute-start.1
  4.5 2.6 %first.1 = (f32[2,320,256]{2,1,0:T(8,128)S(1)}, bf16[320,800]{1,0:T(8,128)(2,1)S(1)}, bf16[2,320,80]{2,1,0:T(8,128)(2,1)S(1)}, f32[320,256]{1,0:T(8,128)S(1)}, f...) custom-call(f32[2,320,256]{2,1,0:T(8,128)S(1)} %bitcast.9, ...), custom_call_target="tpu_custom_call" | custom-call | flops 524288000 | bytes 4112384 | tf_op jit(solution)/shard_map/first/pallas_call | solution.py:479
  7.2 0.0 collective-permute-done.far_ref
  7.2 0.0 collective-permute-done.1.near_ref
  7.2 0.5 %carry.1 = (f32[2,320,256]{2,1,0:T(8,128)S(1)}, f32[80,256]{1,0:T(8,128)S(1)}, f32[80,256]{1,0:T(8,128)S(1)}, f32[80,256]{1,0:T(8,128)S(1)}, f32[80,256]{1,0:T(8,128)S(1)}, /*index=5*/f32[2,80,128]{2,1,0:T(8,128)S(1)}) custom-call(f32[2,320,256]{2,1,0:T(8,128)S(1)} %get-tuple-element.31.part_ref, f32[1,80,128]{2,1,0:T(8,128)S(1)} %collective-permute-done.far_ref, ...), custom_call_target="tpu_custom_call" | custom-call | bytes 2250752 | tf_op jit(solution)/shard_map/carry/pallas_call | solution.py:479
  7.7 1.3 %collective-permute-start.2 = (f32[80,256]{1,0:T(8,128)S(1)}, f32[80,256]{1,0:T(8,128)S(1)}, u32[]{:S(2)}, u32[]{:S(2)}) collective-permute-start(f32[80,256]{1,0:T(8,128)S(1)} %get-tuple-element.40), channel_id=1, source_target_pairs={{0,4},{4,0},{8,12},{12,8},{1,5},{5,1},{9,13},{13,9},{2,6},{6,2},{1... | collective-permute-start | bytes 245768 | tf_op jit(solution)/shard_map/ppermute | solution.py:511
  9.0 0.2 collective-permute-start.5
  9.2 1.8 %collective-permute-done.2.other_ref = f32[80,256]{1,0:T(8,128)S(1)} collective-permute-done((f32[80,256]{1,0:T(8,128)S(1)}, f32[80,256]{1,0:T(8,128)S(1)}, u32[]{:S(2)}, u32[]{:S(2)}) %collective-permute-start.2) | collective-permute-done | bytes 81952 | tf_op jit(solution)/shard_map/ppermute | solution.py:511
  11.1 2.4 %collective-permute-start.3 = (f32[80,256]{1,0:T(8,128)S(1)}, f32[80,256]{1,0:T(8,128)S(1)}, u32[]{:S(2)}, u32[]{:S(2)}) collective-permute-start(f32[80,256]{1,0:T(8,128)S(1)} %pair.2.here_ref), channel_id=1, source_target_pairs={{0,8},{4,12},{8,0},{12,4},{1,9},{5,13},{9,1},{13,5},{2,10},{6,14},... | collective-permute-start | bytes 245768 | tf_op jit(solution)/shard_map/ppermute | solution.py:511
  13.4 0.0 collective-permute-done.5.other_ref
  13.5 2.3 %collective-permute-start.6 = (f32[80,256]{1,0:T(8,128)S(1)}, f32[80,256]{1,0:T(8,128)S(1)}, u32[]{:S(2)}, u32[]{:S(2)}) collective-permute-start(f32[80,256]{1,0:T(8,128)S(1)} %pair.3.here_ref), channel_id=1, source_target_pairs={{0,8},{4,12},{8,0},{12,4},{1,9},{5,13},{9,1},{13,5},{2,10},{6,14},... | collective-permute-start | bytes 245768 | tf_op jit(solution)/shard_map/ppermute | solution.py:511
  15.7 1.0 %collective-permute-start.8 = (f32[2,80,128]{2,1,0:T(8,128)S(1)}, f32[2,80,128]{2,1,0:T(8,128)S(1)}, u32[]{:S(2)}, u32[]{:S(2)}) collective-permute-start(f32[2,80,128]{2,1,0:T(8,128)S(1)} %get-tuple-element.54.edges_ref), channel_id=1, source_target_pairs={{0,4},{4,0},{8,12},{12,8},{1,5},{5,1},{9,13},{13,9},{2,6},{6,2},{1... | collective-permute-start | bytes 245768 | tf_op jit(solution)/shard_map/ppermute | solution.py:511
  16.7 0.0 collective-permute-done.3.there_ref
  16.8 0.6 %collective-permute-start.4 = (f32[80,256]{1,0:T(8,128)S(1)}, f32[80,256]{1,0:T(8,128)S(1)}, u32[]{:S(2)}, u32[]{:S(2)}) collective-permute-start(f32[80,256]{1,0:T(8,128)S(1)} %get-tuple-element.42.pass0_ref), channel_id=1, source_target_pairs={{0,4},{4,0},{8,12},{12,8},{1,5},{5,1},{9,13},{13,9},{2,6},{6,2},{1... | collective-permute-start | bytes 245768 | tf_op jit(solution)/shard_map/ppermute | solution.py:511
  17.3 3.1 %collective-permute-done.6.there_ref = f32[80,256]{1,0:T(8,128)S(1)} collective-permute-done((f32[80,256]{1,0:T(8,128)S(1)}, f32[80,256]{1,0:T(8,128)S(1)}, u32[]{:S(2)}, u32[]{:S(2)}) %collective-permute-start.6) | collective-permute-done | bytes 81952 | tf_op jit(solution)/shard_map/ppermute | solution.py:511
  20.4 0.5 %collective-permute-start.7 = (f32[80,256]{1,0:T(8,128)S(1)}, f32[80,256]{1,0:T(8,128)S(1)}, u32[]{:S(2)}, u32[]{:S(2)}) collective-permute-start(f32[80,256]{1,0:T(8,128)S(1)} %get-tuple-element.46.pass3_ref), channel_id=1, source_target_pairs={{0,4},{4,0},{8,12},{12,8},{1,5},{5,1},{9,13},{13,9},{2,6},{6,2},{1... | collective-permute-start | bytes 245768 | tf_op jit(solution)/shard_map/ppermute | solution.py:511
  20.9 0.0 collective-permute-done.8.others_ref
  20.9 0.2 spread.1
  21.1 4.0 %collective-permute-start.9 = (f32[1,80,128]{2,1,0:T(8,128)S(1)}, f32[1,80,128]{2,1,0:T(8,128)S(1)}, u32[]{:S(2)}, u32[]{:S(2)}) collective-permute-start(f32[1,80,128]{2,1,0:T(8,128)S(1)} %get-tuple-element.55), channel_id=1, source_target_pairs={{1,6},{3,4},{2,5},{0,7},{5,2},{7,0},{6,1},{4,3},{9,14},{11,12},{10... | collective-permute-start | bytes 122888 | tf_op jit(solution)/shard_map/ppermute | solution.py:503
  25.2 0.0 collective-permute-start.10
  25.2 0.0 collective-permute-done.4.refs_1_
  25.2 0.0 collective-permute-done.7.refs_3_
  25.2 0.2 solve.1
  25.4 1.9 %collective-permute-start.11 = (f32[1,80,128]{2,1,0:T(8,128)S(1)}, f32[1,80,128]{2,1,0:T(8,128)S(1)}, u32[]{:S(2)}, u32[]{:S(2)}) collective-permute-start(f32[1,80,128]{2,1,0:T(8,128)S(1)} %get-tuple-element.57), channel_id=1, source_target_pairs={{0,1},{2,3},{1,0},{3,2},{4,5},{6,7},{5,4},{7,6},{8,9},{10,11},{9,8... | collective-permute-start | bytes 122888 | tf_op jit(solution)/shard_map/ppermute | solution.py:493
  27.3 1.7 %second.1 = (f32[2,320,256]{2,1,0:T(8,128)S(1)}, f32[2,320,256]{2,1,0:T(8,128)}) custom-call(f32[2,320,256]{2,1,0:T(8,128)S(1)} %get-tuple-element.48.state_ref, f32[5,64,256]{2,1,0:T(8,128)S(1)} %get-tuple-element.49.before_ref, f32[2,320,256]{2,1,0:T(8,128)S(1)} %get-tuple-element.50.forcing_ref, bf16[320,800]{1,0:T(8,128)(2,1)S(1)} %get-tuple-element.51.weights_ref, ...), custom_call_target="tpu_custom_call" | custom-call | flops 524288000 | bytes 3479552 | tf_op jit(solution)/shard_map/second/pallas_call | solution.py:479
  28.9 0.0 collective-permute-done.9.far_pass_ref
  28.9 0.0 collective-permute-done.10.far_ref
  29.0 0.0 collective-permute-done.11.near_ref
  29.0 1.1 %finish.1 = bf16[2,320,256]{2,1,0:T(8,128)(2,1)} custom-call(f32[2,320,256]{2,1,0:T(8,128)S(1)} %get-tuple-element.53.part_ref, f32[1,80,128]{2,1,0:T(8,128)S(1)} %collective-permute-done.9.far_pass_ref, f32[1,80,128]{2,1,0:T(8,128)S(1)} %collective-permute-done.10.far_ref, f32[1,80,128]{2,1,0:T(8,128)S(1)} %collective-permute-done.11.near_ref, ...), custom_call_target="tpu_custom_call" | custom-call | bytes 1226752 | tf_op jit(solution)/shard_map/finish/pallas_call | solution.py:479
  (4 shorter events, 0.1 us)
Async XLA Ops:
  1.8 5.3 %collective-permute-start = (f32[1,80,128]{2,1,0:T(8,128)S(1)}, f32[1,80,128]{2,1,0:T(8,128)S(1)}, u32[]{:S(2)}, u32[]{:S(2)}) collective-permute-start(f32[1,80,128]{2,1,0:T(8,128)S(1)} %get-tuple-element.32), channel_id=1, source_target_pairs={{1,2},{3,0},{2,1},{0,3},{5,6},{7,4},{6,5},{4,7},{9,10},{11,8},{10,... | collective-permute-start | bytes 122888 | tf_op jit(solution)/shard_map/ppermute | solution.py:501
  4.5 2.7 %collective-permute-start.1 = (f32[1,80,128]{2,1,0:T(8,128)S(1)}, f32[1,80,128]{2,1,0:T(8,128)S(1)}, u32[]{:S(2)}, u32[]{:S(2)}) collective-permute-start(f32[1,80,128]{2,1,0:T(8,128)S(1)} %get-tuple-element.33), channel_id=1, source_target_pairs={{0,1},{2,3},{1,0},{3,2},{4,5},{6,7},{5,4},{7,6},{8,9},{10,11},{9,8... | collective-permute-start | bytes 122888 | tf_op jit(solution)/shard_map/ppermute | solution.py:493
  7.7 3.3 %collective-permute-start.2 = (f32[80,256]{1,0:T(8,128)S(1)}, f32[80,256]{1,0:T(8,128)S(1)}, u32[]{:S(2)}, u32[]{:S(2)}) collective-permute-start(f32[80,256]{1,0:T(8,128)S(1)} %get-tuple-element.40), channel_id=1, source_target_pairs={{0,4},{4,0},{8,12},{12,8},{1,5},{5,1},{9,13},{13,9},{2,6},{6,2},{1... | collective-permute-start | bytes 245768 | tf_op jit(solution)/shard_map/ppermute | solution.py:511
  9.0 4.4 %collective-permute-start.5 = (f32[80,256]{1,0:T(8,128)S(1)}, f32[80,256]{1,0:T(8,128)S(1)}, u32[]{:S(2)}, u32[]{:S(2)}) collective-permute-start(f32[80,256]{1,0:T(8,128)S(1)} %get-tuple-element.44), channel_id=1, source_target_pairs={{0,4},{4,0},{8,12},{12,8},{1,5},{5,1},{9,13},{13,9},{2,6},{6,2},{1... | collective-permute-start | bytes 245768 | tf_op jit(solution)/shard_map/ppermute | solution.py:511
  11.1 5.6 %collective-permute-start.3 = (f32[80,256]{1,0:T(8,128)S(1)}, f32[80,256]{1,0:T(8,128)S(1)}, u32[]{:S(2)}, u32[]{:S(2)}) collective-permute-start(f32[80,256]{1,0:T(8,128)S(1)} %pair.2.here_ref), channel_id=1, source_target_pairs={{0,8},{4,12},{8,0},{12,4},{1,9},{5,13},{9,1},{13,5},{2,10},{6,14},... | collective-permute-start | bytes 245768 | tf_op jit(solution)/shard_map/ppermute | solution.py:511
  13.5 6.9 %collective-permute-start.6 = (f32[80,256]{1,0:T(8,128)S(1)}, f32[80,256]{1,0:T(8,128)S(1)}, u32[]{:S(2)}, u32[]{:S(2)}) collective-permute-start(f32[80,256]{1,0:T(8,128)S(1)} %pair.3.here_ref), channel_id=1, source_target_pairs={{0,8},{4,12},{8,0},{12,4},{1,9},{5,13},{9,1},{13,5},{2,10},{6,14},... | collective-permute-start | bytes 245768 | tf_op jit(solution)/shard_map/ppermute | solution.py:511
  15.7 5.2 %collective-permute-start.8 = (f32[2,80,128]{2,1,0:T(8,128)S(1)}, f32[2,80,128]{2,1,0:T(8,128)S(1)}, u32[]{:S(2)}, u32[]{:S(2)}) collective-permute-start(f32[2,80,128]{2,1,0:T(8,128)S(1)} %get-tuple-element.54.edges_ref), channel_id=1, source_target_pairs={{0,4},{4,0},{8,12},{12,8},{1,5},{5,1},{9,13},{13,9},{2,6},{6,2},{1... | collective-permute-start | bytes 245768 | tf_op jit(solution)/shard_map/ppermute | solution.py:511
  16.8 8.4 %collective-permute-start.4 = (f32[80,256]{1,0:T(8,128)S(1)}, f32[80,256]{1,0:T(8,128)S(1)}, u32[]{:S(2)}, u32[]{:S(2)}) collective-permute-start(f32[80,256]{1,0:T(8,128)S(1)} %get-tuple-element.42.pass0_ref), channel_id=1, source_target_pairs={{0,4},{4,0},{8,12},{12,8},{1,5},{5,1},{9,13},{13,9},{2,6},{6,2},{1... | collective-permute-start | bytes 245768 | tf_op jit(solution)/shard_map/ppermute | solution.py:511
  20.4 4.7 %collective-permute-start.7 = (f32[80,256]{1,0:T(8,128)S(1)}, f32[80,256]{1,0:T(8,128)S(1)}, u32[]{:S(2)}, u32[]{:S(2)}) collective-permute-start(f32[80,256]{1,0:T(8,128)S(1)} %get-tuple-element.46.pass3_ref), channel_id=1, source_target_pairs={{0,4},{4,0},{8,12},{12,8},{1,5},{5,1},{9,13},{13,9},{2,6},{6,2},{1... | collective-permute-start | bytes 245768 | tf_op jit(solution)/shard_map/ppermute | solution.py:511
  21.1 7.8 %collective-permute-start.9 = (f32[1,80,128]{2,1,0:T(8,128)S(1)}, f32[1,80,128]{2,1,0:T(8,128)S(1)}, u32[]{:S(2)}, u32[]{:S(2)}) collective-permute-start(f32[1,80,128]{2,1,0:T(8,128)S(1)} %get-tuple-element.55), channel_id=1, source_target_pairs={{1,6},{3,4},{2,5},{0,7},{5,2},{7,0},{6,1},{4,3},{9,14},{11,12},{10... | collective-permute-start | bytes 122888 | tf_op jit(solution)/shard_map/ppermute | solution.py:503
  25.2 3.8 %collective-permute-start.10 = (f32[1,80,128]{2,1,0:T(8,128)S(1)}, f32[1,80,128]{2,1,0:T(8,128)S(1)}, u32[]{:S(2)}, u32[]{:S(2)}) collective-permute-start(f32[1,80,128]{2,1,0:T(8,128)S(1)} %get-tuple-element.56), channel_id=1, source_target_pairs={{1,2},{3,0},{2,1},{0,3},{5,6},{7,4},{6,5},{4,7},{9,10},{11,8},{10,... | collective-permute-start | bytes 122888 | tf_op jit(solution)/shard_map/ppermute | solution.py:501
  25.4 3.6 %collective-permute-start.11 = (f32[1,80,128]{2,1,0:T(8,128)S(1)}, f32[1,80,128]{2,1,0:T(8,128)S(1)}, u32[]{:S(2)}, u32[]{:S(2)}) collective-permute-start(f32[1,80,128]{2,1,0:T(8,128)S(1)} %get-tuple-element.57), channel_id=1, source_target_pairs={{0,1},{2,3},{1,0},{3,2},{4,5},{6,7},{5,4},{7,6},{8,9},{10,11},{9,8... | collective-permute-start | bytes 122888 | tf_op jit(solution)/shard_map/ppermute | solution.py:493

commit v10 on v9

--- a/solution.py
+++ b/solution.py
@@ -143,10 +143,12 @@
                 stack[place : place + FACE, n * LANES : (n + 1) * LANES] = high
                 stack[place : place + FACE, wide + n * LANES : wide + (n + 1) * LANES] = low
     ahead()
-    image = jnp.dot(weights_ref[...], stack[:, 0:wide], preferred_element_type=jnp.float32)
-    return image + jnp.dot(
-        weights_ref[...], stack[:, wide:], preferred_element_type=jnp.float32
-    )
+    halves = []
+    for part in (slice(0, rows // 2), slice(rows // 2, rows)):
+        image = jnp.dot(weights_ref[part], stack[:, 0:wide], preferred_element_type=jnp.float32)
+        low = jnp.dot(weights_ref[part], stack[:, wide:], preferred_element_type=jnp.float32)
+        halves.append(image + low)
+    return jnp.concatenate(halves, axis=0)
 
 
 def even_place():

time: 30.5 us -> 30.6 us (level)
  the two profiles are of different devices: /device:TPU:1 before, /device:TPU:19 now
where the time goes in v10:
time: 30.6 us; the launch traced here: 30.4 us
  starting transfers between devices  16.3 us (53%)
  Pallas kernels  7.57 us (25%)
  waiting for transfers between devices  5.84 us (19%)
  between operations  0.72 us (2%)
    ppermute x7, starting transfers between devices, swapped(): return lax.ppermute(value, 'tm', [(i, i ^ step) for i in range(count)])  9.63 us
    pallas_call x11, Pallas kernels, call(): pl.pallas_call(kernel, name=name, out_shape=outs, in_specs=in_specs or [V...  7.57 us
    ppermute x7, waiting for transfers between devices, swapped(): return lax.ppermute(value, 'tm', [(i, i ^ step) for i in range(count)])  5.03 us
    ppermute x2, starting transfers between devices, near_exchange(): return lax.ppermute(near, 'space', pairs + [(j, i) for i, j in pairs])  3.04 us
    ppermute x1, starting transfers between devices, far_exchange(): lax.ppermute(far, ('tm', 'space'), [(k * count + i, (k ^ 1) * count + j)...  2.73 us
    ppermute x2, starting transfers between devices, far_exchange(): return lax.ppermute(far, 'space', pairs)  0.88 us
    ppermute x2, waiting for transfers between devices, far_exchange(): return lax.ppermute(far, 'space', pairs)  0.8 us
  transfers between devices with their start and end apart: 12, of which 5 were waited for; matrix products, arithmetic and copies ran while one was open for 0% of the time, Pallas kernels for 16%

profile of v10, /device:TPU:19, one launch (start us, length us, event | category | flops | bytes accessed | tf_op | source)
XLA Modules:
  0.0 30.4 jit_solution(16926342651481640690)
XLA Ops:
  0.6 1.2 %ends.1 = (f32[1,80,128]{2,1,0:T(8,128)S(1)}, f32[1,80,128]{2,1,0:T(8,128)S(1)}, f32[2,5,64,256]{3,2,1,0:T(8,128)S(1)}) custom-call(f32[2,5,64,256]{3,2,1,0:T(8,128)} %bitcast.10), custom_call_target="tpu_custom_call" | custom-call | bytes 1392640 | tf_op jit(solution)/shard_map/ends/pallas_call | solution.py:481
  1.8 0.9 %collective-permute-start = (f32[1,80,128]{2,1,0:T(8,128)S(1)}, f32[1,80,128]{2,1,0:T(8,128)S(1)}, u32[]{:S(2)}, u32[]{:S(2)}) collective-permute-start(f32[1,80,128]{2,1,0:T(8,128)S(1)} %get-tuple-element.32), channel_id=1, source_target_pairs={{1,2},{3,0},{2,1},{0,3},{5,6},{7,4},{6,5},{4,7},{9,10},{11,8},{10,... | collective-permute-start | bytes 122888 | tf_op jit(solution)/shard_map/ppermute | solution.py:503
  2.7 0.0 collective-permute-start.1
  2.7 2.5 %first.1 = (f32[2,320,256]{2,1,0:T(8,128)S(1)}, bf16[320,800]{1,0:T(8,128)(2,1)S(1)}, bf16[2,320,80]{2,1,0:T(8,128)(2,1)S(1)}, f32[320,256]{1,0:T(8,128)S(1)}, f...) custom-call(f32[2,320,256]{2,1,0:T(8,128)S(1)} %bitcast.9, ...), custom_call_target="tpu_custom_call" | custom-call | flops 524288000 | bytes 4112384 | tf_op jit(solution)/shard_map/first/pallas_call | solution.py:481
  5.2 0.8 %collective-permute-done.far_ref = f32[1,80,128]{2,1,0:T(8,128)S(1)} collective-permute-done((f32[1,80,128]{2,1,0:T(8,128)S(1)}, f32[1,80,128]{2,1,0:T(8,128)S(1)}, u32[]{:S(2)}, u32[]{:S(2)}) %collective-permute-start) | collective-permute-done | bytes 40992 | tf_op jit(solution)/shard_map/ppermute | solution.py:503
  6.0 0.0 collective-permute-done.1.near_ref
  6.0 0.5 %carry.1 = (f32[2,320,256]{2,1,0:T(8,128)S(1)}, f32[80,256]{1,0:T(8,128)S(1)}, f32[80,256]{1,0:T(8,128)S(1)}, f32[80,256]{1,0:T(8,128)S(1)}, f32[80,256]{1,0:T(8,128)S(1)}, /*index=5*/f32[2,80,128]{2,1,0:T(8,128)S(1)}) custom-call(f32[2,320,256]{2,1,0:T(8,128)S(1)} %get-tuple-element.31.part_ref, f32[1,80,128]{2,1,0:T(8,128)S(1)} %collective-permute-done.far_ref, ...), custom_call_target="tpu_custom_call" | custom-call | bytes 2250752 | tf_op jit(solution)/shard_map/carry/pallas_call | solution.py:481
  6.6 1.3 %collective-permute-start.2 = (f32[80,256]{1,0:T(8,128)S(1)}, f32[80,256]{1,0:T(8,128)S(1)}, u32[]{:S(2)}, u32[]{:S(2)}) collective-permute-start(f32[80,256]{1,0:T(8,128)S(1)} %get-tuple-element.40), channel_id=1, source_target_pairs={{0,4},{4,0},{8,12},{12,8},{1,5},{5,1},{9,13},{13,9},{2,6},{6,2},{1... | collective-permute-start | bytes 245768 | tf_op jit(solution)/shard_map/ppermute | solution.py:513
  7.9 0.2 collective-permute-start.5
  8.1 2.2 %collective-permute-done.2.other_ref = f32[80,256]{1,0:T(8,128)S(1)} collective-permute-done((f32[80,256]{1,0:T(8,128)S(1)}, f32[80,256]{1,0:T(8,128)S(1)}, u32[]{:S(2)}, u32[]{:S(2)}) %collective-permute-start.2) | collective-permute-done | bytes 81952 | tf_op jit(solution)/shard_map/ppermute | solution.py:513
  10.3 0.1 collective-permute-start.3
  10.4 1.7 %collective-permute-done.5.other_ref = f32[80,256]{1,0:T(8,128)S(1)} collective-permute-done((f32[80,256]{1,0:T(8,128)S(1)}, f32[80,256]{1,0:T(8,128)S(1)}, u32[]{:S(2)}, u32[]{:S(2)}) %collective-permute-start.5) | collective-permute-done | bytes 81952 | tf_op jit(solution)/shard_map/ppermute | solution.py:513
  12.2 0.6 %collective-permute-start.6 = (f32[80,256]{1,0:T(8,128)S(1)}, f32[80,256]{1,0:T(8,128)S(1)}, u32[]{:S(2)}, u32[]{:S(2)}) collective-permute-start(f32[80,256]{1,0:T(8,128)S(1)} %pair.3.here_ref), channel_id=1, source_target_pairs={{0,8},{4,12},{8,0},{12,4},{1,9},{5,13},{9,1},{13,5},{2,10},{6,14},... | collective-permute-start | bytes 245768 | tf_op jit(solution)/shard_map/ppermute | solution.py:513
  12.8 1.3 %collective-permute-start.8 = (f32[2,80,128]{2,1,0:T(8,128)S(1)}, f32[2,80,128]{2,1,0:T(8,128)S(1)}, u32[]{:S(2)}, u32[]{:S(2)}) collective-permute-start(f32[2,80,128]{2,1,0:T(8,128)S(1)} %get-tuple-element.54.edges_ref), channel_id=1, source_target_pairs={{0,4},{4,0},{8,12},{12,8},{1,5},{5,1},{9,13},{13,9},{2,6},{6,2},{1... | collective-permute-start | bytes 245768 | tf_op jit(solution)/shard_map/ppermute | solution.py:513
  14.1 0.5 %collective-permute-done.3.there_ref = f32[80,256]{1,0:T(8,128)S(1)} collective-permute-done((f32[80,256]{1,0:T(8,128)S(1)}, f32[80,256]{1,0:T(8,128)S(1)}, u32[]{:S(2)}, u32[]{:S(2)}) %collective-permute-start.3) | collective-permute-done | bytes 81952 | tf_op jit(solution)/shard_map/ppermute | solution.py:513
  14.7 2.0 %collective-permute-start.4 = (f32[80,256]{1,0:T(8,128)S(1)}, f32[80,256]{1,0:T(8,128)S(1)}, u32[]{:S(2)}, u32[]{:S(2)}) collective-permute-start(f32[80,256]{1,0:T(8,128)S(1)} %get-tuple-element.42.pass0_ref), channel_id=1, source_target_pairs={{0,4},{4,0},{8,12},{12,8},{1,5},{5,1},{9,13},{13,9},{2,6},{6,2},{1... | collective-permute-start | bytes 245768 | tf_op jit(solution)/shard_map/ppermute | solution.py:513
  16.7 0.6 %collective-permute-done.6.there_ref = f32[80,256]{1,0:T(8,128)S(1)} collective-permute-done((f32[80,256]{1,0:T(8,128)S(1)}, f32[80,256]{1,0:T(8,128)S(1)}, u32[]{:S(2)}, u32[]{:S(2)}) %collective-permute-start.6) | collective-permute-done | bytes 81952 | tf_op jit(solution)/shard_map/ppermute | solution.py:513
  17.3 4.0 %collective-permute-start.7 = (f32[80,256]{1,0:T(8,128)S(1)}, f32[80,256]{1,0:T(8,128)S(1)}, u32[]{:S(2)}, u32[]{:S(2)}) collective-permute-start(f32[80,256]{1,0:T(8,128)S(1)} %get-tuple-element.46.pass3_ref), channel_id=1, source_target_pairs={{0,4},{4,0},{8,12},{12,8},{1,5},{5,1},{9,13},{13,9},{2,6},{6,2},{1... | collective-permute-start | bytes 245768 | tf_op jit(solution)/shard_map/ppermute | solution.py:513
  21.4 0.0 collective-permute-done.8.others_ref
  21.4 0.2 spread.1
  21.6 2.7 %collective-permute-start.9 = (f32[1,80,128]{2,1,0:T(8,128)S(1)}, f32[1,80,128]{2,1,0:T(8,128)S(1)}, u32[]{:S(2)}, u32[]{:S(2)}) collective-permute-start(f32[1,80,128]{2,1,0:T(8,128)S(1)} %get-tuple-element.55), channel_id=1, source_target_pairs={{1,6},{3,4},{2,5},{0,7},{5,2},{7,0},{6,1},{4,3},{9,14},{11,12},{10... | collective-permute-start | bytes 122888 | tf_op jit(solution)/shard_map/ppermute | solution.py:505
  24.3 0.0 collective-permute-start.10
  24.3 0.0 collective-permute-done.4.refs_1_
  24.3 0.0 collective-permute-done.7.refs_3_
  24.3 0.2 solve.1
  24.5 3.0 %collective-permute-start.11 = (f32[1,80,128]{2,1,0:T(8,128)S(1)}, f32[1,80,128]{2,1,0:T(8,128)S(1)}, u32[]{:S(2)}, u32[]{:S(2)}) collective-permute-start(f32[1,80,128]{2,1,0:T(8,128)S(1)} %get-tuple-element.57), channel_id=1, source_target_pairs={{0,1},{2,3},{1,0},{3,2},{4,5},{6,7},{5,4},{7,6},{8,9},{10,11},{9,8... | collective-permute-start | bytes 122888 | tf_op jit(solution)/shard_map/ppermute | solution.py:495
  27.5 1.7 %second.1 = (f32[2,320,256]{2,1,0:T(8,128)S(1)}, f32[2,320,256]{2,1,0:T(8,128)}) custom-call(f32[2,320,256]{2,1,0:T(8,128)S(1)} %get-tuple-element.48.state_ref, f32[5,64,256]{2,1,0:T(8,128)S(1)} %get-tuple-element.49.before_ref, f32[2,320,256]{2,1,0:T(8,128)S(1)} %get-tuple-element.50.forcing_ref, bf16[320,800]{1,0:T(8,128)(2,1)S(1)} %get-tuple-element.51.weights_ref, ...), custom_call_target="tpu_custom_call" | custom-call | flops 524288000 | bytes 3479552 | tf_op jit(solution)/shard_map/second/pallas_call | solution.py:481
  29.3 0.0 collective-permute-done.9.far_pass_ref
  29.3 0.0 collective-permute-done.10.far_ref
  29.3 0.0 collective-permute-done.11.near_ref
  29.3 1.1 %finish.1 = bf16[2,320,256]{2,1,0:T(8,128)(2,1)} custom-call(f32[2,320,256]{2,1,0:T(8,128)S(1)} %get-tuple-element.53.part_ref, f32[1,80,128]{2,1,0:T(8,128)S(1)} %collective-permute-done.9.far_pass_ref, f32[1,80,128]{2,1,0:T(8,128)S(1)} %collective-permute-done.10.far_ref, f32[1,80,128]{2,1,0:T(8,128)S(1)} %collective-permute-done.11.near_ref, ...), custom_call_target="tpu_custom_call" | custom-call | bytes 1226752 | tf_op jit(solution)/shard_map/finish/pallas_call | solution.py:481
  (4 shorter events, 0.1 us)
Async XLA Ops:
  1.8 4.2 %collective-permute-start = (f32[1,80,128]{2,1,0:T(8,128)S(1)}, f32[1,80,128]{2,1,0:T(8,128)S(1)}, u32[]{:S(2)}, u32[]{:S(2)}) collective-permute-start(f32[1,80,128]{2,1,0:T(8,128)S(1)} %get-tuple-element.32), channel_id=1, source_target_pairs={{1,2},{3,0},{2,1},{0,3},{5,6},{7,4},{6,5},{4,7},{9,10},{11,8},{10,... | collective-permute-start | bytes 122888 | tf_op jit(solution)/shard_map/ppermute | solution.py:503
  2.7 3.3 %collective-permute-start.1 = (f32[1,80,128]{2,1,0:T(8,128)S(1)}, f32[1,80,128]{2,1,0:T(8,128)S(1)}, u32[]{:S(2)}, u32[]{:S(2)}) collective-permute-start(f32[1,80,128]{2,1,0:T(8,128)S(1)} %get-tuple-element.33), channel_id=1, source_target_pairs={{0,1},{2,3},{1,0},{3,2},{4,5},{6,7},{5,4},{7,6},{8,9},{10,11},{9,8... | collective-permute-start | bytes 122888 | tf_op jit(solution)/shard_map/ppermute | solution.py:495
  6.6 3.7 %collective-permute-start.2 = (f32[80,256]{1,0:T(8,128)S(1)}, f32[80,256]{1,0:T(8,128)S(1)}, u32[]{:S(2)}, u32[]{:S(2)}) collective-permute-start(f32[80,256]{1,0:T(8,128)S(1)} %get-tuple-element.40), channel_id=1, source_target_pairs={{0,4},{4,0},{8,12},{12,8},{1,5},{5,1},{9,13},{13,9},{2,6},{6,2},{1... | collective-permute-start | bytes 245768 | tf_op jit(solution)/shard_map/ppermute | solution.py:513
  7.9 4.2 %collective-permute-start.5 = (f32[80,256]{1,0:T(8,128)S(1)}, f32[80,256]{1,0:T(8,128)S(1)}, u32[]{:S(2)}, u32[]{:S(2)}) collective-permute-start(f32[80,256]{1,0:T(8,128)S(1)} %get-tuple-element.44), channel_id=1, source_target_pairs={{0,4},{4,0},{8,12},{12,8},{1,5},{5,1},{9,13},{13,9},{2,6},{6,2},{1... | collective-permute-start | bytes 245768 | tf_op jit(solution)/shard_map/ppermute | solution.py:513
  10.3 4.3 %collective-permute-start.3 = (f32[80,256]{1,0:T(8,128)S(1)}, f32[80,256]{1,0:T(8,128)S(1)}, u32[]{:S(2)}, u32[]{:S(2)}) collective-permute-start(f32[80,256]{1,0:T(8,128)S(1)} %pair.2.here_ref), channel_id=1, source_target_pairs={{0,8},{4,12},{8,0},{12,4},{1,9},{5,13},{9,1},{13,5},{2,10},{6,14},... | collective-permute-start | bytes 245768 | tf_op jit(solution)/shard_map/ppermute | solution.py:513
  12.2 5.1 %collective-permute-start.6 = (f32[80,256]{1,0:T(8,128)S(1)}, f32[80,256]{1,0:T(8,128)S(1)}, u32[]{:S(2)}, u32[]{:S(2)}) collective-permute-start(f32[80,256]{1,0:T(8,128)S(1)} %pair.3.here_ref), channel_id=1, source_target_pairs={{0,8},{4,12},{8,0},{12,4},{1,9},{5,13},{9,1},{13,5},{2,10},{6,14},... | collective-permute-start | bytes 245768 | tf_op jit(solution)/shard_map/ppermute | solution.py:513
  12.8 8.6 %collective-permute-start.8 = (f32[2,80,128]{2,1,0:T(8,128)S(1)}, f32[2,80,128]{2,1,0:T(8,128)S(1)}, u32[]{:S(2)}, u32[]{:S(2)}) collective-permute-start(f32[2,80,128]{2,1,0:T(8,128)S(1)} %get-tuple-element.54.edges_ref), channel_id=1, source_target_pairs={{0,4},{4,0},{8,12},{12,8},{1,5},{5,1},{9,13},{13,9},{2,6},{6,2},{1... | collective-permute-start | bytes 245768 | tf_op jit(solution)/shard_map/ppermute | solution.py:513
  14.7 9.6 %collective-permute-start.4 = (f32[80,256]{1,0:T(8,128)S(1)}, f32[80,256]{1,0:T(8,128)S(1)}, u32[]{:S(2)}, u32[]{:S(2)}) collective-permute-start(f32[80,256]{1,0:T(8,128)S(1)} %get-tuple-element.42.pass0_ref), channel_id=1, source_target_pairs={{0,4},{4,0},{8,12},{12,8},{1,5},{5,1},{9,13},{13,9},{2,6},{6,2},{1... | collective-permute-start | bytes 245768 | tf_op jit(solution)/shard_map/ppermute | solution.py:513
  17.3 6.9 %collective-permute-start.7 = (f32[80,256]{1,0:T(8,128)S(1)}, f32[80,256]{1,0:T(8,128)S(1)}, u32[]{:S(2)}, u32[]{:S(2)}) collective-permute-start(f32[80,256]{1,0:T(8,128)S(1)} %get-tuple-element.46.pass3_ref), channel_id=1, source_target_pairs={{0,4},{4,0},{8,12},{12,8},{1,5},{5,1},{9,13},{13,9},{2,6},{6,2},{1... | collective-permute-start | bytes 245768 | tf_op jit(solution)/shard_map/ppermute | solution.py:513
  21.6 7.7 %collective-permute-start.9 = (f32[1,80,128]{2,1,0:T(8,128)S(1)}, f32[1,80,128]{2,1,0:T(8,128)S(1)}, u32[]{:S(2)}, u32[]{:S(2)}) collective-permute-start(f32[1,80,128]{2,1,0:T(8,128)S(1)} %get-tuple-element.55), channel_id=1, source_target_pairs={{1,6},{3,4},{2,5},{0,7},{5,2},{7,0},{6,1},{4,3},{9,14},{11,12},{10... | collective-permute-start | bytes 122888 | tf_op jit(solution)/shard_map/ppermute | solution.py:505
  24.3 5.0 %collective-permute-start.10 = (f32[1,80,128]{2,1,0:T(8,128)S(1)}, f32[1,80,128]{2,1,0:T(8,128)S(1)}, u32[]{:S(2)}, u32[]{:S(2)}) collective-permute-start(f32[1,80,128]{2,1,0:T(8,128)S(1)} %get-tuple-element.56), channel_id=1, source_target_pairs={{1,2},{3,0},{2,1},{0,3},{5,6},{7,4},{6,5},{4,7},{9,10},{11,8},{10,... | collective-permute-start | bytes 122888 | tf_op jit(solution)/shard_map/ppermute | solution.py:503
  24.5 4.8 %collective-permute-start.11 = (f32[1,80,128]{2,1,0:T(8,128)S(1)}, f32[1,80,128]{2,1,0:T(8,128)S(1)}, u32[]{:S(2)}, u32[]{:S(2)}) collective-permute-start(f32[1,80,128]{2,1,0:T(8,128)S(1)} %get-tuple-element.57), channel_id=1, source_target_pairs={{0,1},{2,3},{1,0},{3,2},{4,5},{6,7},{5,4},{7,6},{8,9},{10,11},{9,8... | collective-permute-start | bytes 122888 | tf_op jit(solution)/shard_map/ppermute | solution.py:495
